TPU v7x, 256 devices: a whole 4x4x8 slice. The times are simulated.
256 devices in a mesh: tm: 64 (over x, z, core), orb: 4 (over y).
Axes of the slice: x: 4, y: 4, z: 8, core: 2. Of those that a mesh axis runs over, the one named last changes fastest.
Arguments:
- history: bfloat16 [6, 64, 6, 64, 64, 128], P(None, None, None, 'tm', 'orb'), may hold values from -3 to 3
- hopping: bfloat16 [64, 64], replicated, may hold values from -0.75 to 0.75
- coupling: float32 [64], replicated, may hold values from 1 to 3
Outputs:
- row_one: bfloat16 [6, 64, 64, 128], P(None, 'tm', 'orb')
- corner_one: bfloat16 [64, 128], P('orb')
- row_two: bfloat16 [6, 64, 64, 128], P(None, 'tm', 'orb')
- edge_two: bfloat16 [64, 128], P('orb')
- corner_two: bfloat16 [64, 128], P('orb')
All inputs are finite; a program needn't handle non-finite values.
Results may differ from a plain program's by a relative error of at most 0.0085.
The roundings to bfloat16 on the way count: a program that leaves them out, or rounds other values in their place, can miss the bound.
Values may be sent and summed in bfloat16 or wider, within the bound.
No kernel may reach another device: no remote copies, remote signals or barrier semaphores. Data moves between devices by JAX's collectives and lax.ppermute only.
A program may use at most 128 MiB of HBM per device.

v0:
```python
import jax
import jax.numpy as jnp
from jax import lax
from jax.sharding import PartitionSpec as P

STEP = 0.08


def spread(array, axis, root):
    mine = lax.axis_index(axis) == root
    return lax.psum(jnp.where(mine, array, jnp.zeros_like(array)), axis)


def self_energy(blocks, row_gain, column_gain):
    orbitals = column_gain.shape[0]
    real_part = blocks[..., :orbitals].astype(jnp.float32)
    imag_part = blocks[..., orbitals:].astype(jnp.float32)
    strength = -(row_gain[:, None] * column_gain[None, :]) * (
        real_part * real_part + imag_part * imag_part
    )
    return jnp.concatenate([strength * real_part, strength * imag_part], axis=-1).astype(
        jnp.bfloat16
    )


def combine(first, second, orbitals):
    return jnp.concatenate(
        [
            first[..., :orbitals] - second[..., orbitals:],
            first[..., orbitals:] + second[..., :orbitals],
        ],
        axis=-1,
    )


def advance(older, change, orbitals):
    older = older.astype(jnp.float32)
    return jnp.concatenate(
        [
            older[..., :orbitals] + STEP * change[..., orbitals:],
            older[..., orbitals:] - STEP * change[..., :orbitals],
        ],
        axis=-1,
    )


def hermitian(whole, orbitals):
    real_part = whole[:, :orbitals]
    imag_part = whole[:, orbitals:]
    return jnp.concatenate([real_part + real_part.T, imag_part - imag_part.T], axis=-1)


def body(history, hopping, coupling):
    orbitals = hopping.shape[0]
    rounds = history.shape[0]
    owners = lax.axis_size("tm")
    local_rows = history.shape[4]
    owner = lax.axis_index("tm")
    orbital_slot = lax.axis_index("orb")
    grid = history.reshape(rounds, owners, rounds, local_rows, 2 * orbitals)
    source_time = (
        jnp.arange(rounds, dtype=jnp.int32)[:, None] * owners
        + jnp.arange(owners, dtype=jnp.int32)[None, :]
    )
    target_time = jnp.arange(rounds, dtype=jnp.int32) * owners + owner
    keep = (source_time[:, :, None] <= target_time[None, None, :])[..., None, None]
    masked = jnp.where(keep, grid, jnp.zeros_like(grid))
    row_gain = lax.dynamic_slice_in_dim(coupling, orbital_slot * local_rows, local_rows)
    turned = hopping.T

    def apply_hop(blocks):
        return jnp.concatenate(
            [
                jnp.dot(blocks[..., :orbitals], turned, preferred_element_type=jnp.float32),
                jnp.dot(blocks[..., orbitals:], turned, preferred_element_type=jnp.float32),
            ],
            axis=-1,
        )

    def own_rows(whole):
        return lax.dynamic_slice_in_dim(whole, orbital_slot * local_rows, local_rows, 0)

    def collide(table, sigma, extra):
        columns = table.shape[2]
        empty = jnp.zeros((columns, local_rows, 2 * orbitals), jnp.float32)
        extra_empty = jnp.zeros((local_rows, 2 * orbitals), jnp.float32)
        full_sigma = lax.all_gather(sigma, "orb", axis=1, tiled=True)

        def add_times(total, piece):
            first = jnp.einsum(
                "rmcjk,rmki->cji", table[..., :orbitals], piece, preferred_element_type=jnp.float32
            )
            second = jnp.einsum(
                "rmcjk,rmki->cji", table[..., orbitals:], piece, preferred_element_type=jnp.float32
            )
            main_total = combine(first, second, orbitals)
            if extra is None:
                return (main_total, total[1])
            first_col = jnp.einsum(
                "rmjk,rmki->ji", extra[..., :orbitals], piece, preferred_element_type=jnp.float32
            )
            second_col = jnp.einsum(
                "rmjk,rmki->ji", extra[..., orbitals:], piece, preferred_element_type=jnp.float32
            )
            return (main_total, combine(first_col, second_col, orbitals))

        return add_times(
            (empty, extra_empty), lax.all_gather(full_sigma[:, None], "tm", axis=1, tiled=True)
        )

    def mixed(local_change):
        whole = lax.all_gather(local_change, "orb", axis=0, tiled=True)
        return own_rows(hermitian(whole, orbitals))

    last_row = grid[rounds - 1, owners - 1]
    sigma = self_energy(last_row, row_gain, coupling)
    change = apply_hop(last_row) + STEP * collide(masked, sigma, None)[0]
    row_one = advance(last_row, change, orbitals).astype(jnp.bfloat16)
    corner_local = advance(last_row[rounds - 1], mixed(change[rounds - 1]), orbitals).astype(
        jnp.bfloat16
    )
    corner_rows = lax.all_gather(corner_local, "orb", axis=0, tiled=True)
    corner_full = spread(corner_rows, "tm", owners - 1)
    corner_one = own_rows(corner_full)
    sigma_two = self_energy(row_one, row_gain, coupling)
    corner_sigma = self_energy(corner_full, coupling, coupling)
    own_term = combine(
        jnp.dot(corner_full[:, :orbitals], corner_sigma, preferred_element_type=jnp.float32),
        jnp.dot(corner_full[:, orbitals:], corner_sigma, preferred_element_type=jnp.float32),
        orbitals,
    )
    corner_hop = apply_hop(corner_full)
    instant = combine(
        jnp.einsum(
            "rjk,ki->rji", row_one[..., :orbitals], corner_sigma, preferred_element_type=jnp.float32
        ),
        jnp.einsum(
            "rjk,ki->rji", row_one[..., orbitals:], corner_sigma, preferred_element_type=jnp.float32
        ),
        orbitals,
    )
    swapped = lax.all_to_all(
        row_one.reshape(rounds, local_rows, 2, orbitals),
        "orb",
        split_axis=3,
        concat_axis=1,
        tiled=True,
    )
    signs = jnp.array([-1.0, 1.0], jnp.bfloat16)[None, None, :, None]
    column_blocks = (jnp.transpose(swapped, (0, 3, 2, 1)) * signs).reshape(
        rounds, local_rows, 2 * orbitals
    )
    gathered = lax.all_gather(column_blocks[:, None], "tm", axis=1, tiled=True)
    totals, column_total = collide(masked, sigma_two, gathered)
    change_two = apply_hop(row_one) + instant + STEP * totals
    edge_change = own_rows(corner_hop) + STEP * (column_total + own_rows(own_term))
    edge_mix = mixed(edge_change)
    row_two = advance(row_one, change_two, orbitals).astype(jnp.bfloat16)
    edge_two = advance(corner_one, edge_change, orbitals).astype(jnp.bfloat16)
    corner_two = advance(corner_one, edge_mix, orbitals).astype(jnp.bfloat16)
    shape = (rounds, 1, local_rows, 2 * orbitals)
    return (row_one.reshape(shape), corner_one, row_two.reshape(shape), edge_two, corner_two)


def solution(mesh):
    placed = (P(None, None, None, "tm", "orb", None), P(), P())
    return jax.shard_map(
        body,
        mesh=mesh,
        in_specs=placed,
        out_specs=(
            P(None, "tm", "orb", None),
            P("orb", None),
            P(None, "tm", "orb", None),
            P("orb", None),
            P("orb", None),
        ),
        check_vma=False,
    )
```

profile of v0, /device:TPU:1, one launch (start us, length us, event | category | flops | bytes accessed | tf_op | source)
XLA Modules:
  0.0 473.4 jit_solution(14469968945633936037)
XLA Ops:
  7.2 0.7 dynamic_slice.18
  8.0 0.7 multiply_negate_fusion
  8.7 0.7 fusion.107
  9.6 11.1 %all_gather.24 = bf16[6,64,128]{2,1,0:T(8,128)(2,1)} all-gather(bf16[6,16,128]{2,1,0:T(8,128)(2,1)S(1)} %pad_maximum_fusion.1), channel_id=1, replica_groups=mesh['tm'=64,'orb'=4] {'orb'}, dimensions={1}, use_global_device_ids=true | all-gather | bytes 122880 | tf_op jit(solution)/shard_map/all_gather | solution.py:87
  21.4 5.9 %broadcast_select_fusion = bf16[6,64,6,16,128]{4,3,2,1,0:T(8,128)(2,1)S(1)} fusion(pred[6,64,6]{2,1,0:T(8,128)(4,1)S(1)} %broadcast_compare_fusion, bf16[6,64,6,1,16,128]{5,4,3,2,1,0:T(8,128)(2,1)} %param.4), kind=kLoop, calls=%fused_computation | loop fusion | flops 4718592 | bytes 18876672 | tf_op jit(solution)/shard_map/jit(_where)/select_n | solution.py:67
  27.2 8.1 %fusion.111 = (bf16[6,64,6,16,64]{4,3,2,1,0:T(8,128)(2,1)}, bf16[6,64,6,16,64]{4,3,2,1,0:T(8,128)(2,1)}) fusion(bf16[6,64,6,16,128]{4,3,2,1,0:T(8,128)(2,1)S(1)} %broadcast_select_fusion), kind=kLoop, calls=%fused_computation.159 | loop fusion | bytes 18874368 | tf_op jit(solution)/shard_map/slice | solution.py:91
  35.4 72.1 %all-gather.9.cloned.1.call-done = bf16[6,4096,128]{2,1,0:T(8,128)(2,1)} async-done(((bf16[6,64,128]{2,1,0:T(8,128)(2,1)}), bf16[6,4096,128]{2,1,0:T(8,128)(2,1)}) %all-gather.9.cloned.1.call-update) | async-done | bytes 6291472 | tf_op jit(solution)/shard_map/all_gather | solution.py:108
  107.5 7.7 %fusion.16 = f32[6,16,128]{2,1,0:T(8,128)S(1)} fusion(bf16[6,64,64,128,1]{3,2,1,0,4:T(8,128)(2,1)} %bitcast.115, bf16[6,64,6,16,64]{4,3,2,1,0:T(8,128)(2,1)} %get-tuple-element.32), kind=kOutput, calls=%fused_computation.17 | convolution fusion | flops 603979776 | bytes 11059200 | tf_op jit(solution)/shard_map/rmcjk,rmki->cji/dot_general | solution.py:90
  115.3 0.4 copy-done.2
  115.7 1.8 copy-done.6
  117.5 2.1 fusion.26
  120.3 8.1 %all_to_all.18 = bf16[4,2,1536]{2,1,0:T(2,128)(2,1)S(1)} all-to-all(bf16[4,2,1536]{2,1,0:T(2,128)(2,1)S(1)} %reshape.164), channel_id=1, replica_groups=mesh['tm'=64,'orb'=4] {'orb'}, dimensions={0} | all-to-all | bytes 49152 | tf_op jit(solution)/shard_map/all_to_all | solution.py:142
  129.0 0.7 broadcast_in_dim_reshape.3
  129.9 10.1 %all_gather.28 = bf16[6,64,128]{2,1,0:T(8,128)(2,1)} all-gather(bf16[6,16,128]{2,1,0:T(8,128)(2,1)S(1)} %pad_maximum_fusion.2), channel_id=1, replica_groups=mesh['tm'=64,'orb'=4] {'orb'}, dimensions={1}, use_global_device_ids=true | all-gather | bytes 122880 | tf_op jit(solution)/shard_map/all_gather | solution.py:87
  140.0 0.7 fusion.106
  140.7 9.4 %all-gather.1 = f32[1,64,128]{2,1,0:T(8,128)S(1)} all-gather(f32[1,16,128]{2,1,0:T(8,128)S(1)} %slice.245), channel_id=3, replica_groups=mesh['tm'=64,'orb'=4] {'orb'}, dimensions={1}, use_global_device_ids=true | all-gather | bytes 40960 | tf_op jit(solution)/shard_map/all_gather | solution.py:112
  150.7 9.1 %all_gather.27 = bf16[64,128]{1,0:T(8,128)(2,1)S(1)} all-gather(bf16[16,128]{1,0:T(8,128)(2,1)S(1)} %pad_maximum_fusion.4), channel_id=1, replica_groups=mesh['tm'=64,'orb'=4] {'orb'}, dimensions={0}, use_global_device_ids=true | all-gather | bytes 20480 | tf_op jit(solution)/shard_map/all_gather | solution.py:122
  159.8 250.8 %psum.7 = bf16[64,128]{1,0:T(8,128)(2,1)S(1)} all-reduce(bf16[64,128]{1,0:T(8,128)(2,1)S(1)} %broadcast_select_fusion.1), channel_id=1, replica_groups=mesh['tm'=64,'orb'=4] {'tm'}, use_global_device_ids=true, to_apply=%region_0.1 | all-reduce | flops 8192 | bytes 32768 | tf_op jit(solution)/shard_map/psum | solution.py:11
  410.6 0.6 fusion.108
  411.3 0.7 maximum_bitcast_fusion
  413.5 4.4 fusion.112
  417.9 3.4 copy.147
  421.3 4.3 copy.148
  425.6 7.7 %fusion.21 = f32[6,16,128]{2,1,0:T(8,128)S(1)} fusion(bf16[6,64,64,128,1]{3,2,1,0,4:T(8,128)(2,1)} %bitcast.98, bf16[6,64,6,16,64]{4,3,2,1,0:T(8,128)(2,1)} %get-tuple-element.32), kind=kOutput, calls=%fused_computation.18 | convolution fusion | flops 603979776 | bytes 11059200 | tf_op jit(solution)/shard_map/rmcjk,rmki->cji/dot_general | solution.py:90
  433.4 0.7 slice-done.1
  434.1 1.2 slice-done.2
  435.3 2.1 fusion.31
  437.4 9.2 %fusion.36 = f32[16,128]{1,0:T(8,128)S(1)} fusion(bf16[6,64,16,64]{1,2,0,3:T(8,128)(2,1)S(1)} %copy.147, bf16[6,64,64,128]{3,2,1,0:T(8,128)(2,1)S(1)} %bitcast.100), kind=kOutput, calls=%fused_computation.21 | convolution fusion | flops 100663296 | bytes 7086080 | tf_op jit(solution)/shard_map/rmjk,rmki->ji/dot_general | solution.py:99
  446.6 9.0 %fusion.39 = f32[16,128]{1,0:T(8,128)S(1)} fusion(bf16[6,64,16,64]{1,2,0,3:T(8,128)(2,1)S(1)} %copy-done.3, bf16[6,64,64,128]{3,2,1,0:T(8,128)(2,1)S(1)} %bitcast.101), kind=kOutput, calls=%fused_computation.22 | convolution fusion | flops 100663296 | bytes 7086080 | tf_op jit(solution)/shard_map/rmjk,rmki->ji/dot_general | solution.py:102
  455.7 9.0 %all_gather.31 = f32[64,128]{1,0:T(8,128)S(1)} all-gather(f32[16,128]{1,0:T(8,128)S(1)} %fusion.91), channel_id=1, replica_groups=mesh['tm'=64,'orb'=4] {'orb'}, dimensions={0}, use_global_device_ids=true | all-gather | bytes 40960 | tf_op jit(solution)/shard_map/all_gather | solution.py:112
  465.5 0.7 maximum_bitcast_fusion.1
  466.2 0.7 pad_maximum_fusion.5
  (79 shorter events, 5.4 us)
Async XLA Ops:
  7.2 13.9 %copy-start = (bf16[64,64]{1,0:T(8,128)(2,1)S(1)}, bf16[64,64]{1,0:T(8,128)(2,1)}, u32[]{:S(2)}) copy-start(bf16[64,64]{1,0:T(8,128)(2,1)} %param.5) | copy-start | bytes 24580
  7.2 100.3 %all-gather.9.cloned.1.call-start = ((), (), s32[]{:S(2)}) async-start(), calls=%async_computation.2 | async-start | bytes 6389760 | tf_op jit(solution)/shard_map/all_gather | solution.py:108
  20.8 392.7 %all-gather.7.cloned.1.call-start = ((), (), s32[]{:S(2)}) async-start(), calls=%async_computation.1 | async-start | bytes 1597440 | tf_op jit(solution)/shard_map/all_gather | solution.py:153
  107.5 8.2 %copy-start.2 = (bf16[6,64,6,16,64]{4,3,2,1,0:T(8,128)(2,1)S(1)}, bf16[6,64,6,16,64]{4,3,2,1,0:T(8,128)(2,1)}, u32[]{:S(2)}) copy-start(bf16[6,64,6,16,64]{4,3,2,1,0:T(8,128)(2,1)} %get-tuple-element.33) | copy-start | bytes 14155780
  107.5 9.9 %copy-start.6 = (bf16[6,4096,128]{2,1,0:T(8,128)(2,1)S(1)}, bf16[6,4096,128]{2,1,0:T(8,128)(2,1)}, u32[]{:S(2)}) copy-start(bf16[6,4096,128]{2,1,0:T(8,128)(2,1)} %all-gather.9.cloned.1.call-done) | copy-start | bytes 18874372
  117.5 11.4 %copy-start.5 = (bf16[2]{0:T(256)(128)(2,1)S(1)}, bf16[2]{0:T(256)(128)(2,1)}, u32[]{:S(2)}) copy-start(bf16[2]{0:T(256)(128)(2,1)} %constant.7.clone) | copy-start | bytes 16
  117.5 293.7 %copy-start.4 = (f32[64]{0:T(128)S(1)}, f32[64]{0:T(128)}, u32[]{:S(2)}) copy-start(f32[64]{0:T(128)} %param.6) | copy-start | bytes 772
  129.7 295.9 %all-gather.11.cloned.1.call-start = ((), (), s32[]{:S(2)}) async-start(), calls=%async_computation.3 | async-start | bytes 6389760 | tf_op jit(solution)/shard_map/all_gather | solution.py:108
  421.3 12.1 %slice-start = ((s8[9437184]{0:T(1024)(128)(4,1)}), s8[1048576]{0:T(1024)(128)(4,1)S(1)}, s32[]{:S(2)}) async-start(s8[9437184]{0:T(1024)(128)(4,1)} %bitcast.104), calls=%async_computation.4 | async-start | bytes 2097152
  425.6 7.8 %copy-start.1 = (bf16[6,4096,128]{2,1,0:T(8,128)(2,1)S(1)}, bf16[6,4096,128]{2,1,0:T(8,128)(2,1)}, u32[]{:S(2)}) copy-start(bf16[6,4096,128]{2,1,0:T(8,128)(2,1)} %all-gather.11.cloned.1.call-done) | copy-start | bytes 18874372
  425.6 8.5 %slice-start.1 = ((s8[9437184]{0:T(1024)(128)(4,1)}), s8[4194304]{0:T(1024)(128)(4,1)S(1)}, s32[]{:S(2)}) async-start(s8[9437184]{0:T(1024)(128)(4,1)} %bitcast.104), calls=%async_computation.5 | async-start | bytes 8388608
  425.6 9.7 %slice-start.2 = ((s8[9437184]{0:T(1024)(128)(4,1)}), s8[4194304]{0:T(1024)(128)(4,1)S(1)}, s32[]{:S(2)}) async-start(s8[9437184]{0:T(1024)(128)(4,1)} %bitcast.104), calls=%async_computation.6 | async-start | bytes 8388608
  437.4 9.2 %copy-start.3 = (bf16[6,64,16,64]{1,2,0,3:T(8,128)(2,1)S(1)}, bf16[6,64,16,64]{1,2,0,3:T(8,128)(2,1)}, u32[]{:S(2)}) copy-start(bf16[6,64,16,64]{1,2,0,3:T(8,128)(2,1)} %copy.148) | copy-start | bytes 2359300
Sparse Core Ops, SparseCore 0:
  20.9 86.6 all-gather.8
  129.8 73.1 all-gather.6
  205.9 78.7 all-gather.10
where the time goes:
time: 479 us; the launch traced here: 473 us
  blocking collectives  308 us (64%)
  waiting for transfers between devices  72.2 us (15%)
  matrix products  39.3 us (8%)
  local copies, waits for them, and re-layouts  27.2 us (6%)
  between operations  14 us (3%)
  other arithmetic  13 us (3%)
    psum x1, blocking collectives, spread(): return lax.psum(jnp.where(mine, array, jnp.zeros_like(array)), axis)  251 us
    all_gather x2, waiting for transfers between devices, collide(): lax.all_gather(full_sigma[:, None], 'tm', axis=1, tiled=True)  72.1 us
    all_gather x2, blocking collectives, collide(): full_sigma = lax.all_gather(sigma, 'orb', axis=1, tiled=True)  21.2 us
    all_gather x2, blocking collectives, mixed(): whole = lax.all_gather(local_change, 'orb', axis=0, tiled=True)  18.5 us
    dot_general x2, matrix products, add_times(): jnp.einsum('rmcjk,rmki->cji', table[..., :orbitals], piece, preferred_ele...  15.5 us
    unnamed x27, local copies, waits for them, and re-layouts  12.5 us
  transfers between devices with their start and end apart: 3, of which 1 were waited for; matrix products, arithmetic and copies ran while one was open for 7% of the time, Pallas kernels for 0%

commit v1 on v0

v1 whole, which is shorter than its diff:
```python
import functools

import jax
import jax.numpy as jnp
from jax import lax
from jax.experimental import pallas as pl
from jax.experimental.pallas import tpu as pltpu
from jax.sharding import Mesh, PartitionSpec as P

STEP = 0.08
XS, ZS, CORES, YS = 4, 8, 2, 4
ROUNDS = 6
HALF = ROUNDS // 2
ORB = 64
ROWS = ORB // YS
WIDE = 2 * ORB
COLS = ROUNDS * ROWS
GROUP = ZS * HALF
SHIFTS = (1, 3, 2)


def ring(size, distance):
    return [(i, (i + distance) % size) for i in range(size)]


def swap_cores(array):
    return lax.ppermute(array, "core", [(0, 1), (1, 0)])


def around(array, axis):
    pieces = {0: array}
    for distance in SHIFTS:
        pieces[distance] = lax.ppermute(array, axis, ring(4, distance))
    return [pieces[d] for d in range(4)]


def self_energy(blocks, row_gain, column_gain):
    real_part = blocks[..., :ORB].astype(jnp.float32)
    imag_part = blocks[..., ORB:].astype(jnp.float32)
    strength = -(row_gain[:, None] * column_gain[None, :]) * (
        real_part * real_part + imag_part * imag_part
    )
    return jnp.concatenate([strength * real_part, strength * imag_part], axis=-1).astype(
        jnp.bfloat16
    )


def combine(first, second):
    return jnp.concatenate(
        [
            first[..., :ORB] - second[..., ORB:],
            first[..., ORB:] + second[..., :ORB],
        ],
        axis=-1,
    )


def advance(older, change):
    older = older.astype(jnp.float32)
    return jnp.concatenate(
        [
            older[..., :ORB] + STEP * change[..., ORB:],
            older[..., ORB:] - STEP * change[..., :ORB],
        ],
        axis=-1,
    )


def hermitian(whole):
    real_part = whole[:, :ORB]
    imag_part = whole[:, ORB:]
    return jnp.concatenate([real_part + real_part.T, imag_part - imag_part.T], axis=-1)


def times_i(slab):
    return jnp.concatenate([-slab[:, ORB:], slab[:, :ORB]], axis=-1)


def collide_kernel(place, own, other, a0, a1, a2, a3, b0, b1, b2, b3, out, factor):
    step = pl.program_id(0)
    x, y, core, mine, partner = (place[i] for i in range(5))
    source = lax.rem(x - step + XS, XS)

    def put(round_at, z, dy, slab):
        row = pl.multiple_of(lax.rem(y - dy + YS, YS) * ROWS, ROWS)
        factor[round_at, pl.ds(z * WIDE + row, ROWS), :] = slab
        factor[round_at, pl.ds(z * WIDE + ORB + row, ROWS), :] = times_i(slab)

    for dx, block in enumerate((a0, a1, a2, a3)):

        @pl.when(step == dx)
        def _(block=block):
            for dy in range(YS):
                for z in range(ZS):
                    for r in range(HALF):
                        put(r, z, dy, block[dy * GROUP + z * HALF + r])

    for dy, block in enumerate((b0, b1, b2, b3)):
        for z in range(ZS):
            for r in range(HALF):
                put(HALF + r, z, dy, block[step * GROUP + z * HALF + r])

    @pl.when(step == 0)
    def _():
        out[...] = jnp.zeros_like(out)

    for a in range(ROUNDS):
        low = a * ROWS
        count = COLS - low
        sides = []
        for table, target in ((own, mine), (other, partner)):
            pieces = []
            for z in range(ZS):
                block = table[a, 0, z, 0, low:, :]
                time = (source * ZS + z) * CORES + core
                first = jnp.where(time <= target, block[:ROWS], jnp.zeros_like(block[:ROWS]))
                if count > ROWS:
                    block = jnp.concatenate([first, block[ROWS:]], axis=0)
                else:
                    block = first
                pieces.append(block)
            sides.append(jnp.concatenate(pieces, axis=1))
        product = jnp.dot(
            jnp.concatenate(sides, axis=0), factor[a], preferred_element_type=jnp.float32
        )
        out[0, low:, :] += product[:count]
        out[1, low:, :] += product[count:]


def collide(place, own, other, first, second):
    whole = [pl.BlockSpec(a.shape, lambda i, p: (0, 0, 0)) for a in first + second]
    return pl.pallas_call(
        collide_kernel,
        grid_spec=pltpu.PrefetchScalarGridSpec(
            num_scalar_prefetch=1,
            grid=(XS,),
            in_specs=[
                pl.BlockSpec(
                    (ROUNDS, 1, ZS, 1, COLS, WIDE),
                    lambda i, p: (0, lax.rem(p[0] - i + XS, XS), 0, p[2], 0, 0),
                ),
                pl.BlockSpec(
                    (ROUNDS, 1, ZS, 1, COLS, WIDE),
                    lambda i, p: (0, lax.rem(p[0] - i + XS, XS), 0, 0, 0, 0),
                ),
            ]
            + whole,
            out_specs=pl.BlockSpec((2, COLS, WIDE), lambda i, p: (0, 0, 0)),
            scratch_shapes=[pltpu.VMEM((ROUNDS, ZS * WIDE, WIDE), jnp.bfloat16)],
        ),
        out_shape=jax.ShapeDtypeStruct((2, COLS, WIDE), jnp.float32),
        compiler_params=pltpu.CompilerParams(vmem_limit_bytes=40 * 1024 * 1024),
        name="collide",
    )(place, own, other, *first, *second)


def split(value):
    high = lax.reduce_precision(value, 8, 7)
    return high.astype(jnp.bfloat16), (value - high).astype(jnp.bfloat16)


def body(history, hopping, coupling):
    x, z = lax.axis_index("x"), lax.axis_index("z")
    core, y = lax.axis_index("core"), lax.axis_index("orb")
    owner = (x * ZS + z) * CORES + core
    place = jnp.stack([x, y, core, owner, owner + 1 - 2 * core]).astype(jnp.int32)
    table = history.reshape(ROUNDS, XS, ZS, CORES, COLS, WIDE)
    partner = swap_cores(
        lax.dynamic_slice_in_dim(table, 1 - core, 1, axis=3)
    )
    row_gain = lax.dynamic_slice_in_dim(coupling, y * ROWS, ROWS)
    turned = hopping.T

    def apply_hop(blocks):
        return jnp.concatenate(
            [
                jnp.dot(blocks[..., :ORB], turned, preferred_element_type=jnp.float32),
                jnp.dot(blocks[..., ORB:], turned, preferred_element_type=jnp.float32),
            ],
            axis=-1,
        )

    def own_rows(whole):
        return lax.dynamic_slice_in_dim(whole, y * ROWS, ROWS, 0)

    def in_order(pieces):
        twice = jnp.stack([pieces[d] for d in (3, 2, 1, 0, 3, 2, 1)])
        return lax.dynamic_slice_in_dim(twice, 3 - y, 4, 0)

    def over_z(payload):
        return lax.all_to_all(jnp.broadcast_to(payload[None], (ZS,) + payload.shape), "z", 0, 0)

    def finish(parts):
        return (parts[0] + swap_cores(parts[1])).reshape(ROUNDS, ROWS, WIDE)

    last_row = history[ROUNDS - 1, XS * ZS * CORES - 1, :, 0]

    sigma = self_energy(last_row, row_gain, coupling)
    planes = over_z(sigma)
    first = around(planes[:, :HALF].reshape(GROUP, ROWS, WIDE), "orb")
    second = around(planes[:, HALF:].reshape(GROUP, ROWS, WIDE), "x")
    first = around(jnp.concatenate(first), "x")
    second = around(jnp.concatenate(second), "orb")
    change = apply_hop(last_row) + STEP * finish(collide(place, table, partner, first, second))
    row_one = advance(last_row, change).astype(jnp.bfloat16)
    sigma_two = self_energy(row_one, row_gain, coupling)

    overlap = jnp.einsum(
        "skj,ski->ji", row_one, sigma_two, preferred_element_type=jnp.float32
    )
    partial = combine(-overlap[:ORB], overlap[ORB:])
    column = own_rows(partial)
    for distance in SHIFTS:
        slab = lax.dynamic_slice_in_dim(partial, lax.rem(y + distance, YS) * ROWS, ROWS, 0)
        column = column + lax.ppermute(slab, "orb", ring(4, distance))

    last = ROUNDS - 1
    payload = jnp.concatenate([sigma_two, jnp.stack(split(change[last]) + (last_row[last],))])
    planes = over_z(payload)
    riders = planes[ZS - 1, ROUNDS:]
    first = around(
        jnp.concatenate([planes[:, :HALF].reshape(GROUP, ROWS, WIDE), riders]), "orb"
    )
    second = around(
        jnp.concatenate(
            [planes[:, HALF:ROUNDS].reshape(GROUP, ROWS, WIDE), jnp.stack(split(column))]
        ),
        "x",
    )
    riders = in_order([piece[GROUP:] for piece in first])
    newest = (riders[:, 0].astype(jnp.float32) + riders[:, 1].astype(jnp.float32)).reshape(
        ORB, WIDE
    )
    corner = advance(riders[:, 2].reshape(ORB, WIDE), hermitian(newest)).astype(jnp.bfloat16)
    column = sum(
        piece[GROUP].astype(jnp.float32) + piece[GROUP + 1].astype(jnp.float32)
        for piece in second
    )
    first = around(
        jnp.concatenate(
            [piece[:GROUP] for piece in first] + [corner.reshape(YS, ROWS, WIDE)]
        ),
        "x",
    )
    second = around(jnp.concatenate([piece[:GROUP] for piece in second]), "orb")
    column = jnp.sum(
        lax.all_to_all(
            jnp.broadcast_to(column[None], (ZS * CORES,) + column.shape), ("z", "core"), 0, 0
        ),
        axis=0,
    )
    column = in_order(around(column, "orb")).reshape(ORB, WIDE)
    from_last = lax.rem(x + 1, XS)
    corner = sum(
        jnp.where(from_last == d, first[d][4 * GROUP :], jnp.zeros((), jnp.bfloat16))
        for d in range(XS)
    )
    corner = jnp.where(core == 1, corner, swap_cores(corner)).reshape(ORB, WIDE)
    corner_sigma = self_energy(corner, coupling, coupling)

    def times_corner(blocks):
        return combine(
            jnp.dot(blocks[..., :ORB], corner_sigma, preferred_element_type=jnp.float32),
            jnp.dot(blocks[..., ORB:], corner_sigma, preferred_element_type=jnp.float32),
        )

    totals = finish(collide(place, table, partner, first, second))
    change_two = apply_hop(row_one) + times_corner(row_one) + STEP * totals
    row_two = advance(row_one, change_two).astype(jnp.bfloat16)
    edge_change = apply_hop(corner) + STEP * (column + times_corner(corner))
    edge_two = own_rows(advance(corner, edge_change)).astype(jnp.bfloat16)
    corner_two = own_rows(advance(corner, hermitian(edge_change))).astype(jnp.bfloat16)
    shape = (ROUNDS, 1, ROWS, WIDE)
    return (
        row_one.reshape(shape),
        own_rows(corner),
        row_two.reshape(shape),
        edge_two,
        corner_two,
    )


def solution(mesh):
    fine = Mesh(mesh.devices.reshape(XS, ZS, CORES, YS), ("x", "z", "core", "orb"))
    tm = ("x", "z", "core")
    return jax.shard_map(
        body,
        mesh=fine,
        in_specs=(P(None, None, None, tm, "orb", None), P(), P()),
        out_specs=(
            P(None, tm, "orb", None),
            P("orb", None),
            P(None, tm, "orb", None),
            P("orb", None),
            P("orb", None),
        ),
        check_vma=False,
    )
```

time: 479 us -> 180 us (0.38); the launches traced: 473 us -> 179 us
  blocking collectives: 308 us -> 17.1 us
  starting transfers between devices: 0.12 us -> 45.1 us
  matrix products: 39.3 us -> 2.48 us
  local copies, waits for them, and re-layouts: 27.2 us -> 9.76 us
  Pallas kernels: 0 us -> 14.7 us
  between operations: 14 us -> 1.11 us
  waiting for transfers between devices: 72.2 us -> 83.4 us
  other arithmetic: 13 us -> 5.73 us
    psum x1 -> x0, blocking collectives: 251 us -> none  [spread(): return lax.psum(jnp.where(mine, array, jnp.zeros_like(array)), axis)]
    all_gather x3 -> x0, waiting for transfers between devices: 72.2 us -> none  [the longest x2 72.1 us: collide(): lax.all_gather(full_sigma[:, None], 'tm', axis=1, tiled=True)]
    ppermute x0 -> x34, waiting for transfers between devices: none -> 68.4 us  [the longest x27 65.5 us: around(): pieces[distance] = lax.ppermute(array, axis, ring(4, distance))]
    all_gather x5 -> x0, blocking collectives: 48.7 us -> none  [the longest x2 21.2 us: collide(): full_sigma = lax.all_gather(sigma, 'orb', axis=1, tiled=True)]
    ppermute x0 -> x34, starting transfers between devices: none -> 36.9 us  [the longest x27 25.9 us: around(): pieces[distance] = lax.ppermute(array, axis, ring(4, distance))]
    dot_general x16 -> x11, matrix products: 39.3 us -> 2.48 us  [the longest x3 1.02 us: apply_hop(): jnp.dot(blocks[..., :ORB], turned, preferred_element_type=jnp.float32)]
    all_to_all x0 -> x2, waiting for transfers between devices: none -> 15 us  [the longest x1 8.63 us: body(): lax.all_to_all(jnp.broadcast_to(column[None], (ZS * CORES,) + column.shap...]
    pallas_call x0 -> x2, Pallas kernels: none -> 14.7 us  [collide(): pl.pallas_call(collide_kernel, grid_spec=pltpu.PrefetchScalarGridSpec(num...]
  transfers between devices with their start and end apart: 3 -> 36, of which waited for: 1 -> 24; matrix products, arithmetic and copies ran while one was open for 7% -> 5% of each run, Pallas kernels for 0% -> 4%
where the time goes in v1:
time: 180 us; the launch traced here: 179 us
  waiting for transfers between devices  83.4 us (46%)
  starting transfers between devices  45.1 us (25%)
  blocking collectives  17.1 us (10%)
  Pallas kernels  14.7 us (8%)
  local copies, waits for them, and re-layouts  9.76 us (5%)
  other arithmetic  5.73 us (3%)
  matrix products  2.48 us (1%)
    ppermute x27, waiting for transfers between devices, around(): pieces[distance] = lax.ppermute(array, axis, ring(4, distance))  65.5 us
    ppermute x27, starting transfers between devices, around(): pieces[distance] = lax.ppermute(array, axis, ring(4, distance))  25.9 us
    all_to_all x1, blocking collectives, over_z(): lax.all_to_all(jnp.broadcast_to(payload[None], (ZS,) + payload.shape), 'z...  17.1 us
    pallas_call x2, Pallas kernels, collide(): pl.pallas_call(collide_kernel, grid_spec=pltpu.PrefetchScalarGridSpec(num...  14.7 us
    all_to_all x1, waiting for transfers between devices, body(): lax.all_to_all(jnp.broadcast_to(column[None], (ZS * CORES,) + column.shap...  8.63 us
    ppermute x4, starting transfers between devices, swap_cores(): return lax.ppermute(array, 'core', [(0, 1), (1, 0)])  8.04 us
    all_to_all x1, waiting for transfers between devices, over_z(): lax.all_to_all(jnp.broadcast_to(payload[None], (ZS,) + payload.shape), 'z...  6.39 us
    dynamic_slice x1, local copies, waits for them, and re-layouts, body(): partner = swap_cores(lax.dynamic_slice_in_dim(table, 1 - core, 1, axis=3))  5.75 us
  transfers between devices with their start and end apart: 36, of which 24 were waited for; matrix products, arithmetic and copies ran while one was open for 5% of the time, Pallas kernels for 4%

profile of v1, /device:TPU:1, one launch (start us, length us, event | category | flops | bytes accessed | tf_op | source)
XLA Modules:
  0.0 179.3 jit_solution(12535466909420951417)
XLA Ops:
  0.7 5.8 %constant_dynamic-slice_fusion.3 = bf16[6,4,8,1,96,128]{5,4,3,2,1,0:T(8,128)(2,1)} fusion(bf16[6,4,8,2,96,128]{5,4,3,2,1,0:T(8,128)(2,1)} %bitcast.143, s32[]{:T(128)S(6)} %select_n.57), kind=kLoop, calls=%fused_computation.179 | loop fusion | bytes 9437188 | tf_op jit(solution)/shard_map/dynamic_slice | solution.py:169
  6.4 3.2 %collective-permute-start = (bf16[6,4,8,1,96,128]{5,4,3,2,1,0:T(8,128)(2,1)}, bf16[6,4,8,1,96,128]{5,4,3,2,1,0:T(8,128)(2,1)}, u32[]{:S(2)}, u32[]{:S(2)}) collective-permute-start(bf16[6,4,8,1,96,128]{5,4,3,2,1,0:T(8,128)(2,1)} %constant_dynamic-slice_fusion.3), channel_id=1, source_target_pairs={{0,4},{4,0},{1,5},{5,1},{2,6},{6,2},{3,7},{7,3},{8,12},{12,8},{9,1... | collective-permute-start | bytes 14155784 | tf_op jit(solution)/shard_map/ppermute | solution.py:27
  10.8 17.1 %all_to_all.15 = bf16[8,6,16,128]{3,2,1,0:T(8,128)(2,1)S(1)} all-to-all(bf16[8,6,16,128]{3,2,1,0:T(8,128)(2,1)S(1)} %broadcast_in_dim.12), channel_id=1, replica_groups=mesh['x'=4,'z'=8,'core'=2,'orb'=4] {'z'}, dimensions={0} | all-to-all | bytes 393216 | tf_op jit(solution)/shard_map/all_to_all | solution.py:191
  27.8 2.8 %collective-permute-start.3 = (bf16[24,16,128]{2,1,0:T(8,128)(2,1)S(1)}, bf16[24,16,128]{2,1,0:T(8,128)(2,1)S(1)}, u32[]{:S(2)}, u32[]{:S(2)}) collective-permute-start(bf16[24,16,128]{2,1,0:T(8,128)(2,1)S(1)} %bitcast.165), channel_id=1, source_target_pairs={{0,3},{1,0},{2,1},{3,2},{4,7},{5,4},{6,5},{7,6},{8,11},{9,8},{10,9... | collective-permute-start | bytes 294920 | tf_op jit(solution)/shard_map/ppermute | solution.py:33
  32.3 3.4 %collective-permute-done.2 = bf16[24,16,128]{2,1,0:T(8,128)(2,1)S(1)} collective-permute-done((bf16[24,16,128]{2,1,0:T(8,128)(2,1)S(1)}, bf16[24,16,128]{2,1,0:T(8,128)(2,1)S(1)}, u32[]{:S(2)}, u32[]{:S(2)}) %collective-permute-start.2) | collective-permute-done | bytes 98336 | tf_op jit(solution)/shard_map/ppermute | solution.py:33
  35.7 2.8 %collective-permute-done.1 = bf16[24,16,128]{2,1,0:T(8,128)(2,1)S(1)} collective-permute-done((bf16[24,16,128]{2,1,0:T(8,128)(2,1)S(1)}, bf16[24,16,128]{2,1,0:T(8,128)(2,1)S(1)}, u32[]{:S(2)}, u32[]{:S(2)}) %collective-permute-start.1) | collective-permute-done | bytes 98336 | tf_op jit(solution)/shard_map/ppermute | solution.py:33
  39.9 2.5 %collective-permute-start.5 = (bf16[96,16,128]{2,1,0:T(8,128)(2,1)S(1)}, bf16[96,16,128]{2,1,0:T(8,128)(2,1)S(1)}, u32[]{:S(2)}, u32[]{:S(2)}) collective-permute-start(bf16[96,16,128]{2,1,0:T(8,128)(2,1)S(1)} %pad_maximum_fusion.a0), channel_id=1, source_target_pairs={{0,128},{64,192},{128,0},{192,64},{1,129},{65,193},{129,1},{193,65... | collective-permute-start | bytes 1179656 | tf_op jit(solution)/shard_map/ppermute | solution.py:33
  43.7 9.8 %collective-permute-done.9 = bf16[24,16,128]{2,1,0:T(8,128)(2,1)S(1)} collective-permute-done((bf16[24,16,128]{2,1,0:T(8,128)(2,1)S(1)}, bf16[24,16,128]{2,1,0:T(8,128)(2,1)S(1)}, u32[]{:S(2)}, u32[]{:S(2)}) %collective-permute-start.9) | collective-permute-done | bytes 98336 | tf_op jit(solution)/shard_map/ppermute | solution.py:33
  53.6 7.5 %collective-permute-done.8 = bf16[24,16,128]{2,1,0:T(8,128)(2,1)S(1)} collective-permute-done((bf16[24,16,128]{2,1,0:T(8,128)(2,1)S(1)}, bf16[24,16,128]{2,1,0:T(8,128)(2,1)S(1)}, u32[]{:S(2)}, u32[]{:S(2)}) %collective-permute-start.8) | collective-permute-done | bytes 98336 | tf_op jit(solution)/shard_map/ppermute | solution.py:33
  61.1 3.4 %collective-permute-done.7 = bf16[24,16,128]{2,1,0:T(8,128)(2,1)S(1)} collective-permute-done((bf16[24,16,128]{2,1,0:T(8,128)(2,1)S(1)}, bf16[24,16,128]{2,1,0:T(8,128)(2,1)S(1)}, u32[]{:S(2)}, u32[]{:S(2)}) %collective-permute-start.7) | collective-permute-done | bytes 98336 | tf_op jit(solution)/shard_map/ppermute | solution.py:33
  65.3 2.3 %collective-permute-start.12 = (bf16[96,16,128]{2,1,0:T(8,128)(2,1)S(1)}, bf16[96,16,128]{2,1,0:T(8,128)(2,1)S(1)}, u32[]{:S(2)}, u32[]{:S(2)}) collective-permute-start(bf16[96,16,128]{2,1,0:T(8,128)(2,1)S(1)} %pad_maximum_fusion.1.b0), channel_id=1, source_target_pairs={{0,3},{1,0},{2,1},{3,2},{4,7},{5,4},{6,5},{7,6},{8,11},{9,8},{10,9... | collective-permute-start | bytes 1179656 | tf_op jit(solution)/shard_map/ppermute | solution.py:33
  68.7 15.8 %collective-permute-done.10.b1 = bf16[96,16,128]{2,1,0:T(8,128)(2,1)S(1)} collective-permute-done((bf16[96,16,128]{2,1,0:T(8,128)(2,1)S(1)}, bf16[96,16,128]{2,1,0:T(8,128)(2,1)S(1)}, u32[]{:S(2)}, u32[]{:S(2)}) %collective-permute-start.10) | collective-permute-done | bytes 393248 | tf_op jit(solution)/shard_map/ppermute | solution.py:33
  84.8 7.3 %collide.2 = f32[2,96,128]{2,1,0:T(8,128)S(1)} custom-call(s32[5]{0:T(128)S(1)} %stack.64.place, bf16[6,4,8,2,96,128]{5,4,3,2,1,0:T(8,128)(2,1)} %bitcast.145, bf16[6,4,8,1,96,128]{5,4,3,2,1,0:T(8,128)(2,1)} %collective-permute-done.other, bf16[96,16,128]{2,1,0:T(8,128)(2,1)S(1)} %pad_maximum_fusion.a0, bf16[96,16,128]{2,1,0:T(8,128)(2,1)S(1)} %collective-permute-done.4.a1, ...), custom_call_target="tpu_custom_call" | custom-call | tf_op jit(solution)/shard_map/collide/pallas_call | solution.py:132
  92.2 1.7 collective-permute-start.13
  97.1 3.4 %all-to-all-start.1 = ((bf16[8,9,16,128]{3,2,1,0:T(8,128)(2,1)}), bf16[8,9,16,128]{3,2,1,0:T(8,128)(2,1)S(1)}, u32[]{:S(2)}, u32[]{:S(2)}) async-start(bf16[8,9,16,128]{3,2,1,0:T(8,128)(2,1)} %broadcast_in_dim.13), calls=%async_computation.1 | async-start | bytes 589824 | tf_op jit(solution)/shard_map/all_to_all | solution.py:191
  101.4 1.8 %collective-permute-start.22 = (f32[16,128]{1,0:T(8,128)S(1)}, f32[16,128]{1,0:T(8,128)S(1)}, u32[]{:S(2)}, u32[]{:S(2)}) collective-permute-start(f32[16,128]{1,0:T(8,128)S(1)} %get-tuple-element.44), channel_id=1, source_target_pairs={{0,3},{1,0},{2,1},{3,2},{4,7},{5,4},{6,5},{7,6},{8,11},{9,8},{10,9... | collective-permute-start | bytes 24584 | tf_op jit(solution)/shard_map/ppermute | solution.py:215
  105.1 1.9 %collective-permute-done.21 = f32[16,128]{1,0:T(8,128)S(1)} collective-permute-done((f32[16,128]{1,0:T(8,128)S(1)}, f32[16,128]{1,0:T(8,128)S(1)}, u32[]{:S(2)}, u32[]{:S(2)}) %collective-permute-start.21) | collective-permute-done | bytes 8224 | tf_op jit(solution)/shard_map/ppermute | solution.py:215
  107.1 6.4 %all-to-all-done.1 = bf16[8,9,16,128]{3,2,1,0:T(8,128)(2,1)S(1)} async-done(((bf16[8,9,16,128]{3,2,1,0:T(8,128)(2,1)}), bf16[8,9,16,128]{3,2,1,0:T(8,128)(2,1)S(1)}, u32[]{:S(2)}, u32[]{:S(2)}) %all-to-all-start.1) | async-done | bytes 294944 | tf_op jit(solution)/shard_map/all_to_all | solution.py:191
  113.6 3.5 %collective-permute-start.15 = (bf16[27,16,128]{2,1,0:T(8,128)(2,1)S(1)}, bf16[27,16,128]{2,1,0:T(8,128)(2,1)S(1)}, u32[]{:S(2)}, u32[]{:S(2)}) collective-permute-start(bf16[27,16,128]{2,1,0:T(8,128)(2,1)S(1)} %pad_maximum_fusion.3), channel_id=1, source_target_pairs={{0,2},{1,3},{2,0},{3,1},{4,6},{5,7},{6,4},{7,5},{8,10},{9,11},{10,... | collective-permute-start | bytes 331784 | tf_op jit(solution)/shard_map/ppermute | solution.py:33
  118.7 2.1 %collective-permute-done.26 = bf16[26,16,128]{2,1,0:T(8,128)(2,1)S(1)} collective-permute-done((bf16[26,16,128]{2,1,0:T(8,128)(2,1)S(1)}, bf16[26,16,128]{2,1,0:T(8,128)(2,1)S(1)}, u32[]{:S(2)}, u32[]{:S(2)}) %collective-permute-start.26) | collective-permute-done | bytes 106528 | tf_op jit(solution)/shard_map/ppermute | solution.py:33
  120.8 1.9 %collective-permute-done.25 = bf16[26,16,128]{2,1,0:T(8,128)(2,1)S(1)} collective-permute-done((bf16[26,16,128]{2,1,0:T(8,128)(2,1)S(1)}, bf16[26,16,128]{2,1,0:T(8,128)(2,1)S(1)}, u32[]{:S(2)}, u32[]{:S(2)}) %collective-permute-start.25) | collective-permute-done | bytes 106528 | tf_op jit(solution)/shard_map/ppermute | solution.py:33
  122.7 2.7 %collective-permute-done.24 = bf16[26,16,128]{2,1,0:T(8,128)(2,1)S(1)} collective-permute-done((bf16[26,16,128]{2,1,0:T(8,128)(2,1)S(1)}, bf16[26,16,128]{2,1,0:T(8,128)(2,1)S(1)}, u32[]{:S(2)}, u32[]{:S(2)}) %collective-permute-start.24) | collective-permute-done | bytes 106528 | tf_op jit(solution)/shard_map/ppermute | solution.py:33
  126.8 4.8 %all-to-all-start.2 = ((f32[16,16,128]{2,1,0:T(8,128)}), f32[16,16,128]{2,1,0:T(8,128)S(1)}, u32[]{:S(2)}, u32[]{:S(2)}) async-start(f32[16,16,128]{2,1,0:T(8,128)} %broadcast_in_dim.15), calls=%async_computation.2 | async-start | bytes 262144 | tf_op jit(solution)/shard_map/all_to_all | solution.py:247
  132.1 8.6 %all-to-all-done.2 = f32[16,16,128]{2,1,0:T(8,128)S(1)} async-done(((f32[16,16,128]{2,1,0:T(8,128)}), f32[16,16,128]{2,1,0:T(8,128)S(1)}, u32[]{:S(2)}, u32[]{:S(2)}) %all-to-all-start.2) | async-done | bytes 131104 | tf_op jit(solution)/shard_map/all_to_all | solution.py:247
  140.8 2.1 %collective-permute-start.31 = (f32[16,128]{1,0:T(8,128)S(1)}, f32[16,128]{1,0:T(8,128)S(1)}, u32[]{:S(2)}, u32[]{:S(2)}) collective-permute-start(f32[16,128]{1,0:T(8,128)S(1)} %reduce_sum.9), channel_id=1, source_target_pairs={{0,3},{1,0},{2,1},{3,2},{4,7},{5,4},{6,5},{7,6},{8,11},{9,8},{10,9... | collective-permute-start | bytes 24584 | tf_op jit(solution)/shard_map/ppermute | solution.py:33
  145.1 2.4 %collective-permute-start.32 = (f32[16,128]{1,0:T(8,128)S(1)}, f32[16,128]{1,0:T(8,128)S(1)}, u32[]{:S(2)}, u32[]{:S(2)}) collective-permute-start(f32[16,128]{1,0:T(8,128)S(1)} %reduce_sum.9), channel_id=1, source_target_pairs={{0,2},{1,3},{2,0},{3,1},{4,6},{5,7},{6,4},{7,5},{8,10},{9,11},{10,... | collective-permute-start | bytes 24584 | tf_op jit(solution)/shard_map/ppermute | solution.py:33
  147.5 1.9 %collective-permute-done.32 = f32[16,128]{1,0:T(8,128)S(1)} collective-permute-done((f32[16,128]{1,0:T(8,128)S(1)}, f32[16,128]{1,0:T(8,128)S(1)}, u32[]{:S(2)}, u32[]{:S(2)}) %collective-permute-start.32) | collective-permute-done | bytes 8224 | tf_op jit(solution)/shard_map/ppermute | solution.py:33
  150.6 2.8 %collective-permute-done.33 = f32[16,128]{1,0:T(8,128)S(1)} collective-permute-done((f32[16,128]{1,0:T(8,128)S(1)}, f32[16,128]{1,0:T(8,128)S(1)}, u32[]{:S(2)}, u32[]{:S(2)}) %collective-permute-start.33) | collective-permute-done | bytes 8224 | tf_op jit(solution)/shard_map/ppermute | solution.py:33
  155.2 1.3 collective-permute-done.18.a2
  156.5 7.1 %collective-permute-done.17.a1 = bf16[100,16,128]{2,1,0:T(8,128)(2,1)S(1)} collective-permute-done((bf16[100,16,128]{2,1,0:T(8,128)(2,1)S(1)}, bf16[100,16,128]{2,1,0:T(8,128)(2,1)S(1)}, u32[]{:S(2)}, u32[]{:S(2)}) %collective-permute-start.17) | collective-permute-done | bytes 409632 | tf_op jit(solution)/shard_map/ppermute | solution.py:33
  163.7 3.0 %collective-permute-start.20 = (bf16[4,16,128]{2,1,0:T(8,128)(2,1)S(1)}, bf16[4,16,128]{2,1,0:T(8,128)(2,1)S(1)}, u32[]{:S(2)}, u32[]{:S(2)}) collective-permute-start(bf16[4,16,128]{2,1,0:T(8,128)(2,1)S(1)} %fusion.42), channel_id=1, source_target_pairs={{0,4},{4,0},{1,5},{5,1},{2,6},{6,2},{3,7},{7,3},{8,12},{12,8},{9,1... | collective-permute-start | bytes 49160 | tf_op jit(solution)/shard_map/ppermute | solution.py:27
  166.7 7.3 %collide.3 = f32[2,96,128]{2,1,0:T(8,128)S(1)} custom-call(s32[5]{0:T(128)S(1)} %stack.64.place, bf16[6,4,8,2,96,128]{5,4,3,2,1,0:T(8,128)(2,1)} %bitcast.146, bf16[6,4,8,1,96,128]{5,4,3,2,1,0:T(8,128)(2,1)} %collective-permute-done.other, bf16[100,16,128]{2,1,0:T(8,128)(2,1)S(1)} %constant_dynamic-update-slice_fusion.7.a0, ...), custom_call_target="tpu_custom_call" | custom-call | tf_op jit(solution)/shard_map/collide/pallas_call | solution.py:132
  (150 shorter events, 27.8 us)
Async XLA Ops:
  6.4 78.4 %collective-permute-start = (bf16[6,4,8,1,96,128]{5,4,3,2,1,0:T(8,128)(2,1)}, bf16[6,4,8,1,96,128]{5,4,3,2,1,0:T(8,128)(2,1)}, u32[]{:S(2)}, u32[]{:S(2)}) collective-permute-start(bf16[6,4,8,1,96,128]{5,4,3,2,1,0:T(8,128)(2,1)} %constant_dynamic-slice_fusion.3), channel_id=1, source_target_pairs={{0,4},{4,0},{1,5},{5,1},{2,6},{6,2},{3,7},{7,3},{8,12},{12,8},{9,1... | collective-permute-start | bytes 14155784 | tf_op jit(solution)/shard_map/ppermute | solution.py:27
  27.8 4.5 %collective-permute-start.3 = (bf16[24,16,128]{2,1,0:T(8,128)(2,1)S(1)}, bf16[24,16,128]{2,1,0:T(8,128)(2,1)S(1)}, u32[]{:S(2)}, u32[]{:S(2)}) collective-permute-start(bf16[24,16,128]{2,1,0:T(8,128)(2,1)S(1)} %bitcast.165), channel_id=1, source_target_pairs={{0,3},{1,0},{2,1},{3,2},{4,7},{5,4},{6,5},{7,6},{8,11},{9,8},{10,9... | collective-permute-start | bytes 294920 | tf_op jit(solution)/shard_map/ppermute | solution.py:33
  30.7 5.1 %collective-permute-start.2 = (bf16[24,16,128]{2,1,0:T(8,128)(2,1)S(1)}, bf16[24,16,128]{2,1,0:T(8,128)(2,1)S(1)}, u32[]{:S(2)}, u32[]{:S(2)}) collective-permute-start(bf16[24,16,128]{2,1,0:T(8,128)(2,1)S(1)} %bitcast.166), channel_id=1, source_target_pairs={{0,2},{1,3},{2,0},{3,1},{4,6},{5,7},{6,4},{7,5},{8,10},{9,11},{10,... | collective-permute-start | bytes 294920 | tf_op jit(solution)/shard_map/ppermute | solution.py:33
  31.0 7.5 %collective-permute-start.1 = (bf16[24,16,128]{2,1,0:T(8,128)(2,1)S(1)}, bf16[24,16,128]{2,1,0:T(8,128)(2,1)S(1)}, u32[]{:S(2)}, u32[]{:S(2)}) collective-permute-start(bf16[24,16,128]{2,1,0:T(8,128)(2,1)S(1)} %bitcast.167), channel_id=1, source_target_pairs={{0,1},{1,2},{2,3},{3,0},{4,5},{5,6},{6,7},{7,4},{8,9},{9,10},{10,1... | collective-permute-start | bytes 294920 | tf_op jit(solution)/shard_map/ppermute | solution.py:33
  38.6 26.1 %collective-permute-start.4 = (bf16[96,16,128]{2,1,0:T(8,128)(2,1)S(1)}, bf16[96,16,128]{2,1,0:T(8,128)(2,1)S(1)}, u32[]{:S(2)}, u32[]{:S(2)}) collective-permute-start(bf16[96,16,128]{2,1,0:T(8,128)(2,1)S(1)} %pad_maximum_fusion.a0), channel_id=1, source_target_pairs={{0,64},{64,128},{128,192},{192,0},{1,65},{65,129},{129,193},{193,1... | collective-permute-start | bytes 1179656 | tf_op jit(solution)/shard_map/ppermute | solution.py:33
  39.9 25.4 %collective-permute-start.5 = (bf16[96,16,128]{2,1,0:T(8,128)(2,1)S(1)}, bf16[96,16,128]{2,1,0:T(8,128)(2,1)S(1)}, u32[]{:S(2)}, u32[]{:S(2)}) collective-permute-start(bf16[96,16,128]{2,1,0:T(8,128)(2,1)S(1)} %pad_maximum_fusion.a0), channel_id=1, source_target_pairs={{0,128},{64,192},{128,0},{192,64},{1,129},{65,193},{129,1},{193,65... | collective-permute-start | bytes 1179656 | tf_op jit(solution)/shard_map/ppermute | solution.py:33
  42.3 11.2 %collective-permute-start.9 = (bf16[24,16,128]{2,1,0:T(8,128)(2,1)S(1)}, bf16[24,16,128]{2,1,0:T(8,128)(2,1)S(1)}, u32[]{:S(2)}, u32[]{:S(2)}) collective-permute-start(bf16[24,16,128]{2,1,0:T(8,128)(2,1)S(1)} %bitcast.161), channel_id=1, source_target_pairs={{0,192},{64,0},{128,64},{192,128},{1,193},{65,1},{129,65},{193,129... | collective-permute-start | bytes 294920 | tf_op jit(solution)/shard_map/ppermute | solution.py:33
  43.5 17.6 %collective-permute-start.8 = (bf16[24,16,128]{2,1,0:T(8,128)(2,1)S(1)}, bf16[24,16,128]{2,1,0:T(8,128)(2,1)S(1)}, u32[]{:S(2)}, u32[]{:S(2)}) collective-permute-start(bf16[24,16,128]{2,1,0:T(8,128)(2,1)S(1)} %bitcast.162), channel_id=1, source_target_pairs={{0,128},{64,192},{128,0},{192,64},{1,129},{65,193},{129,1},{193,65... | collective-permute-start | bytes 294920 | tf_op jit(solution)/shard_map/ppermute | solution.py:33
  53.5 11.0 %collective-permute-start.7 = (bf16[24,16,128]{2,1,0:T(8,128)(2,1)S(1)}, bf16[24,16,128]{2,1,0:T(8,128)(2,1)S(1)}, u32[]{:S(2)}, u32[]{:S(2)}) collective-permute-start(bf16[24,16,128]{2,1,0:T(8,128)(2,1)S(1)} %bitcast.163), channel_id=1, source_target_pairs={{0,64},{64,128},{128,192},{192,0},{1,65},{65,129},{129,193},{193,1... | collective-permute-start | bytes 294920 | tf_op jit(solution)/shard_map/ppermute | solution.py:33
  61.1 7.6 %collective-permute-start.6 = (bf16[96,16,128]{2,1,0:T(8,128)(2,1)S(1)}, bf16[96,16,128]{2,1,0:T(8,128)(2,1)S(1)}, u32[]{:S(2)}, u32[]{:S(2)}) collective-permute-start(bf16[96,16,128]{2,1,0:T(8,128)(2,1)S(1)} %pad_maximum_fusion.a0), channel_id=1, source_target_pairs={{0,192},{64,0},{128,64},{192,128},{1,193},{65,1},{129,65},{193,129... | collective-permute-start | bytes 1179656 | tf_op jit(solution)/shard_map/ppermute | solution.py:33
  64.6 19.9 %collective-permute-start.10 = (bf16[96,16,128]{2,1,0:T(8,128)(2,1)S(1)}, bf16[96,16,128]{2,1,0:T(8,128)(2,1)S(1)}, u32[]{:S(2)}, u32[]{:S(2)}) collective-permute-start(bf16[96,16,128]{2,1,0:T(8,128)(2,1)S(1)} %pad_maximum_fusion.1.b0), channel_id=1, source_target_pairs={{0,1},{1,2},{2,3},{3,0},{4,5},{5,6},{6,7},{7,4},{8,9},{9,10},{10,1... | collective-permute-start | bytes 1179656 | tf_op jit(solution)/shard_map/ppermute | solution.py:33
  64.7 19.8 %collective-permute-start.11 = (bf16[96,16,128]{2,1,0:T(8,128)(2,1)S(1)}, bf16[96,16,128]{2,1,0:T(8,128)(2,1)S(1)}, u32[]{:S(2)}, u32[]{:S(2)}) collective-permute-start(bf16[96,16,128]{2,1,0:T(8,128)(2,1)S(1)} %pad_maximum_fusion.1.b0), channel_id=1, source_target_pairs={{0,2},{1,3},{2,0},{3,1},{4,6},{5,7},{6,4},{7,5},{8,10},{9,11},{10,... | collective-permute-start | bytes 1179656 | tf_op jit(solution)/shard_map/ppermute | solution.py:33
  65.3 19.6 %collective-permute-start.12 = (bf16[96,16,128]{2,1,0:T(8,128)(2,1)S(1)}, bf16[96,16,128]{2,1,0:T(8,128)(2,1)S(1)}, u32[]{:S(2)}, u32[]{:S(2)}) collective-permute-start(bf16[96,16,128]{2,1,0:T(8,128)(2,1)S(1)} %pad_maximum_fusion.1.b0), channel_id=1, source_target_pairs={{0,3},{1,0},{2,1},{3,2},{4,7},{5,4},{6,5},{7,6},{8,11},{9,8},{10,9... | collective-permute-start | bytes 1179656 | tf_op jit(solution)/shard_map/ppermute | solution.py:33
  97.1 16.4 %all-to-all-start.1 = ((bf16[8,9,16,128]{3,2,1,0:T(8,128)(2,1)}), bf16[8,9,16,128]{3,2,1,0:T(8,128)(2,1)S(1)}, u32[]{:S(2)}, u32[]{:S(2)}) async-start(bf16[8,9,16,128]{3,2,1,0:T(8,128)(2,1)} %broadcast_in_dim.13), calls=%async_computation.1 | async-start | bytes 589824 | tf_op jit(solution)/shard_map/all_to_all | solution.py:191
  100.7 4.0 %collective-permute-start.23 = (f32[16,128]{1,0:T(8,128)S(1)}, f32[16,128]{1,0:T(8,128)S(1)}, u32[]{:S(2)}, u32[]{:S(2)}) collective-permute-start(f32[16,128]{1,0:T(8,128)S(1)} %get-tuple-element.45), channel_id=1, source_target_pairs={{0,2},{1,3},{2,0},{3,1},{4,6},{5,7},{6,4},{7,5},{8,10},{9,11},{10,... | collective-permute-start | bytes 24584 | tf_op jit(solution)/shard_map/ppermute | solution.py:215
  103.2 3.9 %collective-permute-start.21 = (f32[16,128]{1,0:T(8,128)S(1)}, f32[16,128]{1,0:T(8,128)S(1)}, u32[]{:S(2)}, u32[]{:S(2)}) collective-permute-start(f32[16,128]{1,0:T(8,128)S(1)} %get-tuple-element.43), channel_id=1, source_target_pairs={{0,1},{1,2},{2,3},{3,0},{4,5},{5,6},{6,7},{7,4},{8,9},{9,10},{10,1... | collective-permute-start | bytes 24584 | tf_op jit(solution)/shard_map/ppermute | solution.py:215
  113.6 18.0 %collective-permute-start.16 = (bf16[27,16,128]{2,1,0:T(8,128)(2,1)S(1)}, bf16[27,16,128]{2,1,0:T(8,128)(2,1)S(1)}, u32[]{:S(2)}, u32[]{:S(2)}) collective-permute-start(bf16[27,16,128]{2,1,0:T(8,128)(2,1)S(1)} %pad_maximum_fusion.3), channel_id=1, source_target_pairs={{0,1},{1,2},{2,3},{3,0},{4,5},{5,6},{6,7},{7,4},{8,9},{9,10},{10,1... | collective-permute-start | bytes 331784 | tf_op jit(solution)/shard_map/ppermute | solution.py:33
  113.6 17.9 %collective-permute-start.15 = (bf16[27,16,128]{2,1,0:T(8,128)(2,1)S(1)}, bf16[27,16,128]{2,1,0:T(8,128)(2,1)S(1)}, u32[]{:S(2)}, u32[]{:S(2)}) collective-permute-start(bf16[27,16,128]{2,1,0:T(8,128)(2,1)S(1)} %pad_maximum_fusion.3), channel_id=1, source_target_pairs={{0,2},{1,3},{2,0},{3,1},{4,6},{5,7},{6,4},{7,5},{8,10},{9,11},{10,... | collective-permute-start | bytes 331784 | tf_op jit(solution)/shard_map/ppermute | solution.py:33
  117.2 5.4 %collective-permute-start.25 = (bf16[26,16,128]{2,1,0:T(8,128)(2,1)S(1)}, bf16[26,16,128]{2,1,0:T(8,128)(2,1)S(1)}, u32[]{:S(2)}, u32[]{:S(2)}) collective-permute-start(bf16[26,16,128]{2,1,0:T(8,128)(2,1)S(1)} %pad_maximum_fusion.4), channel_id=1, source_target_pairs={{0,128},{64,192},{128,0},{192,64},{1,129},{65,193},{129,1},{193,65... | collective-permute-start | bytes 319496 | tf_op jit(solution)/shard_map/ppermute | solution.py:33
  117.9 7.4 %collective-permute-start.24 = (bf16[26,16,128]{2,1,0:T(8,128)(2,1)S(1)}, bf16[26,16,128]{2,1,0:T(8,128)(2,1)S(1)}, u32[]{:S(2)}, u32[]{:S(2)}) collective-permute-start(bf16[26,16,128]{2,1,0:T(8,128)(2,1)S(1)} %pad_maximum_fusion.4), channel_id=1, source_target_pairs={{0,64},{64,128},{128,192},{192,0},{1,65},{65,129},{129,193},{193,1... | collective-permute-start | bytes 319496 | tf_op jit(solution)/shard_map/ppermute | solution.py:33
  120.8 10.8 %collective-permute-start.14 = (bf16[27,16,128]{2,1,0:T(8,128)(2,1)S(1)}, bf16[27,16,128]{2,1,0:T(8,128)(2,1)S(1)}, u32[]{:S(2)}, u32[]{:S(2)}) collective-permute-start(bf16[27,16,128]{2,1,0:T(8,128)(2,1)S(1)} %pad_maximum_fusion.3), channel_id=1, source_target_pairs={{0,3},{1,0},{2,1},{3,2},{4,7},{5,4},{6,5},{7,6},{8,11},{9,8},{10,9... | collective-permute-start | bytes 331784 | tf_op jit(solution)/shard_map/ppermute | solution.py:33
  125.4 41.2 %collective-permute-start.27 = (bf16[96,16,128]{2,1,0:T(8,128)(2,1)S(1)}, bf16[96,16,128]{2,1,0:T(8,128)(2,1)S(1)}, u32[]{:S(2)}, u32[]{:S(2)}) collective-permute-start(bf16[96,16,128]{2,1,0:T(8,128)(2,1)S(1)} %pad_maximum_fusion.2.b0), channel_id=1, source_target_pairs={{0,1},{1,2},{2,3},{3,0},{4,5},{5,6},{6,7},{7,4},{8,9},{9,10},{10,1... | collective-permute-start | bytes 1179656 | tf_op jit(solution)/shard_map/ppermute | solution.py:33
  125.5 41.2 %collective-permute-start.28 = (bf16[96,16,128]{2,1,0:T(8,128)(2,1)S(1)}, bf16[96,16,128]{2,1,0:T(8,128)(2,1)S(1)}, u32[]{:S(2)}, u32[]{:S(2)}) collective-permute-start(bf16[96,16,128]{2,1,0:T(8,128)(2,1)S(1)} %pad_maximum_fusion.2.b0), channel_id=1, source_target_pairs={{0,2},{1,3},{2,0},{3,1},{4,6},{5,7},{6,4},{7,5},{8,10},{9,11},{10,... | collective-permute-start | bytes 1179656 | tf_op jit(solution)/shard_map/ppermute | solution.py:33
  126.8 14.0 %all-to-all-start.2 = ((f32[16,16,128]{2,1,0:T(8,128)}), f32[16,16,128]{2,1,0:T(8,128)S(1)}, u32[]{:S(2)}, u32[]{:S(2)}) async-start(f32[16,16,128]{2,1,0:T(8,128)} %broadcast_in_dim.15), calls=%async_computation.2 | async-start | bytes 262144 | tf_op jit(solution)/shard_map/all_to_all | solution.py:247
  140.8 4.3 %collective-permute-start.31 = (f32[16,128]{1,0:T(8,128)S(1)}, f32[16,128]{1,0:T(8,128)S(1)}, u32[]{:S(2)}, u32[]{:S(2)}) collective-permute-start(f32[16,128]{1,0:T(8,128)S(1)} %reduce_sum.9), channel_id=1, source_target_pairs={{0,3},{1,0},{2,1},{3,2},{4,7},{5,4},{6,5},{7,6},{8,11},{9,8},{10,9... | collective-permute-start | bytes 24584 | tf_op jit(solution)/shard_map/ppermute | solution.py:33
  143.0 11.4 %collective-permute-start.19 = (bf16[100,16,128]{2,1,0:T(8,128)(2,1)S(1)}, bf16[100,16,128]{2,1,0:T(8,128)(2,1)S(1)}, u32[]{:S(2)}, u32[]{:S(2)}) collective-permute-start(bf16[100,16,128]{2,1,0:T(8,128)(2,1)S(1)} %constant_dynamic-update-slice_fusion.7.a0), channel_id=1, source_target_pairs={{0,192},{64,0},{128,64},{192,128},{1,193},{65,1},{129,65},{193,129... | collective-permute-start | bytes 1228808 | tf_op jit(solution)/shard_map/ppermute | solution.py:33
  144.2 12.3 %collective-permute-start.18 = (bf16[100,16,128]{2,1,0:T(8,128)(2,1)S(1)}, bf16[100,16,128]{2,1,0:T(8,128)(2,1)S(1)}, u32[]{:S(2)}, u32[]{:S(2)}) collective-permute-start(bf16[100,16,128]{2,1,0:T(8,128)(2,1)S(1)} %constant_dynamic-update-slice_fusion.7.a0), channel_id=1, source_target_pairs={{0,128},{64,192},{128,0},{192,64},{1,129},{65,193},{129,1},{193,65... | collective-permute-start | bytes 1228808 | tf_op jit(solution)/shard_map/ppermute | solution.py:33
  145.1 4.3 %collective-permute-start.32 = (f32[16,128]{1,0:T(8,128)S(1)}, f32[16,128]{1,0:T(8,128)S(1)}, u32[]{:S(2)}, u32[]{:S(2)}) collective-permute-start(f32[16,128]{1,0:T(8,128)S(1)} %reduce_sum.9), channel_id=1, source_target_pairs={{0,2},{1,3},{2,0},{3,1},{4,6},{5,7},{6,4},{7,5},{8,10},{9,11},{10,... | collective-permute-start | bytes 24584 | tf_op jit(solution)/shard_map/ppermute | solution.py:33
  149.4 4.0 %collective-permute-start.33 = (f32[16,128]{1,0:T(8,128)S(1)}, f32[16,128]{1,0:T(8,128)S(1)}, u32[]{:S(2)}, u32[]{:S(2)}) collective-permute-start(f32[16,128]{1,0:T(8,128)S(1)} %reduce_sum.9), channel_id=1, source_target_pairs={{0,1},{1,2},{2,3},{3,0},{4,5},{5,6},{6,7},{7,4},{8,9},{9,10},{10,1... | collective-permute-start | bytes 24584 | tf_op jit(solution)/shard_map/ppermute | solution.py:33
  153.4 10.2 %collective-permute-start.17 = (bf16[100,16,128]{2,1,0:T(8,128)(2,1)S(1)}, bf16[100,16,128]{2,1,0:T(8,128)(2,1)S(1)}, u32[]{:S(2)}, u32[]{:S(2)}) collective-permute-start(bf16[100,16,128]{2,1,0:T(8,128)(2,1)S(1)} %constant_dynamic-update-slice_fusion.7.a0), channel_id=1, source_target_pairs={{0,64},{64,128},{128,192},{192,0},{1,65},{65,129},{129,193},{193,1... | collective-permute-start | bytes 1228808 | tf_op jit(solution)/shard_map/ppermute | solution.py:33
  154.4 12.3 %collective-permute-start.29 = (bf16[96,16,128]{2,1,0:T(8,128)(2,1)S(1)}, bf16[96,16,128]{2,1,0:T(8,128)(2,1)S(1)}, u32[]{:S(2)}, u32[]{:S(2)}) collective-permute-start(bf16[96,16,128]{2,1,0:T(8,128)(2,1)S(1)} %pad_maximum_fusion.2.b0), channel_id=1, source_target_pairs={{0,3},{1,0},{2,1},{3,2},{4,7},{5,4},{6,5},{7,6},{8,11},{9,8},{10,9... | collective-permute-start | bytes 1179656 | tf_op jit(solution)/shard_map/ppermute | solution.py:33
  163.7 10.5 %collective-permute-start.20 = (bf16[4,16,128]{2,1,0:T(8,128)(2,1)S(1)}, bf16[4,16,128]{2,1,0:T(8,128)(2,1)S(1)}, u32[]{:S(2)}, u32[]{:S(2)}) collective-permute-start(bf16[4,16,128]{2,1,0:T(8,128)(2,1)S(1)} %fusion.42), channel_id=1, source_target_pairs={{0,4},{4,0},{1,5},{5,1},{2,6},{6,2},{3,7},{7,3},{8,12},{12,8},{9,1... | collective-permute-start | bytes 49160 | tf_op jit(solution)/shard_map/ppermute | solution.py:27
  (6 other events, 89.5 us)

commit v2 on v1

v2 whole, which is shorter than its diff:
```python
import jax
import jax.numpy as jnp
from jax import lax
from jax.experimental import pallas as pl
from jax.experimental.pallas import tpu as pltpu
from jax.sharding import Mesh, PartitionSpec as P

STEP = 0.08
XS, ZS, CORES, YS = 4, 8, 2, 4
ROUNDS = 6
ORB = 64
ROWS = ORB // YS
WIDE = 2 * ORB
COLS = ROUNDS * ROWS
TIMES = ROUNDS * XS * ZS * CORES
EXTRA = 3
HALF = ROUNDS // 2
DEEP = 2
STEPS = ZS // DEEP
GROUP = ZS * HALF


def swap_cores(array):
    return lax.ppermute(array, "core", [(0, 1), (1, 0)])


def around(array, axis):
    pieces = {0: array}
    for distance in (1, 3, 2):
        pairs = [(i, (i + distance) % 4) for i in range(4)]
        pieces[distance] = lax.ppermute(array, axis, pairs)
    return [pieces[d] for d in range(4)]


def halves_swapped(value):
    return jnp.concatenate([value[:, ORB:], value[:, :ORB]], axis=-1)


def times_i(value):
    return jnp.concatenate([-value[:, ORB:], value[:, :ORB]], axis=-1)


def matrix_of(value):
    return jnp.concatenate([value, times_i(value)], axis=0)


def stepped(older, change):
    return older.astype(jnp.float32) - STEP * times_i(change)


def self_energy(blocks, gain):
    parts = blocks.astype(jnp.float32)
    square = parts * parts
    return (gain * (square + halves_swapped(square)) * parts).astype(jnp.bfloat16)


def hermitian(whole):
    real_part = whole[:, :ORB]
    imag_part = whole[:, ORB:]
    return jnp.concatenate([real_part + real_part.T, imag_part - imag_part.T], axis=-1)


def head_kernel(place, last, column, row, payload, gain_out):
    pair = jnp.concatenate([row[...], row[...]], axis=1)
    gain = -(column[...] * pair)
    gain = jnp.concatenate([gain] * ROUNDS, axis=0)
    gain_out[...] = gain
    sigma = self_energy(last[0, 0], gain)
    for z in range(ZS):
        payload[z] = sigma


def head(place, rows_of, coupling):
    return pl.pallas_call(
        head_kernel,
        grid_spec=pltpu.PrefetchScalarGridSpec(
            num_scalar_prefetch=1,
            grid=(1,),
            in_specs=[
                pl.BlockSpec(
                    (1, 1, COLS, WIDE), lambda i, p: (ROUNDS - 1, TIMES // ROUNDS - 1, 0, 0)
                ),
                pl.BlockSpec((ROWS, 1), lambda i, p: (p[4], 0)),
                pl.BlockSpec((1, ORB), lambda i, p: (0, 0)),
            ],
            out_specs=[
                pl.BlockSpec((ZS, COLS, WIDE), lambda i, p: (0, 0, 0)),
                pl.BlockSpec((COLS, WIDE), lambda i, p: (0, 0)),
            ],
        ),
        out_shape=[
            jax.ShapeDtypeStruct((ZS, COLS, WIDE), jnp.bfloat16),
            jax.ShapeDtypeStruct((COLS, WIDE), jnp.float32),
        ],
        compiler_params=pltpu.CompilerParams(vmem_limit_bytes=56 * 1024 * 1024),
        name="head",
    )(place, rows_of, coupling.reshape(ORB, 1), coupling.reshape(1, ORB))


def collide_kernel(
    place, own, other, a0, a1, a2, a3, b0, b1, low_two, high_two, b3, out, total, factor
):
    step = pl.program_id(0)
    core, x, y = place[0], place[3], place[4]
    firsts = (a0, a1, a2, a3)
    sources = [lax.rem(x - dx + XS, XS) for dx in range(XS)]
    empty = jnp.zeros((ORB, WIDE), jnp.bfloat16)

    @pl.when(step == 0)
    def _():
        total[...] = jnp.zeros_like(total)
        factor[...] = jnp.zeros_like(factor)

    for dy in range(YS):
        row = pl.multiple_of(lax.rem(y - dy + YS, YS) * ROWS, ROWS)
        for dx in range(XS):
            if dy == 2:
                piece = (low_two, high_two)[dx // 2].at[dx % 2]
            else:
                piece = (b0, b1, None, b3)[dy].at[dx]
            for z in range(DEEP):
                base = (dx * DEEP + z) * WIDE
                for r in range(HALF):
                    slab = piece[z * HALF + r]
                    factor[r, pl.ds(base + row, ROWS), :WIDE] = slab
                    factor[r, pl.ds(base + ORB + row, ROWS), WIDE:] = slab

    for a in range(ROUNDS):
        low, count = a * ROWS, COLS - a * ROWS
        sides = []
        for table, target in ((own, place[1]), (other, place[2])):
            blocks = []
            for dx in range(XS):
                for z in range(DEEP):
                    block = table[a, sources[dx], z, 0, low:, :]
                    time = (sources[dx] * ZS + step * DEEP + z) * CORES + core
                    diagonal = jnp.where(
                        time <= target, block[:ROWS], jnp.zeros_like(block[:ROWS])
                    )
                    if count > ROWS:
                        diagonal = jnp.concatenate([diagonal, block[ROWS:]], axis=0)
                    blocks.append(diagonal)
            sides.append(jnp.concatenate(blocks, axis=1))
        if a < HALF:
            blocks = []
            for dx in range(XS):
                for z in range(DEEP):
                    block = jnp.concatenate(
                        [
                            firsts[dx][lax.rem(y - i + YS, YS), z * HALF + a]
                            for i in range(YS)
                        ],
                        axis=0,
                    )
                    blocks.append(jnp.concatenate([block, empty], axis=1))
                    blocks.append(jnp.concatenate([empty, block], axis=1))
            right = jnp.concatenate(blocks, axis=0)
        else:
            right = factor[a - HALF]
        product = jnp.dot(
            jnp.concatenate(sides, axis=0), right, preferred_element_type=jnp.float32
        )
        total[0, low:, :] += product[:count]
        total[1, low:, :] += product[count:]

    @pl.when(step == STEPS - 1)
    def _():
        for side in range(2):
            out[side] = total[side, :, :WIDE] + times_i(total[side, :, WIDE:])


def collide(place, own, other, first, second):
    half = pl.BlockSpec(
        (ROUNDS, XS, DEEP, 1, COLS, WIDE), lambda i, p: (0, 0, i, p[0], 0, 0)
    )
    pieces = first + second
    slabs = [
        pl.BlockSpec((piece.shape[0], DEEP * HALF, ROWS, WIDE), lambda i, p: (0, i, 0, 0))
        for piece in pieces
    ]
    return pl.pallas_call(
        collide_kernel,
        grid_spec=pltpu.PrefetchScalarGridSpec(
            num_scalar_prefetch=1,
            grid=(STEPS,),
            in_specs=[half, half] + slabs,
            out_specs=pl.BlockSpec((2, COLS, WIDE), lambda i, p: (0, 0, 0)),
            scratch_shapes=[
                pltpu.VMEM((2, COLS, 2 * WIDE), jnp.float32),
                pltpu.VMEM((HALF, XS * DEEP * WIDE, 2 * WIDE), jnp.bfloat16),
            ],
        ),
        out_shape=jax.ShapeDtypeStruct((2, COLS, WIDE), jnp.float32),
        compiler_params=pltpu.CompilerParams(vmem_limit_bytes=48 * 1024 * 1024),
        name="collide",
    )(place, own, other, *pieces)


def pair(value):
    high = value.astype(jnp.bfloat16)
    return high, (value - high.astype(jnp.float32)).astype(jnp.bfloat16)


def joined(high, low):
    return high.astype(jnp.float32) + low.astype(jnp.float32)


def update_kernel(sums, theirs, last, hop, gain, row_out, payload):
    older = last[...]
    change = jnp.dot(older, hop[...], preferred_element_type=jnp.float32) + STEP * (
        sums[0] + theirs[...]
    )
    row = stepped(older, change).astype(jnp.bfloat16)
    sigma = self_energy(row, gain[...])
    row_out[...] = row
    overlap = lax.dot_general(
        row, sigma, (((0,), (0,)), ((), ())), preferred_element_type=jnp.float32
    )
    column = (times_i(overlap[ORB:]) - overlap[:ORB]).astype(jnp.bfloat16)
    riders = pair(change[COLS - ROWS :]) + (older[COLS - ROWS :], column)
    whole = jnp.concatenate((sigma,) + riders, axis=0)
    for z in range(ZS):
        payload[z] = whole


def update(sums, theirs, last, hop, gain):
    return pl.pallas_call(
        update_kernel,
        out_shape=[
            jax.ShapeDtypeStruct((COLS, WIDE), jnp.bfloat16),
            jax.ShapeDtypeStruct((ZS, COLS + EXTRA * ROWS + ORB, WIDE), jnp.bfloat16),
        ],
        name="update",
    )(sums, theirs, last, hop, gain)


def close_kernel(sums, theirs, row, hop, corner_factor, row_out):
    older = row[...]
    change = (
        jnp.dot(older, hop[...], preferred_element_type=jnp.float32)
        + jnp.dot(older, corner_factor[...], preferred_element_type=jnp.float32)
        + STEP * (sums[0] + theirs[...])
    )
    row_out[...] = stepped(older, change).astype(jnp.bfloat16)


def close(sums, theirs, row, hop, corner_factor):
    return pl.pallas_call(
        close_kernel,
        out_shape=jax.ShapeDtypeStruct((COLS, WIDE), jnp.bfloat16),
        name="close",
    )(sums, theirs, row, hop, corner_factor)


def body(history, hopping, coupling):
    x, z = lax.axis_index("x"), lax.axis_index("z")
    core, y = lax.axis_index("core"), lax.axis_index("orb")
    owner = (x * ZS + z) * CORES + core
    place = jnp.stack([core, owner, owner + 1 - 2 * core, x, y]).astype(jnp.int32)
    table = history.reshape(ROUNDS, XS, ZS, CORES, COLS, WIDE)
    rows_of = history.reshape(ROUNDS, TIMES // ROUNDS, COLS, WIDE)
    turned = hopping.T
    empty = jnp.zeros_like(turned)
    hop = jnp.concatenate(
        [
            jnp.concatenate([turned, empty], axis=1),
            jnp.concatenate([empty, turned], axis=1),
        ],
        axis=0,
    )
    corner_gain = -(coupling[:, None] * jnp.concatenate([coupling, coupling])[None, :])

    def own_rows(whole):
        return lax.dynamic_slice_in_dim(whole, y * ROWS, ROWS, 0)

    def along_both(first, second):
        first, second = lax.optimization_barrier((first, second))
        first, second = around(first, "orb"), around(second, "x")
        first, second = lax.optimization_barrier((first, second))
        first, second = jnp.concatenate(first), jnp.concatenate(second)
        first, second = lax.optimization_barrier((first, second))
        return along_again(first, second)

    def along_again(first, second):
        ahead = lax.ppermute(second, "orb", [(i, (i + 1) % YS) for i in range(YS)])
        behind = lax.ppermute(second, "orb", [(i, (i + 3) % YS) for i in range(YS)])
        middle = second.shape[0] // 2
        low = lax.ppermute(ahead[:middle], "orb", [(i, (i + 1) % YS) for i in range(YS)])
        high = lax.ppermute(behind[middle:], "orb", [(i, (i + 3) % YS) for i in range(YS)])
        first = [piece.reshape(YS, -1, ROWS, WIDE) for piece in around(first, "x")]
        second = [
            piece.reshape(-1, second.shape[0] // XS, ROWS, WIDE)
            for piece in (second, ahead, low, high, behind)
        ]
        return lax.optimization_barrier((first, second))

    def plane_parts(planes):
        parts = planes.reshape(ZS, -1, ROWS, WIDE)
        return (
            parts[:, :HALF].reshape(GROUP, ROWS, WIDE),
            parts[:, HALF:ROUNDS].reshape(GROUP, ROWS, WIDE),
        )

    def ring_sum(pieces):
        a, b, c, d = pieces
        return (a + c) + (b + d)

    other = swap_cores(table)
    payload, gains = head(place, rows_of, coupling)
    planes = lax.all_to_all(payload, "z", 0, 0)
    last_row = rows_of[ROUNDS - 1, TIMES // ROUNDS - 1]
    planes, other, last_row, hop, gains, corner_gain = lax.optimization_barrier(
        (planes, other, last_row, hop, gains, corner_gain)
    )
    first, second = along_both(*plane_parts(planes))
    sums = collide(place, table, other, first, second)
    row_one, payload = update(sums, swap_cores(sums[1]), last_row, hop, gains)

    planes = lax.all_to_all(payload, "z", 0, 0)
    first, second = plane_parts(planes)
    parts = planes.reshape(ZS, -1, ROWS, WIDE)
    riders = parts[ZS - 1, ROUNDS : ROUNDS + EXTRA]
    column = jnp.sum(parts[:, ROUNDS + EXTRA :].astype(jnp.float32), axis=0)
    first, second = along_both(
        jnp.concatenate([first, riders]),
        jnp.concatenate([second, column.astype(jnp.bfloat16)]),
    )
    from_last = lax.rem(x + 1, XS)
    riders = first[0][:, GROUP:]
    for d in range(1, XS):
        riders = jnp.where(from_last == d, first[d][:, GROUP:], riders)
    riders = jnp.stack([riders[d] for d in (3, 2, 1, 0, 3, 2, 1)])
    riders = lax.dynamic_slice_in_dim(riders, 3 - y, YS, 0)
    newest = joined(riders[:, 0], riders[:, 1]).reshape(ORB, WIDE)
    corner = stepped(riders[:, 2].reshape(ORB, WIDE), hermitian(newest)).astype(jnp.bfloat16)
    corner = jnp.where(core == 1, corner, swap_cores(corner))
    columns = [piece[:, GROUP:].astype(jnp.float32) for piece in second]
    columns = [columns[0], columns[1], jnp.concatenate(columns[2:4]), columns[4]]
    column = ring_sum([ring_sum(piece) for piece in columns]).reshape(ORB, WIDE)
    column = column + swap_cores(column)
    corner_factor = matrix_of(self_energy(corner, corner_gain))
    edge_change = jnp.dot(corner, hop, preferred_element_type=jnp.float32) + STEP * (
        column + jnp.dot(corner, corner_factor, preferred_element_type=jnp.float32)
    )
    edge_two = own_rows(stepped(corner, edge_change)).astype(jnp.bfloat16)
    corner_two = own_rows(stepped(corner, hermitian(edge_change))).astype(jnp.bfloat16)

    sums = collide(place, table, other, first, second)
    row_two = close(sums, swap_cores(sums[1]), row_one, hop, corner_factor)
    shape = (ROUNDS, 1, ROWS, WIDE)
    return (
        row_one.reshape(shape),
        own_rows(corner),
        row_two.reshape(shape),
        edge_two,
        corner_two,
    )


def solution(mesh):
    fine = Mesh(mesh.devices.reshape(XS, ZS, CORES, YS), ("x", "z", "core", "orb"))
    tm = ("x", "z", "core")
    return jax.shard_map(
        body,
        mesh=fine,
        in_specs=(P(None, None, None, tm, "orb", None), P(), P()),
        out_specs=(
            P(None, tm, "orb", None),
            P("orb", None),
            P(None, tm, "orb", None),
            P("orb", None),
            P("orb", None),
        ),
        check_vma=False,
    )
```

time: 180 us -> 151 us (0.84)
  waiting for transfers between devices: 83.4 us -> 46.8 us
  Pallas kernels: 14.7 us -> 20 us
  starting transfers between devices: 45.1 us -> 47.8 us
  local copies, waits for them, and re-layouts: 9.76 us -> 7.49 us
  blocking collectives: 17.1 us -> 19.2 us
  matrix products: 2.48 us -> 0.41 us
    ppermute x30 -> x26, waiting for transfers between devices: 68.2 us -> 37.5 us  [the longest x18 28.3 us: around(): pieces[distance] = lax.ppermute(array, axis, pairs)]
    all_to_all x2 -> x1, waiting for transfers between devices: 15 us -> 8.36 us  [body(): planes = lax.all_to_all(payload, 'z', 0, 0)]
    pallas_call x0 -> x3, Pallas kernels: none -> 6.35 us  [the longest x1 2.33 us: head(): pl.pallas_call(head_kernel, grid_spec=pltpu.PrefetchScalarGridSpec(num_sc...]
    dynamic_slice x3 -> x1, local copies, waits for them, and re-layouts: 5.83 us -> 0.61 us  [own_rows(): return lax.dynamic_slice_in_dim(whole, y * ROWS, ROWS, 0)]
    ppermute x30 -> x26, starting transfers between devices: 28.9 us -> 33.6 us  [the longest x18 21.6 us: around(): pieces[distance] = lax.ppermute(array, axis, pairs)]
    convert_element_type x7 -> x9, other arithmetic: 1.62 us -> 4.89 us  [the longest x5 4.03 us: body(): columns = [piece[:, GROUP:].astype(jnp.float32) for piece in second]]
    all_to_all x1, blocking collectives: 17.1 us -> 19.2 us  [body(): planes = lax.all_to_all(payload, 'z', 0, 0)]
    dot_general x11 -> x2, matrix products: 2.48 us -> 0.41 us  [the longest x1 0.21 us: body(): jnp.dot(corner, hop, preferred_element_type=jnp.float32)]
  transfers between devices with their start and end apart: 36 -> 32, of which waited for: 24 -> 13; matrix products, arithmetic and copies ran while one was open for 5% -> 6% of each run, Pallas kernels for 4% -> 2%
where the time goes in v2:
time: 151 us; the launch traced here: 150 us
  starting transfers between devices  47.8 us (32%)
  waiting for transfers between devices  46.8 us (31%)
  Pallas kernels  20 us (13%)
  blocking collectives  19.2 us (13%)
  local copies, waits for them, and re-layouts  7.49 us (5%)
  other arithmetic  7.39 us (5%)
    ppermute x18, waiting for transfers between devices, around(): pieces[distance] = lax.ppermute(array, axis, pairs)  28.3 us
    ppermute x18, starting transfers between devices, around(): pieces[distance] = lax.ppermute(array, axis, pairs)  21.6 us
    all_to_all x1, blocking collectives, body(): planes = lax.all_to_all(payload, 'z', 0, 0)  19.2 us
    pallas_call x2, Pallas kernels, collide(): pl.pallas_call(collide_kernel, grid_spec=pltpu.PrefetchScalarGridSpec(num...  13.7 us
    ppermute x2, waiting for transfers between devices, along_again(): ahead = lax.ppermute(second, 'orb', [(i, (i + 1) % YS) for i in range(YS)])  9.21 us
    all_to_all x1, waiting for transfers between devices, body(): planes = lax.all_to_all(payload, 'z', 0, 0)  8.36 us
    ppermute x5, starting transfers between devices, swap_cores(): return lax.ppermute(array, 'core', [(0, 1), (1, 0)])  7.73 us
    all_to_all x1, starting transfers between devices, body(): planes = lax.all_to_all(payload, 'z', 0, 0)  6.45 us
  transfers between devices with their start and end apart: 32, of which 13 were waited for; matrix products, arithmetic and copies ran while one was open for 6% of the time, Pallas kernels for 2%

profile of v2, /device:TPU:1, one launch (start us, length us, event | category | flops | bytes accessed | tf_op | source)
XLA Modules:
  0.0 150.1 jit_solution(14240706243137814207)
XLA Ops:
  0.7 3.3 %collective-permute-start = (bf16[6,4,8,2,96,128]{5,4,3,2,1,0:T(8,128)(2,1)}, bf16[6,4,8,2,96,128]{5,4,3,2,1,0:T(8,128)(2,1)}, u32[]{:S(2)}, u32[]{:S(2)}) collective-permute-start(bf16[6,4,8,2,96,128]{5,4,3,2,1,0:T(8,128)(2,1)} %bitcast.95), channel_id=1, source_target_pairs={{0,4},{4,0},{1,5},{5,1},{2,6},{6,2},{3,7},{7,3},{8,12},{12,8},{9,1... | collective-permute-start | bytes 28311560 | tf_op jit(solution)/shard_map/ppermute | solution.py:24
  5.9 2.3 %head.1 = (bf16[8,96,128]{2,1,0:T(8,128)(2,1)}, f32[96,128]{1,0:T(8,128)}) custom-call(s32[5]{0:T(128)} %stack.26.place, bf16[6,64,96,128]{3,2,1,0:T(8,128)(2,1)} %bitcast.96, f32[64,1]{1,0:T(8,128)} %copy.41.column, f32[1,64]{1,0:T(1,128)} %bitcast.121), custom_call_target="tpu_custom_call" | custom-call | tf_op jit(solution)/shard_map/head/pallas_call | solution.py:74
  8.3 6.5 %all-to-all-start = ((bf16[8,96,128]{2,1,0:T(8,128)(2,1)}), bf16[8,96,128]{2,1,0:T(8,128)(2,1)S(1)}, u32[]{:S(2)}, u32[]{:S(2)}) async-start(bf16[8,96,128]{2,1,0:T(8,128)(2,1)} %get-tuple-element.57), calls=%async_computation | async-start | bytes 393216 | tf_op jit(solution)/shard_map/all_to_all | solution.py:310
  17.0 8.4 %all-to-all-done = bf16[8,96,128]{2,1,0:T(8,128)(2,1)S(1)} async-done(((bf16[8,96,128]{2,1,0:T(8,128)(2,1)}), bf16[8,96,128]{2,1,0:T(8,128)(2,1)S(1)}, u32[]{:S(2)}, u32[]{:S(2)}) %all-to-all-start) | async-done | bytes 196640 | tf_op jit(solution)/shard_map/all_to_all | solution.py:310
  25.4 1.4 collective-permute-start.1
  26.8 2.6 %collective-permute-start.2 = (bf16[24,16,128]{2,1,0:T(8,128)(2,1)S(1)}, bf16[24,16,128]{2,1,0:T(8,128)(2,1)S(1)}, u32[]{:S(2)}, u32[]{:S(2)}) collective-permute-start(bf16[24,16,128]{2,1,0:T(8,128)(2,1)S(1)} %bitcast.111), channel_id=1, source_target_pairs={{0,2},{1,3},{2,0},{3,1},{4,6},{5,7},{6,4},{7,5},{8,10},{9,11},{10,... | collective-permute-start | bytes 294920 | tf_op jit(solution)/shard_map/ppermute | solution.py:31
  31.7 2.5 %collective-permute-start.5 = (bf16[24,16,128]{2,1,0:T(8,128)(2,1)S(1)}, bf16[24,16,128]{2,1,0:T(8,128)(2,1)S(1)}, u32[]{:S(2)}, u32[]{:S(2)}) collective-permute-start(bf16[24,16,128]{2,1,0:T(8,128)(2,1)S(1)} %bitcast.107), channel_id=1, source_target_pairs={{0,128},{64,192},{128,0},{192,64},{1,129},{65,193},{129,1},{193,65... | collective-permute-start | bytes 294920 | tf_op jit(solution)/shard_map/ppermute | solution.py:31
  35.3 2.0 %collective-permute-done.5 = bf16[24,16,128]{2,1,0:T(8,128)(2,1)S(1)} collective-permute-done((bf16[24,16,128]{2,1,0:T(8,128)(2,1)S(1)}, bf16[24,16,128]{2,1,0:T(8,128)(2,1)S(1)}, u32[]{:S(2)}, u32[]{:S(2)}) %collective-permute-start.5) | collective-permute-done | bytes 98336 | tf_op jit(solution)/shard_map/ppermute | solution.py:31
  39.1 2.3 %collective-permute-start.12 = (bf16[96,16,128]{2,1,0:T(8,128)(2,1)S(1)}, bf16[96,16,128]{2,1,0:T(8,128)(2,1)S(1)}, u32[]{:S(2)}, u32[]{:S(2)}) collective-permute-start(bf16[96,16,128]{2,1,0:T(8,128)(2,1)S(1)} %get-tuple-element.72), channel_id=1, source_target_pairs={{0,3},{1,0},{2,1},{3,2},{4,7},{5,4},{6,5},{7,6},{8,11},{9,8},{10,9... | collective-permute-start | bytes 1179656 | tf_op jit(solution)/shard_map/ppermute | solution.py:286
  41.4 3.5 %collective-permute-start.8 = (bf16[96,16,128]{2,1,0:T(8,128)(2,1)S(1)}, bf16[96,16,128]{2,1,0:T(8,128)(2,1)S(1)}, u32[]{:S(2)}, u32[]{:S(2)}) collective-permute-start(bf16[96,16,128]{2,1,0:T(8,128)(2,1)S(1)} %get-tuple-element.71), channel_id=1, source_target_pairs={{0,128},{64,192},{128,0},{192,64},{1,129},{65,193},{129,1},{193,65... | collective-permute-start | bytes 1179656 | tf_op jit(solution)/shard_map/ppermute | solution.py:31
  44.9 3.3 %collective-permute-done.10 = bf16[96,16,128]{2,1,0:T(8,128)(2,1)S(1)} collective-permute-done((bf16[96,16,128]{2,1,0:T(8,128)(2,1)S(1)}, bf16[96,16,128]{2,1,0:T(8,128)(2,1)S(1)}, u32[]{:S(2)}, u32[]{:S(2)}) %collective-permute-start.10) | collective-permute-done | bytes 393248 | tf_op jit(solution)/shard_map/ppermute | solution.py:285
  48.4 2.7 %collective-permute-start.13 = (bf16[48,16,128]{2,1,0:T(8,128)(2,1)S(1)}, bf16[48,16,128]{2,1,0:T(8,128)(2,1)S(1)}, u32[]{:S(2)}, u32[]{:S(2)}) collective-permute-start(bf16[48,16,128]{2,1,0:T(8,128)(2,1)S(1)} %slice.157), channel_id=1, source_target_pairs={{0,3},{1,0},{2,1},{3,2},{4,7},{5,4},{6,5},{7,6},{8,11},{9,8},{10,9... | collective-permute-start | bytes 589832 | tf_op jit(solution)/shard_map/ppermute | solution.py:289
  51.1 8.5 %collective-permute-done.8 = bf16[96,16,128]{2,1,0:T(8,128)(2,1)S(1)} collective-permute-done((bf16[96,16,128]{2,1,0:T(8,128)(2,1)S(1)}, bf16[96,16,128]{2,1,0:T(8,128)(2,1)S(1)}, u32[]{:S(2)}, u32[]{:S(2)}) %collective-permute-start.8) | collective-permute-done | bytes 393248 | tf_op jit(solution)/shard_map/ppermute | solution.py:31
  59.6 2.1 %collective-permute-done.9 = bf16[96,16,128]{2,1,0:T(8,128)(2,1)S(1)} collective-permute-done((bf16[96,16,128]{2,1,0:T(8,128)(2,1)S(1)}, bf16[96,16,128]{2,1,0:T(8,128)(2,1)S(1)}, u32[]{:S(2)}, u32[]{:S(2)}) %collective-permute-start.9) | collective-permute-done | bytes 393248 | tf_op jit(solution)/shard_map/ppermute | solution.py:31
  61.7 6.7 %collide.2.sums = f32[2,96,128]{2,1,0:T(8,128)S(1)} custom-call(s32[5]{0:T(128)S(1)} %copy-done.2, bf16[6,4,8,2,96,128]{5,4,3,2,1,0:T(8,128)(2,1)} %bitcast.98, bf16[6,4,8,2,96,128]{5,4,3,2,1,0:T(8,128)(2,1)} %collective-permute-done.other, bf16[4,24,16,128]{3,2,1,0:T(8,128)(2,1)S(1)} %bitcast.74, bf16[4,24,16,128]{3,2,1,0:T(8,128)(2,1)S(1)} %bitcast.88, ...), custom_call_target="tpu_custom_call" | custom-call | tf_op jit(solution)/shard_map/collide/pallas_call | solution.py:181
  68.5 2.1 %collective-permute-start.14 = (f32[96,128]{1,0:T(8,128)S(1)}, f32[96,128]{1,0:T(8,128)S(1)}, u32[]{:S(2)}, u32[]{:S(2)}) collective-permute-start(f32[96,128]{1,0:T(8,128)S(1)} %slice_bitcast_fusion.1), channel_id=1, source_target_pairs={{0,4},{4,0},{1,5},{5,1},{2,6},{6,2},{3,7},{7,3},{8,12},{12,8},{9,1... | collective-permute-start | bytes 147464 | tf_op jit(solution)/shard_map/ppermute | solution.py:24
  72.0 2.2 %update.1 = (bf16[96,128]{1,0:T(8,128)(2,1)}, bf16[8,208,128]{2,1,0:T(8,128)(2,1)}) custom-call(f32[2,96,128]{2,1,0:T(8,128)} %copy-done.1, f32[96,128]{1,0:T(8,128)} %copy-done.6, bf16[96,128]{1,0:T(8,128)(2,1)} %slice_bitcast_fusion.2.last, bf16[128,128]{1,0:T(8,128)(2,1)} %fusion.2.hop, f32[96,128]{1,0:T(8,128)} %get-tuple-element.84.gain), custom_call_target="tpu_custom_call" | custom-call | tf_op jit(solution)/shard_map/update/pallas_call | solution.py:227
  74.2 19.2 %all_to_all.10 = bf16[8,208,128]{2,1,0:T(8,128)(2,1)S(1)} all-to-all(bf16[8,208,128]{2,1,0:T(8,128)(2,1)} %get-tuple-element.86), channel_id=1, replica_groups=mesh['x'=4,'z'=8,'core'=2,'orb'=4] {'z'}, dimensions={0} | all-to-all | bytes 851968 | tf_op jit(solution)/shard_map/all_to_all | solution.py:319
  94.2 2.9 %collective-permute-start.19 = (bf16[28,16,128]{2,1,0:T(8,128)(2,1)S(1)}, bf16[28,16,128]{2,1,0:T(8,128)(2,1)S(1)}, u32[]{:S(2)}, u32[]{:S(2)}) collective-permute-start(bf16[28,16,128]{2,1,0:T(8,128)(2,1)S(1)} %pad_maximum_fusion.4), channel_id=1, source_target_pairs={{0,128},{64,192},{128,0},{192,64},{1,129},{65,193},{129,1},{193,65... | collective-permute-start | bytes 344072 | tf_op jit(solution)/shard_map/ppermute | solution.py:31
  99.7 2.7 %collective-permute-done.16 = bf16[27,16,128]{2,1,0:T(8,128)(2,1)S(1)} collective-permute-done((bf16[27,16,128]{2,1,0:T(8,128)(2,1)S(1)}, bf16[27,16,128]{2,1,0:T(8,128)(2,1)S(1)}, u32[]{:S(2)}, u32[]{:S(2)}) %collective-permute-start.16) | collective-permute-done | bytes 110624 | tf_op jit(solution)/shard_map/ppermute | solution.py:31
  102.4 1.6 %collective-permute-done.17 = bf16[27,16,128]{2,1,0:T(8,128)(2,1)S(1)} collective-permute-done((bf16[27,16,128]{2,1,0:T(8,128)(2,1)S(1)}, bf16[27,16,128]{2,1,0:T(8,128)(2,1)S(1)}, u32[]{:S(2)}, u32[]{:S(2)}) %collective-permute-start.17) | collective-permute-done | bytes 110624 | tf_op jit(solution)/shard_map/ppermute | solution.py:31
  104.2 1.4 collective-permute-start.24
  105.6 2.4 %collective-permute-start.26 = (bf16[112,16,128]{2,1,0:T(8,128)(2,1)S(1)}, bf16[112,16,128]{2,1,0:T(8,128)(2,1)S(1)}, u32[]{:S(2)}, u32[]{:S(2)}) collective-permute-start(bf16[112,16,128]{2,1,0:T(8,128)(2,1)S(1)} %pad_maximum_fusion), channel_id=1, source_target_pairs={{0,3},{1,0},{2,1},{3,2},{4,7},{5,4},{6,5},{7,6},{8,11},{9,8},{10,9... | collective-permute-start | bytes 1376264 | tf_op jit(solution)/shard_map/ppermute | solution.py:286
  108.5 1.5 collective-permute-start.22
  110.9 5.9 %collective-permute-done.24 = bf16[112,16,128]{2,1,0:T(8,128)(2,1)S(1)} collective-permute-done((bf16[112,16,128]{2,1,0:T(8,128)(2,1)S(1)}, bf16[112,16,128]{2,1,0:T(8,128)(2,1)S(1)}, u32[]{:S(2)}, u32[]{:S(2)}) %collective-permute-start.24) | collective-permute-done | bytes 458784 | tf_op jit(solution)/shard_map/ppermute | solution.py:285
  118.3 2.7 %collective-permute-start.27 = (bf16[56,16,128]{2,1,0:T(8,128)(2,1)}, bf16[56,16,128]{2,1,0:T(8,128)(2,1)}, u32[]{:S(2)}, u32[]{:S(2)}) collective-permute-start(bf16[56,16,128]{2,1,0:T(8,128)(2,1)} %slice.164), channel_id=1, source_target_pairs={{0,3},{1,0},{2,1},{3,2},{4,7},{5,4},{6,5},{7,6},{8,11},{9,8},{10,9... | collective-permute-start | bytes 688136 | tf_op jit(solution)/shard_map/ppermute | solution.py:289
  121.0 5.6 %collective-permute-done.22 = bf16[108,16,128]{2,1,0:T(8,128)(2,1)S(1)} collective-permute-done((bf16[108,16,128]{2,1,0:T(8,128)(2,1)S(1)}, bf16[108,16,128]{2,1,0:T(8,128)(2,1)S(1)}, u32[]{:S(2)}, u32[]{:S(2)}) %collective-permute-start.22) | collective-permute-done | bytes 442400 | tf_op jit(solution)/shard_map/ppermute | solution.py:31
  126.7 3.6 %collective-permute-done.23 = bf16[108,16,128]{2,1,0:T(8,128)(2,1)S(1)} collective-permute-done((bf16[108,16,128]{2,1,0:T(8,128)(2,1)S(1)}, bf16[108,16,128]{2,1,0:T(8,128)(2,1)S(1)}, u32[]{:S(2)}, u32[]{:S(2)}) %collective-permute-start.23) | collective-permute-done | bytes 442400 | tf_op jit(solution)/shard_map/ppermute | solution.py:31
  131.6 1.4 slice_convert_fusion.3
  134.3 6.9 %collide.3.sums = f32[2,96,128]{2,1,0:T(8,128)S(1)} custom-call(s32[5]{0:T(128)S(1)} %copy-done.2, bf16[6,4,8,2,96,128]{5,4,3,2,1,0:T(8,128)(2,1)} %bitcast.99, bf16[6,4,8,2,96,128]{5,4,3,2,1,0:T(8,128)(2,1)} %collective-permute-done.other, bf16[4,27,16,128]{3,2,1,0:T(8,128)(2,1)S(1)} %bitcast.72, bf16[4,27,16,128]{3,2,1,0:T(8,128)(2,1)S(1)} %bitcast.82, ...), custom_call_target="tpu_custom_call" | custom-call | tf_op jit(solution)/shard_map/collide/pallas_call | solution.py:181
  141.8 1.8 %collective-permute-start.28 = (bf16[64,128]{1,0:T(8,128)(2,1)S(1)}, bf16[64,128]{1,0:T(8,128)(2,1)S(1)}, u32[]{:S(2)}, u32[]{:S(2)}) collective-permute-start(bf16[64,128]{1,0:T(8,128)(2,1)S(1)} %fusion.11), channel_id=1, source_target_pairs={{0,4},{4,0},{1,5},{5,1},{2,6},{6,2},{3,7},{7,3},{8,12},{12,8},{9,1... | collective-permute-start | bytes 49160 | tf_op jit(solution)/shard_map/ppermute | solution.py:24
  148.3 1.8 %close.1 = bf16[96,128]{1,0:T(8,128)(2,1)} custom-call(f32[2,96,128]{2,1,0:T(8,128)} %copy-done, f32[96,128]{1,0:T(8,128)} %copy-done.5, bf16[96,128]{1,0:T(8,128)(2,1)} %get-tuple-element.85.row, bf16[128,128]{1,0:T(8,128)(2,1)} %fusion.2.hop, bf16[128,128]{1,0:T(8,128)(2,1)} %copy-done.4), custom_call_target="tpu_custom_call" | custom-call | tf_op jit(solution)/shard_map/close/pallas_call | solution.py:248
  (116 shorter events, 25.4 us)
Async XLA Ops:
  0.7 24.7 %collective-permute-start = (bf16[6,4,8,2,96,128]{5,4,3,2,1,0:T(8,128)(2,1)}, bf16[6,4,8,2,96,128]{5,4,3,2,1,0:T(8,128)(2,1)}, u32[]{:S(2)}, u32[]{:S(2)}) collective-permute-start(bf16[6,4,8,2,96,128]{5,4,3,2,1,0:T(8,128)(2,1)} %bitcast.95), channel_id=1, source_target_pairs={{0,4},{4,0},{1,5},{5,1},{2,6},{6,2},{3,7},{7,3},{8,12},{12,8},{9,1... | collective-permute-start | bytes 28311560 | tf_op jit(solution)/shard_map/ppermute | solution.py:24
  8.3 17.1 %all-to-all-start = ((bf16[8,96,128]{2,1,0:T(8,128)(2,1)}), bf16[8,96,128]{2,1,0:T(8,128)(2,1)S(1)}, u32[]{:S(2)}, u32[]{:S(2)}) async-start(bf16[8,96,128]{2,1,0:T(8,128)(2,1)} %get-tuple-element.57), calls=%async_computation | async-start | bytes 393216 | tf_op jit(solution)/shard_map/all_to_all | solution.py:310
  25.4 8.7 %collective-permute-start.1 = (bf16[24,16,128]{2,1,0:T(8,128)(2,1)S(1)}, bf16[24,16,128]{2,1,0:T(8,128)(2,1)S(1)}, u32[]{:S(2)}, u32[]{:S(2)}) collective-permute-start(bf16[24,16,128]{2,1,0:T(8,128)(2,1)S(1)} %bitcast.110), channel_id=1, source_target_pairs={{0,1},{1,2},{2,3},{3,0},{4,5},{5,6},{6,7},{7,4},{8,9},{9,10},{10,1... | collective-permute-start | bytes 294920 | tf_op jit(solution)/shard_map/ppermute | solution.py:31
  26.8 8.5 %collective-permute-start.2 = (bf16[24,16,128]{2,1,0:T(8,128)(2,1)S(1)}, bf16[24,16,128]{2,1,0:T(8,128)(2,1)S(1)}, u32[]{:S(2)}, u32[]{:S(2)}) collective-permute-start(bf16[24,16,128]{2,1,0:T(8,128)(2,1)S(1)} %bitcast.111), channel_id=1, source_target_pairs={{0,2},{1,3},{2,0},{3,1},{4,6},{5,7},{6,4},{7,5},{8,10},{9,11},{10,... | collective-permute-start | bytes 294920 | tf_op jit(solution)/shard_map/ppermute | solution.py:31
  29.4 5.9 %collective-permute-start.3 = (bf16[24,16,128]{2,1,0:T(8,128)(2,1)S(1)}, bf16[24,16,128]{2,1,0:T(8,128)(2,1)S(1)}, u32[]{:S(2)}, u32[]{:S(2)}) collective-permute-start(bf16[24,16,128]{2,1,0:T(8,128)(2,1)S(1)} %bitcast.112), channel_id=1, source_target_pairs={{0,3},{1,0},{2,1},{3,2},{4,7},{5,4},{6,5},{7,6},{8,11},{9,8},{10,9... | collective-permute-start | bytes 294920 | tf_op jit(solution)/shard_map/ppermute | solution.py:31
  30.5 4.8 %collective-permute-start.4 = (bf16[24,16,128]{2,1,0:T(8,128)(2,1)S(1)}, bf16[24,16,128]{2,1,0:T(8,128)(2,1)S(1)}, u32[]{:S(2)}, u32[]{:S(2)}) collective-permute-start(bf16[24,16,128]{2,1,0:T(8,128)(2,1)S(1)} %bitcast.106), channel_id=1, source_target_pairs={{0,64},{64,128},{128,192},{192,0},{1,65},{65,129},{129,193},{193,1... | collective-permute-start | bytes 294920 | tf_op jit(solution)/shard_map/ppermute | solution.py:31
  31.7 5.6 %collective-permute-start.5 = (bf16[24,16,128]{2,1,0:T(8,128)(2,1)S(1)}, bf16[24,16,128]{2,1,0:T(8,128)(2,1)S(1)}, u32[]{:S(2)}, u32[]{:S(2)}) collective-permute-start(bf16[24,16,128]{2,1,0:T(8,128)(2,1)S(1)} %bitcast.107), channel_id=1, source_target_pairs={{0,128},{64,192},{128,0},{192,64},{1,129},{65,193},{129,1},{193,65... | collective-permute-start | bytes 294920 | tf_op jit(solution)/shard_map/ppermute | solution.py:31
  34.1 4.4 %collective-permute-start.6 = (bf16[24,16,128]{2,1,0:T(8,128)(2,1)S(1)}, bf16[24,16,128]{2,1,0:T(8,128)(2,1)S(1)}, u32[]{:S(2)}, u32[]{:S(2)}) collective-permute-start(bf16[24,16,128]{2,1,0:T(8,128)(2,1)S(1)} %bitcast.108), channel_id=1, source_target_pairs={{0,192},{64,0},{128,64},{192,128},{1,193},{65,1},{129,65},{193,129... | collective-permute-start | bytes 294920 | tf_op jit(solution)/shard_map/ppermute | solution.py:31
  38.7 9.6 %collective-permute-start.10 = (bf16[96,16,128]{2,1,0:T(8,128)(2,1)S(1)}, bf16[96,16,128]{2,1,0:T(8,128)(2,1)S(1)}, u32[]{:S(2)}, u32[]{:S(2)}) collective-permute-start(bf16[96,16,128]{2,1,0:T(8,128)(2,1)S(1)} %get-tuple-element.72), channel_id=1, source_target_pairs={{0,1},{1,2},{2,3},{3,0},{4,5},{5,6},{6,7},{7,4},{8,9},{9,10},{10,1... | collective-permute-start | bytes 1179656 | tf_op jit(solution)/shard_map/ppermute | solution.py:285
  39.1 9.2 %collective-permute-start.12 = (bf16[96,16,128]{2,1,0:T(8,128)(2,1)S(1)}, bf16[96,16,128]{2,1,0:T(8,128)(2,1)S(1)}, u32[]{:S(2)}, u32[]{:S(2)}) collective-permute-start(bf16[96,16,128]{2,1,0:T(8,128)(2,1)S(1)} %get-tuple-element.72), channel_id=1, source_target_pairs={{0,3},{1,0},{2,1},{3,2},{4,7},{5,4},{6,5},{7,6},{8,11},{9,8},{10,9... | collective-permute-start | bytes 1179656 | tf_op jit(solution)/shard_map/ppermute | solution.py:286
  41.4 9.7 %collective-permute-start.7 = (bf16[96,16,128]{2,1,0:T(8,128)(2,1)S(1)}, bf16[96,16,128]{2,1,0:T(8,128)(2,1)S(1)}, u32[]{:S(2)}, u32[]{:S(2)}) collective-permute-start(bf16[96,16,128]{2,1,0:T(8,128)(2,1)S(1)} %get-tuple-element.71), channel_id=1, source_target_pairs={{0,64},{64,128},{128,192},{192,0},{1,65},{65,129},{129,193},{193,1... | collective-permute-start | bytes 1179656 | tf_op jit(solution)/shard_map/ppermute | solution.py:31
  41.4 18.1 %collective-permute-start.8 = (bf16[96,16,128]{2,1,0:T(8,128)(2,1)S(1)}, bf16[96,16,128]{2,1,0:T(8,128)(2,1)S(1)}, u32[]{:S(2)}, u32[]{:S(2)}) collective-permute-start(bf16[96,16,128]{2,1,0:T(8,128)(2,1)S(1)} %get-tuple-element.71), channel_id=1, source_target_pairs={{0,128},{64,192},{128,0},{192,64},{1,129},{65,193},{129,1},{193,65... | collective-permute-start | bytes 1179656 | tf_op jit(solution)/shard_map/ppermute | solution.py:31
  44.9 16.7 %collective-permute-start.9 = (bf16[96,16,128]{2,1,0:T(8,128)(2,1)S(1)}, bf16[96,16,128]{2,1,0:T(8,128)(2,1)S(1)}, u32[]{:S(2)}, u32[]{:S(2)}) collective-permute-start(bf16[96,16,128]{2,1,0:T(8,128)(2,1)S(1)} %get-tuple-element.71), channel_id=1, source_target_pairs={{0,192},{64,0},{128,64},{192,128},{1,193},{65,1},{129,65},{193,129... | collective-permute-start | bytes 1179656 | tf_op jit(solution)/shard_map/ppermute | solution.py:31
  48.2 13.4 %collective-permute-start.11 = (bf16[48,16,128]{2,1,0:T(8,128)(2,1)S(1)}, bf16[48,16,128]{2,1,0:T(8,128)(2,1)S(1)}, u32[]{:S(2)}, u32[]{:S(2)}) collective-permute-start(bf16[48,16,128]{2,1,0:T(8,128)(2,1)S(1)} %slice.156), channel_id=1, source_target_pairs={{0,1},{1,2},{2,3},{3,0},{4,5},{5,6},{6,7},{7,4},{8,9},{9,10},{10,1... | collective-permute-start | bytes 589832 | tf_op jit(solution)/shard_map/ppermute | solution.py:288
  48.4 13.3 %collective-permute-start.13 = (bf16[48,16,128]{2,1,0:T(8,128)(2,1)S(1)}, bf16[48,16,128]{2,1,0:T(8,128)(2,1)S(1)}, u32[]{:S(2)}, u32[]{:S(2)}) collective-permute-start(bf16[48,16,128]{2,1,0:T(8,128)(2,1)S(1)} %slice.157), channel_id=1, source_target_pairs={{0,3},{1,0},{2,1},{3,2},{4,7},{5,4},{6,5},{7,6},{8,11},{9,8},{10,9... | collective-permute-start | bytes 589832 | tf_op jit(solution)/shard_map/ppermute | solution.py:289
  68.5 2.9 %collective-permute-start.14 = (f32[96,128]{1,0:T(8,128)S(1)}, f32[96,128]{1,0:T(8,128)S(1)}, u32[]{:S(2)}, u32[]{:S(2)}) collective-permute-start(f32[96,128]{1,0:T(8,128)S(1)} %slice_bitcast_fusion.1), channel_id=1, source_target_pairs={{0,4},{4,0},{1,5},{5,1},{2,6},{6,2},{3,7},{7,3},{8,12},{12,8},{9,1... | collective-permute-start | bytes 147464 | tf_op jit(solution)/shard_map/ppermute | solution.py:24
  93.6 5.4 %collective-permute-start.15 = (bf16[27,16,128]{2,1,0:T(8,128)(2,1)S(1)}, bf16[27,16,128]{2,1,0:T(8,128)(2,1)S(1)}, u32[]{:S(2)}, u32[]{:S(2)}) collective-permute-start(bf16[27,16,128]{2,1,0:T(8,128)(2,1)S(1)} %pad_maximum_fusion.5), channel_id=1, source_target_pairs={{0,1},{1,2},{2,3},{3,0},{4,5},{5,6},{6,7},{7,4},{8,9},{9,10},{10,1... | collective-permute-start | bytes 331784 | tf_op jit(solution)/shard_map/ppermute | solution.py:31
  93.7 10.4 %collective-permute-start.18 = (bf16[28,16,128]{2,1,0:T(8,128)(2,1)S(1)}, bf16[28,16,128]{2,1,0:T(8,128)(2,1)S(1)}, u32[]{:S(2)}, u32[]{:S(2)}) collective-permute-start(bf16[28,16,128]{2,1,0:T(8,128)(2,1)S(1)} %pad_maximum_fusion.4), channel_id=1, source_target_pairs={{0,64},{64,128},{128,192},{192,0},{1,65},{65,129},{129,193},{193,1... | collective-permute-start | bytes 344072 | tf_op jit(solution)/shard_map/ppermute | solution.py:31
  94.2 9.9 %collective-permute-start.19 = (bf16[28,16,128]{2,1,0:T(8,128)(2,1)S(1)}, bf16[28,16,128]{2,1,0:T(8,128)(2,1)S(1)}, u32[]{:S(2)}, u32[]{:S(2)}) collective-permute-start(bf16[28,16,128]{2,1,0:T(8,128)(2,1)S(1)} %pad_maximum_fusion.4), channel_id=1, source_target_pairs={{0,128},{64,192},{128,0},{192,64},{1,129},{65,193},{129,1},{193,65... | collective-permute-start | bytes 344072 | tf_op jit(solution)/shard_map/ppermute | solution.py:31
  97.0 7.0 %collective-permute-start.20 = (bf16[28,16,128]{2,1,0:T(8,128)(2,1)S(1)}, bf16[28,16,128]{2,1,0:T(8,128)(2,1)S(1)}, u32[]{:S(2)}, u32[]{:S(2)}) collective-permute-start(bf16[28,16,128]{2,1,0:T(8,128)(2,1)S(1)} %pad_maximum_fusion.4), channel_id=1, source_target_pairs={{0,192},{64,0},{128,64},{192,128},{1,193},{65,1},{129,65},{193,129... | collective-permute-start | bytes 344072 | tf_op jit(solution)/shard_map/ppermute | solution.py:31
  97.0 5.4 %collective-permute-start.16 = (bf16[27,16,128]{2,1,0:T(8,128)(2,1)S(1)}, bf16[27,16,128]{2,1,0:T(8,128)(2,1)S(1)}, u32[]{:S(2)}, u32[]{:S(2)}) collective-permute-start(bf16[27,16,128]{2,1,0:T(8,128)(2,1)S(1)} %pad_maximum_fusion.5), channel_id=1, source_target_pairs={{0,2},{1,3},{2,0},{3,1},{4,6},{5,7},{6,4},{7,5},{8,10},{9,11},{10,... | collective-permute-start | bytes 331784 | tf_op jit(solution)/shard_map/ppermute | solution.py:31
  99.0 5.0 %collective-permute-start.17 = (bf16[27,16,128]{2,1,0:T(8,128)(2,1)S(1)}, bf16[27,16,128]{2,1,0:T(8,128)(2,1)S(1)}, u32[]{:S(2)}, u32[]{:S(2)}) collective-permute-start(bf16[27,16,128]{2,1,0:T(8,128)(2,1)S(1)} %pad_maximum_fusion.5), channel_id=1, source_target_pairs={{0,3},{1,0},{2,1},{3,2},{4,7},{5,4},{6,5},{7,6},{8,11},{9,8},{10,9... | collective-permute-start | bytes 331784 | tf_op jit(solution)/shard_map/ppermute | solution.py:31
  104.2 12.7 %collective-permute-start.24 = (bf16[112,16,128]{2,1,0:T(8,128)(2,1)S(1)}, bf16[112,16,128]{2,1,0:T(8,128)(2,1)S(1)}, u32[]{:S(2)}, u32[]{:S(2)}) collective-permute-start(bf16[112,16,128]{2,1,0:T(8,128)(2,1)S(1)} %pad_maximum_fusion), channel_id=1, source_target_pairs={{0,1},{1,2},{2,3},{3,0},{4,5},{5,6},{6,7},{7,4},{8,9},{9,10},{10,1... | collective-permute-start | bytes 1376264 | tf_op jit(solution)/shard_map/ppermute | solution.py:285
  105.6 12.0 %collective-permute-start.26 = (bf16[112,16,128]{2,1,0:T(8,128)(2,1)S(1)}, bf16[112,16,128]{2,1,0:T(8,128)(2,1)S(1)}, u32[]{:S(2)}, u32[]{:S(2)}) collective-permute-start(bf16[112,16,128]{2,1,0:T(8,128)(2,1)S(1)} %pad_maximum_fusion), channel_id=1, source_target_pairs={{0,3},{1,0},{2,1},{3,2},{4,7},{5,4},{6,5},{7,6},{8,11},{9,8},{10,9... | collective-permute-start | bytes 1376264 | tf_op jit(solution)/shard_map/ppermute | solution.py:286
  108.0 13.0 %collective-permute-start.21 = (bf16[108,16,128]{2,1,0:T(8,128)(2,1)S(1)}, bf16[108,16,128]{2,1,0:T(8,128)(2,1)S(1)}, u32[]{:S(2)}, u32[]{:S(2)}) collective-permute-start(bf16[108,16,128]{2,1,0:T(8,128)(2,1)S(1)} %pad_maximum_fusion.1), channel_id=1, source_target_pairs={{0,64},{64,128},{128,192},{192,0},{1,65},{65,129},{129,193},{193,1... | collective-permute-start | bytes 1327112 | tf_op jit(solution)/shard_map/ppermute | solution.py:31
  108.5 18.1 %collective-permute-start.22 = (bf16[108,16,128]{2,1,0:T(8,128)(2,1)S(1)}, bf16[108,16,128]{2,1,0:T(8,128)(2,1)S(1)}, u32[]{:S(2)}, u32[]{:S(2)}) collective-permute-start(bf16[108,16,128]{2,1,0:T(8,128)(2,1)S(1)} %pad_maximum_fusion.1), channel_id=1, source_target_pairs={{0,128},{64,192},{128,0},{192,64},{1,129},{65,193},{129,1},{193,65... | collective-permute-start | bytes 1327112 | tf_op jit(solution)/shard_map/ppermute | solution.py:31
  110.0 20.3 %collective-permute-start.23 = (bf16[108,16,128]{2,1,0:T(8,128)(2,1)S(1)}, bf16[108,16,128]{2,1,0:T(8,128)(2,1)S(1)}, u32[]{:S(2)}, u32[]{:S(2)}) collective-permute-start(bf16[108,16,128]{2,1,0:T(8,128)(2,1)S(1)} %pad_maximum_fusion.1), channel_id=1, source_target_pairs={{0,192},{64,0},{128,64},{192,128},{1,193},{65,1},{129,65},{193,129... | collective-permute-start | bytes 1327112 | tf_op jit(solution)/shard_map/ppermute | solution.py:31
  117.6 12.6 %collective-permute-start.25 = (bf16[56,16,128]{2,1,0:T(8,128)(2,1)}, bf16[56,16,128]{2,1,0:T(8,128)(2,1)S(1)}, u32[]{:S(2)}, u32[]{:S(2)}) collective-permute-start(bf16[56,16,128]{2,1,0:T(8,128)(2,1)} %slice.163), channel_id=1, source_target_pairs={{0,1},{1,2},{2,3},{3,0},{4,5},{5,6},{6,7},{7,4},{8,9},{9,10},{10,1... | collective-permute-start | bytes 688136 | tf_op jit(solution)/shard_map/ppermute | solution.py:288
  118.3 11.9 %collective-permute-start.27 = (bf16[56,16,128]{2,1,0:T(8,128)(2,1)}, bf16[56,16,128]{2,1,0:T(8,128)(2,1)}, u32[]{:S(2)}, u32[]{:S(2)}) collective-permute-start(bf16[56,16,128]{2,1,0:T(8,128)(2,1)} %slice.164), channel_id=1, source_target_pairs={{0,3},{1,0},{2,1},{3,2},{4,7},{5,4},{6,5},{7,6},{8,11},{9,8},{10,9... | collective-permute-start | bytes 688136 | tf_op jit(solution)/shard_map/ppermute | solution.py:289
  141.8 3.4 %collective-permute-start.28 = (bf16[64,128]{1,0:T(8,128)(2,1)S(1)}, bf16[64,128]{1,0:T(8,128)(2,1)S(1)}, u32[]{:S(2)}, u32[]{:S(2)}) collective-permute-start(bf16[64,128]{1,0:T(8,128)(2,1)S(1)} %fusion.11), channel_id=1, source_target_pairs={{0,4},{4,0},{1,5},{5,1},{2,6},{6,2},{3,7},{7,3},{8,12},{12,8},{9,1... | collective-permute-start | bytes 49160 | tf_op jit(solution)/shard_map/ppermute | solution.py:24
  143.5 4.1 %collective-permute-start.29 = (f32[96,128]{1,0:T(8,128)S(1)}, f32[96,128]{1,0:T(8,128)S(1)}, u32[]{:S(2)}, u32[]{:S(2)}) collective-permute-start(f32[96,128]{1,0:T(8,128)S(1)} %slice_bitcast_fusion), channel_id=1, source_target_pairs={{0,4},{4,0},{1,5},{5,1},{2,6},{6,2},{3,7},{7,3},{8,12},{12,8},{9,1... | collective-permute-start | bytes 147464 | tf_op jit(solution)/shard_map/ppermute | solution.py:24
  144.7 1.7 %collective-permute-start.30 = (f32[64,128]{1,0:T(8,128)S(1)}, f32[64,128]{1,0:T(8,128)S(1)}, u32[]{:S(2)}, u32[]{:S(2)}) collective-permute-start(f32[64,128]{1,0:T(8,128)S(1)} %bitcast.116), channel_id=1, source_target_pairs={{0,4},{4,0},{1,5},{5,1},{2,6},{6,2},{3,7},{7,3},{8,12},{12,8},{9,1... | collective-permute-start | bytes 98312 | tf_op jit(solution)/shard_map/ppermute | solution.py:24
  (9 other events, 109.0 us)

commit v3 on v2

--- a/solution.py
+++ b/solution.py
@@ -60,46 +60,97 @@
     return jnp.concatenate([real_part + real_part.T, imag_part - imag_part.T], axis=-1)
 
 
-def head_kernel(place, last, column, row, payload, gain_out):
-    pair = jnp.concatenate([row[...], row[...]], axis=1)
-    gain = -(column[...] * pair)
-    gain = jnp.concatenate([gain] * ROUNDS, axis=0)
-    gain_out[...] = gain
-    sigma = self_energy(last[0, 0], gain)
+def gain_of(row, first, count):
+    lane = lax.broadcasted_iota(jnp.int32, (count, ORB), 1)
+    line = lax.broadcasted_iota(jnp.int32, (count, ORB), 0)
+    mine = jnp.where(lane == line + first, jnp.broadcast_to(row, (count, ORB)), 0.0)
+    column = jnp.sum(mine, axis=1, keepdims=True)
+    return -(column * jnp.concatenate([row, row], axis=1))
+
+
+def hopped(blocks, hopping):
+    empty = jnp.zeros_like(hopping)
+    both = jnp.concatenate(
+        [
+            jnp.concatenate([hopping, empty], axis=1),
+            jnp.concatenate([empty, hopping], axis=1),
+        ],
+        axis=0,
+    )
+    return lax.dot_general(
+        blocks, both, (((1,), (1,)), ((), ())), preferred_element_type=jnp.float32
+    )
+
+
+def own_gain(coupling):
+    gain = gain_of(coupling, lax.axis_index("orb") * ROWS, ROWS)
+    return jnp.concatenate([gain] * ROUNDS, axis=0)
+
+
+LAST = pl.BlockSpec((1, 1, COLS, WIDE), lambda i: (ROUNDS - 1, TIMES // ROUNDS - 1, 0, 0))
+
+
+def plain(shape):
+    return pl.BlockSpec(shape, lambda i: (0,) * len(shape))
+
+
+def head_kernel(last, coupling, payload):
+    sigma = self_energy(last[0, 0], own_gain(coupling[...]))
     for z in range(ZS):
         payload[z] = sigma
 
 
-def head(place, rows_of, coupling):
+def head(rows_of, coupling):
+    shape = (ZS, COLS, WIDE)
     return pl.pallas_call(
         head_kernel,
-        grid_spec=pltpu.PrefetchScalarGridSpec(
-            num_scalar_prefetch=1,
-            grid=(1,),
-            in_specs=[
-                pl.BlockSpec(
-                    (1, 1, COLS, WIDE), lambda i, p: (ROUNDS - 1, TIMES // ROUNDS - 1, 0, 0)
-                ),
-                pl.BlockSpec((ROWS, 1), lambda i, p: (p[4], 0)),
-                pl.BlockSpec((1, ORB), lambda i, p: (0, 0)),
-            ],
-            out_specs=[
-                pl.BlockSpec((ZS, COLS, WIDE), lambda i, p: (0, 0, 0)),
-                pl.BlockSpec((COLS, WIDE), lambda i, p: (0, 0)),
-            ],
-        ),
-        out_shape=[
-            jax.ShapeDtypeStruct((ZS, COLS, WIDE), jnp.bfloat16),
-            jax.ShapeDtypeStruct((COLS, WIDE), jnp.float32),
-        ],
+        grid=(1,),
+        in_specs=[LAST, plain((1, ORB))],
+        out_specs=plain(shape),
+        out_shape=jax.ShapeDtypeStruct(shape, jnp.bfloat16),
         compiler_params=pltpu.CompilerParams(vmem_limit_bytes=56 * 1024 * 1024),
         name="head",
-    )(place, rows_of, coupling.reshape(ORB, 1), coupling.reshape(1, ORB))
-
-
-def collide_kernel(
-    place, own, other, a0, a1, a2, a3, b0, b1, low_two, high_two, b3, out, total, factor
-):
+    )(rows_of, coupling)
+
+
+def ring_sum(pieces):
+    a, b, c, d = pieces
+    return (a + c) + (b + d)
+
+
+def collect(place, riders, out):
+    x, y = place[3], place[4]
+    firsts, (b0, b1, low_two, high_two, b3) = riders[:XS], riders[XS:]
+    source = lax.rem(x + 1, XS)
+
+    def rider(index):
+        rows = []
+        for i in range(YS):
+            slab = firsts[0][lax.rem(y - i + YS, YS), index]
+            for d in range(1, XS):
+                slab = jnp.where(source == d, firsts[d][lax.rem(y - i + YS, YS), index], slab)
+            rows.append(slab)
+        return jnp.concatenate(rows, axis=0)
+
+    newest = joined(rider(0), rider(1))
+    corner = stepped(rider(2), hermitian(newest)).astype(jnp.bfloat16)
+    for i in range(YS):
+        rings = []
+        for dy in range(YS):
+            if dy == 2:
+                slabs = [low_two[0, i], low_two[1, i], high_two[0, i], high_two[1, i]]
+            else:
+                piece = (b0, b1, None, b3)[dy]
+                slabs = [piece[dx, i] for dx in range(XS)]
+            rings.append(ring_sum([slab.astype(jnp.float32) for slab in slabs]))
+        out[COLS + i * ROWS : COLS + (i + 1) * ROWS] = ring_sum(rings)
+    out[COLS + ORB :] = corner.astype(jnp.float32)
+
+
+def collide_kernel(place, own, other, *refs):
+    pieces, riders = refs[:9], refs[9:-4]
+    mine, swapped, total, factor = refs[-4:]
+    a0, a1, a2, a3, b0, b1, low_two, high_two, b3 = pieces
     step = pl.program_id(0)
     core, x, y = place[0], place[3], place[4]
     firsts = (a0, a1, a2, a3)
@@ -165,8 +216,10 @@
 
     @pl.when(step == STEPS - 1)
     def _():
-        for side in range(2):
-            out[side] = total[side, :, :WIDE] + times_i(total[side, :, WIDE:])
+        for side, out in enumerate((mine, swapped)):
+            out[:COLS] = total[side, :, :WIDE] + times_i(total[side, :, WIDE:])
+        if riders:
+            collect(place, riders, swapped)
 
 
 def collide(place, own, other, first, second):
@@ -174,26 +227,37 @@
         (ROUNDS, XS, DEEP, 1, COLS, WIDE), lambda i, p: (0, 0, i, p[0], 0, 0)
     )
     pieces = first + second
-    slabs = [
+    specs = [
         pl.BlockSpec((piece.shape[0], DEEP * HALF, ROWS, WIDE), lambda i, p: (0, i, 0, 0))
         for piece in pieces
     ]
+    riding = first[0].shape[1] > GROUP
+    riders = pieces if riding else []
+    for piece in riders:
+        extra = piece.shape[1] - GROUP
+        specs.append(
+            pl.BlockSpec(
+                (piece.shape[0], extra, ROWS, WIDE),
+                lambda i, p, at=GROUP // extra: (0, at, 0, 0),
+            )
+        )
+    rows = (COLS, COLS + 2 * ORB if riding else COLS)
     return pl.pallas_call(
         collide_kernel,
         grid_spec=pltpu.PrefetchScalarGridSpec(
             num_scalar_prefetch=1,
             grid=(STEPS,),
-            in_specs=[half, half] + slabs,
-            out_specs=pl.BlockSpec((2, COLS, WIDE), lambda i, p: (0, 0, 0)),
+            in_specs=[half, half] + specs,
+            out_specs=[pl.BlockSpec((n, WIDE), lambda i, p: (0, 0)) for n in rows],
             scratch_shapes=[
                 pltpu.VMEM((2, COLS, 2 * WIDE), jnp.float32),
                 pltpu.VMEM((HALF, XS * DEEP * WIDE, 2 * WIDE), jnp.bfloat16),
             ],
         ),
-        out_shape=jax.ShapeDtypeStruct((2, COLS, WIDE), jnp.float32),
+        out_shape=[jax.ShapeDtypeStruct((n, WIDE), jnp.float32) for n in rows],
         compiler_params=pltpu.CompilerParams(vmem_limit_bytes=48 * 1024 * 1024),
         name="collide",
-    )(place, own, other, *pieces)
+    )(place, own, other, *pieces, *riders)
 
 
 def pair(value):
@@ -205,13 +269,11 @@
     return high.astype(jnp.float32) + low.astype(jnp.float32)
 
 
-def update_kernel(sums, theirs, last, hop, gain, row_out, payload):
-    older = last[...]
-    change = jnp.dot(older, hop[...], preferred_element_type=jnp.float32) + STEP * (
-        sums[0] + theirs[...]
-    )
+def update_kernel(ours, theirs, last, hopping, coupling, row_out, payload):
+    older = last[0, 0]
+    change = hopped(older, hopping[...]) + STEP * (ours[...] + theirs[...])
     row = stepped(older, change).astype(jnp.bfloat16)
-    sigma = self_energy(row, gain[...])
+    sigma = self_energy(row, own_gain(coupling[...]))
     row_out[...] = row
     overlap = lax.dot_general(
         row, sigma, (((0,), (0,)), ((), ())), preferred_element_type=jnp.float32
@@ -223,33 +285,58 @@
         payload[z] = whole
 
 
-def update(sums, theirs, last, hop, gain):
+def update(ours, theirs, rows_of, hopping, coupling):
+    shapes = [(COLS, WIDE), (ZS, COLS + EXTRA * ROWS + ORB, WIDE)]
     return pl.pallas_call(
         update_kernel,
-        out_shape=[
-            jax.ShapeDtypeStruct((COLS, WIDE), jnp.bfloat16),
-            jax.ShapeDtypeStruct((ZS, COLS + EXTRA * ROWS + ORB, WIDE), jnp.bfloat16),
+        grid=(1,),
+        in_specs=[
+            plain((COLS, WIDE)),
+            plain((COLS, WIDE)),
+            LAST,
+            plain((ORB, ORB)),
+            plain((1, ORB)),
         ],
+        out_specs=[plain(shape) for shape in shapes],
+        out_shape=[jax.ShapeDtypeStruct(shape, jnp.bfloat16) for shape in shapes],
+        compiler_params=pltpu.CompilerParams(vmem_limit_bytes=56 * 1024 * 1024),
         name="update",
-    )(sums, theirs, last, hop, gain)
-
-
-def close_kernel(sums, theirs, row, hop, corner_factor, row_out):
+    )(ours, theirs, rows_of, hopping, coupling)
+
+
+def close_kernel(ours, kept, theirs, row, hopping, coupling, *refs):
+    row_two, corner_one, edge_two, corner_two, lines = refs
+    hop = hopping[...]
+    on_last = lax.axis_index("core") == 1
+    corner = jnp.where(on_last, kept[COLS + ORB :], theirs[COLS + ORB :]).astype(jnp.bfloat16)
+    column = kept[COLS : COLS + ORB] + theirs[COLS : COLS + ORB]
+    corner_factor = matrix_of(self_energy(corner, gain_of(coupling[...], 0, ORB)))
     older = row[...]
     change = (
-        jnp.dot(older, hop[...], preferred_element_type=jnp.float32)
-        + jnp.dot(older, corner_factor[...], preferred_element_type=jnp.float32)
-        + STEP * (sums[0] + theirs[...])
-    )
-    row_out[...] = stepped(older, change).astype(jnp.bfloat16)
-
-
-def close(sums, theirs, row, hop, corner_factor):
+        hopped(older, hop)
+        + jnp.dot(older, corner_factor, preferred_element_type=jnp.float32)
+        + STEP * (ours[...] + theirs[:COLS])
+    )
+    row_two[...] = stepped(older, change).astype(jnp.bfloat16)
+    edge_change = hopped(corner, hop) + STEP * (
+        column + jnp.dot(corner, corner_factor, preferred_element_type=jnp.float32)
+    )
+    lines[0] = corner.astype(jnp.float32)
+    lines[1] = stepped(corner, edge_change)
+    lines[2] = stepped(corner, hermitian(edge_change))
+    own = pl.ds(pl.multiple_of(lax.axis_index("orb") * ROWS, ROWS), ROWS)
+    for i, out in enumerate((corner_one, edge_two, corner_two)):
+        out[...] = lines[i, own, :].astype(jnp.bfloat16)
+
+
+def close(ours, kept, theirs, row, hopping, coupling):
+    shapes = [(COLS, WIDE)] + [(ROWS, WIDE)] * 3
     return pl.pallas_call(
         close_kernel,
-        out_shape=jax.ShapeDtypeStruct((COLS, WIDE), jnp.bfloat16),
+        out_shape=[jax.ShapeDtypeStruct(shape, jnp.bfloat16) for shape in shapes],
+        scratch_shapes=[pltpu.VMEM((3, ORB, WIDE), jnp.float32)],
         name="close",
-    )(sums, theirs, row, hop, corner_factor)
+    )(ours, kept, theirs, row, hopping, coupling)
 
 
 def body(history, hopping, coupling):
@@ -259,19 +346,7 @@
     place = jnp.stack([core, owner, owner + 1 - 2 * core, x, y]).astype(jnp.int32)
     table = history.reshape(ROUNDS, XS, ZS, CORES, COLS, WIDE)
     rows_of = history.reshape(ROUNDS, TIMES // ROUNDS, COLS, WIDE)
-    turned = hopping.T
-    empty = jnp.zeros_like(turned)
-    hop = jnp.concatenate(
-        [
-            jnp.concatenate([turned, empty], axis=1),
-            jnp.concatenate([empty, turned], axis=1),
-        ],
-        axis=0,
-    )
-    corner_gain = -(coupling[:, None] * jnp.concatenate([coupling, coupling])[None, :])
-
-    def own_rows(whole):
-        return lax.dynamic_slice_in_dim(whole, y * ROWS, ROWS, 0)
+    coupling = coupling.reshape(1, ORB)
 
     def along_both(first, second):
         first, second = lax.optimization_barrier((first, second))
@@ -301,20 +376,12 @@
             parts[:, HALF:ROUNDS].reshape(GROUP, ROWS, WIDE),
         )
 
-    def ring_sum(pieces):
-        a, b, c, d = pieces
-        return (a + c) + (b + d)
-
     other = swap_cores(table)
-    payload, gains = head(place, rows_of, coupling)
-    planes = lax.all_to_all(payload, "z", 0, 0)
-    last_row = rows_of[ROUNDS - 1, TIMES // ROUNDS - 1]
-    planes, other, last_row, hop, gains, corner_gain = lax.optimization_barrier(
-        (planes, other, last_row, hop, gains, corner_gain)
-    )
+    planes = lax.all_to_all(head(rows_of, coupling), "z", 0, 0)
+    planes, other = lax.optimization_barrier((planes, other))
     first, second = along_both(*plane_parts(planes))
-    sums = collide(place, table, other, first, second)
-    row_one, payload = update(sums, swap_cores(sums[1]), last_row, hop, gains)
+    ours, swapped = collide(place, table, other, first, second)
+    row_one, payload = update(ours, swap_cores(swapped), rows_of, hopping, coupling)
 
     planes = lax.all_to_all(payload, "z", 0, 0)
     first, second = plane_parts(planes)
@@ -325,36 +392,12 @@
         jnp.concatenate([first, riders]),
         jnp.concatenate([second, column.astype(jnp.bfloat16)]),
     )
-    from_last = lax.rem(x + 1, XS)
-    riders = first[0][:, GROUP:]
-    for d in range(1, XS):
-        riders = jnp.where(from_last == d, first[d][:, GROUP:], riders)
-    riders = jnp.stack([riders[d] for d in (3, 2, 1, 0, 3, 2, 1)])
-    riders = lax.dynamic_slice_in_dim(riders, 3 - y, YS, 0)
-    newest = joined(riders[:, 0], riders[:, 1]).reshape(ORB, WIDE)
-    corner = stepped(riders[:, 2].reshape(ORB, WIDE), hermitian(newest)).astype(jnp.bfloat16)
-    corner = jnp.where(core == 1, corner, swap_cores(corner))
-    columns = [piece[:, GROUP:].astype(jnp.float32) for piece in second]
-    columns = [columns[0], columns[1], jnp.concatenate(columns[2:4]), columns[4]]
-    column = ring_sum([ring_sum(piece) for piece in columns]).reshape(ORB, WIDE)
-    column = column + swap_cores(column)
-    corner_factor = matrix_of(self_energy(corner, corner_gain))
-    edge_change = jnp.dot(corner, hop, preferred_element_type=jnp.float32) + STEP * (
-        column + jnp.dot(corner, corner_factor, preferred_element_type=jnp.float32)
-    )
-    edge_two = own_rows(stepped(corner, edge_change)).astype(jnp.bfloat16)
-    corner_two = own_rows(stepped(corner, hermitian(edge_change))).astype(jnp.bfloat16)
-
-    sums = collide(place, table, other, first, second)
-    row_two = close(sums, swap_cores(sums[1]), row_one, hop, corner_factor)
+    ours, swapped = collide(place, table, other, first, second)
+    row_two, corner_one, edge_two, corner_two = close(
+        ours, swapped, swap_cores(swapped), row_one, hopping, coupling
+    )
     shape = (ROUNDS, 1, ROWS, WIDE)
-    return (
-        row_one.reshape(shape),
-        own_rows(corner),
-        row_two.reshape(shape),
-        edge_two,
-        corner_two,
-    )
+    return (row_one.reshape(shape), corner_one, row_two.reshape(shape), edge_two, corner_two)
 
 
 def solution(mesh):

time: 151 us -> 141 us (0.934)
  blocking collectives: 19.2 us -> 36.2 us
  starting transfers between devices: 47.8 us -> 40.5 us
  other arithmetic: 7.39 us -> 0.27 us
  waiting for transfers between devices: 46.8 us -> 40.5 us
  local copies, waits for them, and re-layouts: 7.49 us -> 2.65 us
    all_to_all x0 -> x1, blocking collectives: none -> 17.2 us  [body(): planes = lax.all_to_all(head(rows_of, coupling), 'z', 0, 0)]
    all_to_all x1 -> x0, waiting for transfers between devices: 8.36 us -> none  [body(): planes = lax.all_to_all(payload, 'z', 0, 0)]
    all_to_all x1 -> x0, starting transfers between devices: 6.45 us -> none  [body(): planes = lax.all_to_all(payload, 'z', 0, 0)]
    convert_element_type x9 -> x0, other arithmetic: 4.89 us -> none  [the longest x5 4.03 us: body(): columns = [piece[:, GROUP:].astype(jnp.float32) for piece in second]]
    ppermute x5 -> x3, starting transfers between devices: 7.73 us -> 6.85 us  [swap_cores(): return lax.ppermute(array, 'core', [(0, 1), (1, 0)])]
  transfers between devices with their start and end apart: 32 -> 29, of which waited for: 13 -> 14; matrix products, arithmetic and copies ran while one was open for 6% -> 0% of each run, Pallas kernels for 2% -> 1%
where the time goes in v3:
time: 141 us
  starting transfers between devices  40.5 us (29%)
  waiting for transfers between devices  40.5 us (29%)
  blocking collectives  36.2 us (26%)
  Pallas kernels  19.9 us (14%)
  local copies, waits for them, and re-layouts  2.65 us (2%)
    ppermute x18, waiting for transfers between devices, around(): pieces[distance] = lax.ppermute(array, axis, pairs)  29.4 us
    ppermute x18, starting transfers between devices, around(): pieces[distance] = lax.ppermute(array, axis, pairs)  21.8 us
    all_to_all x1, blocking collectives, body(): planes = lax.all_to_all(payload, 'z', 0, 0)  19 us
    all_to_all x1, blocking collectives, body(): planes = lax.all_to_all(head(rows_of, coupling), 'z', 0, 0)  17.2 us
    pallas_call x2, Pallas kernels, collide(): pl.pallas_call(collide_kernel, grid_spec=pltpu.PrefetchScalarGridSpec(num...  14 us
    ppermute x2, waiting for transfers between devices, along_again(): ahead = lax.ppermute(second, 'orb', [(i, (i + 1) % YS) for i in range(YS)])  9.29 us
    ppermute x3, starting transfers between devices, swap_cores(): return lax.ppermute(array, 'core', [(0, 1), (1, 0)])  6.85 us
    ppermute x2, starting transfers between devices, along_again(): lax.ppermute(behind[middle:], 'orb', [(i, (i + 3) % YS) for i in range(YS)])  5.46 us
  transfers between devices with their start and end apart: 29, of which 14 were waited for; matrix products, arithmetic and copies ran while one was open for 0% of the time, Pallas kernels for 1%

profile of v3, /device:TPU:1, one launch (start us, length us, event | category | flops | bytes accessed | tf_op | source)
XLA Modules:
  0.0 140.9 jit_solution(8226583349120732823)
XLA Ops:
  0.6 3.3 %collective-permute-start = (bf16[6,4,8,2,96,128]{5,4,3,2,1,0:T(8,128)(2,1)}, bf16[6,4,8,2,96,128]{5,4,3,2,1,0:T(8,128)(2,1)}, u32[]{:S(2)}, u32[]{:S(2)}) collective-permute-start(bf16[6,4,8,2,96,128]{5,4,3,2,1,0:T(8,128)(2,1)} %bitcast.67), channel_id=1, source_target_pairs={{0,4},{4,0},{1,5},{5,1},{2,6},{6,2},{3,7},{7,3},{8,12},{12,8},{9,1... | collective-permute-start | bytes 28311560 | tf_op jit(solution)/shard_map/ppermute | solution.py:24
  4.0 1.5 %head.1 = bf16[8,96,128]{2,1,0:T(8,128)(2,1)} custom-call(bf16[6,64,96,128]{3,2,1,0:T(8,128)(2,1)} %bitcast.68, f32[1,64]{1,0:T(1,128)} %bitcast.87), custom_call_target="tpu_custom_call" | custom-call | tf_op jit(solution)/shard_map/head/pallas_call | solution.py:105
  5.5 17.2 %all_to_all.10 = bf16[8,96,128]{2,1,0:T(8,128)(2,1)S(1)} all-to-all(bf16[8,96,128]{2,1,0:T(8,128)(2,1)} %head.1), channel_id=1, replica_groups=mesh['x'=4,'z'=8,'core'=2,'orb'=4] {'z'}, dimensions={0} | all-to-all | bytes 393216 | tf_op jit(solution)/shard_map/all_to_all | solution.py:380
  22.7 1.4 collective-permute-start.1
  24.1 2.6 %collective-permute-start.2 = (bf16[24,16,128]{2,1,0:T(8,128)(2,1)S(1)}, bf16[24,16,128]{2,1,0:T(8,128)(2,1)S(1)}, u32[]{:S(2)}, u32[]{:S(2)}) collective-permute-start(bf16[24,16,128]{2,1,0:T(8,128)(2,1)S(1)} %bitcast.81), channel_id=1, source_target_pairs={{0,2},{1,3},{2,0},{3,1},{4,6},{5,7},{6,4},{7,5},{8,10},{9,11},{10,... | collective-permute-start | bytes 294920 | tf_op jit(solution)/shard_map/ppermute | solution.py:31
  27.8 1.2 collective-permute-start.4
  29.0 2.5 %collective-permute-start.5 = (bf16[24,16,128]{2,1,0:T(8,128)(2,1)S(1)}, bf16[24,16,128]{2,1,0:T(8,128)(2,1)S(1)}, u32[]{:S(2)}, u32[]{:S(2)}) collective-permute-start(bf16[24,16,128]{2,1,0:T(8,128)(2,1)S(1)} %bitcast.77), channel_id=1, source_target_pairs={{0,128},{64,192},{128,0},{192,64},{1,129},{65,193},{129,1},{193,65... | collective-permute-start | bytes 294920 | tf_op jit(solution)/shard_map/ppermute | solution.py:31
  32.6 2.0 %collective-permute-done.5 = bf16[24,16,128]{2,1,0:T(8,128)(2,1)S(1)} collective-permute-done((bf16[24,16,128]{2,1,0:T(8,128)(2,1)S(1)}, bf16[24,16,128]{2,1,0:T(8,128)(2,1)S(1)}, u32[]{:S(2)}, u32[]{:S(2)}) %collective-permute-start.5) | collective-permute-done | bytes 98336 | tf_op jit(solution)/shard_map/ppermute | solution.py:31
  34.6 1.4 collective-permute-done.6
  36.6 2.3 %collective-permute-start.12 = (bf16[96,16,128]{2,1,0:T(8,128)(2,1)S(1)}, bf16[96,16,128]{2,1,0:T(8,128)(2,1)S(1)}, u32[]{:S(2)}, u32[]{:S(2)}) collective-permute-start(bf16[96,16,128]{2,1,0:T(8,128)(2,1)S(1)} %get-tuple-element.72), channel_id=1, source_target_pairs={{0,3},{1,0},{2,1},{3,2},{4,7},{5,4},{6,5},{7,6},{8,11},{9,8},{10,9... | collective-permute-start | bytes 1179656 | tf_op jit(solution)/shard_map/ppermute | solution.py:361
  38.9 3.5 %collective-permute-start.8 = (bf16[96,16,128]{2,1,0:T(8,128)(2,1)S(1)}, bf16[96,16,128]{2,1,0:T(8,128)(2,1)S(1)}, u32[]{:S(2)}, u32[]{:S(2)}) collective-permute-start(bf16[96,16,128]{2,1,0:T(8,128)(2,1)S(1)} %get-tuple-element.71), channel_id=1, source_target_pairs={{0,128},{64,192},{128,0},{192,64},{1,129},{65,193},{129,1},{193,65... | collective-permute-start | bytes 1179656 | tf_op jit(solution)/shard_map/ppermute | solution.py:31
  42.4 3.5 %collective-permute-done.10 = bf16[96,16,128]{2,1,0:T(8,128)(2,1)S(1)} collective-permute-done((bf16[96,16,128]{2,1,0:T(8,128)(2,1)S(1)}, bf16[96,16,128]{2,1,0:T(8,128)(2,1)S(1)}, u32[]{:S(2)}, u32[]{:S(2)}) %collective-permute-start.10) | collective-permute-done | bytes 393248 | tf_op jit(solution)/shard_map/ppermute | solution.py:360
  46.0 2.7 %collective-permute-start.13 = (bf16[48,16,128]{2,1,0:T(8,128)(2,1)S(1)}, bf16[48,16,128]{2,1,0:T(8,128)(2,1)S(1)}, u32[]{:S(2)}, u32[]{:S(2)}) collective-permute-start(bf16[48,16,128]{2,1,0:T(8,128)(2,1)S(1)} %slice.43), channel_id=1, source_target_pairs={{0,3},{1,0},{2,1},{3,2},{4,7},{5,4},{6,5},{7,6},{8,11},{9,8},{10,9... | collective-permute-start | bytes 589832 | tf_op jit(solution)/shard_map/ppermute | solution.py:364
  48.9 8.4 %collective-permute-done.8 = bf16[96,16,128]{2,1,0:T(8,128)(2,1)S(1)} collective-permute-done((bf16[96,16,128]{2,1,0:T(8,128)(2,1)S(1)}, bf16[96,16,128]{2,1,0:T(8,128)(2,1)S(1)}, u32[]{:S(2)}, u32[]{:S(2)}) %collective-permute-start.8) | collective-permute-done | bytes 393248 | tf_op jit(solution)/shard_map/ppermute | solution.py:31
  57.3 1.8 %collective-permute-done.9 = bf16[96,16,128]{2,1,0:T(8,128)(2,1)S(1)} collective-permute-done((bf16[96,16,128]{2,1,0:T(8,128)(2,1)S(1)}, bf16[96,16,128]{2,1,0:T(8,128)(2,1)S(1)}, u32[]{:S(2)}, u32[]{:S(2)}) %collective-permute-start.9) | collective-permute-done | bytes 393248 | tf_op jit(solution)/shard_map/ppermute | solution.py:31
  59.1 6.7 %collide.2 = (f32[96,128]{1,0:T(8,128)S(1)}, f32[96,128]{1,0:T(8,128)S(1)}) custom-call(s32[5]{0:T(128)S(1)} %stack.23.place, bf16[6,4,8,2,96,128]{5,4,3,2,1,0:T(8,128)(2,1)} %bitcast.69, bf16[6,4,8,2,96,128]{5,4,3,2,1,0:T(8,128)(2,1)} %collective-permute-done.other, bf16[4,24,16,128]{3,2,1,0:T(8,128)(2,1)S(1)} %bitcast.54, ...), custom_call_target="tpu_custom_call" | custom-call | tf_op jit(solution)/shard_map/collide/pallas_call | solution.py:245
  66.5 1.8 %collective-permute-start.14 = (f32[96,128]{1,0:T(8,128)S(1)}, f32[96,128]{1,0:T(8,128)S(1)}, u32[]{:S(2)}, u32[]{:S(2)}) collective-permute-start(f32[96,128]{1,0:T(8,128)S(1)} %get-tuple-element.83), channel_id=1, source_target_pairs={{0,4},{4,0},{1,5},{5,1},{2,6},{6,2},{3,7},{7,3},{8,12},{12,8},{9,1... | collective-permute-start | bytes 147464 | tf_op jit(solution)/shard_map/ppermute | solution.py:24
  69.8 2.2 %update.1 = (bf16[96,128]{1,0:T(8,128)(2,1)}, bf16[8,208,128]{2,1,0:T(8,128)(2,1)}) custom-call(f32[96,128]{1,0:T(8,128)} %copy-done.1, f32[96,128]{1,0:T(8,128)} %copy-done.4, bf16[6,64,96,128]{3,2,1,0:T(8,128)(2,1)} %bitcast.70, bf16[64,64]{1,0:T(8,128)(2,1)} %hopping.3, f32[1,64]{1,0:T(1,128)} %bitcast.88), custom_call_target="tpu_custom_call" | custom-call | tf_op jit(solution)/shard_map/update/pallas_call | solution.py:290
  72.0 19.0 %all_to_all.11 = bf16[8,208,128]{2,1,0:T(8,128)(2,1)S(1)} all-to-all(bf16[8,208,128]{2,1,0:T(8,128)(2,1)} %get-tuple-element.85), channel_id=1, replica_groups=mesh['x'=4,'z'=8,'core'=2,'orb'=4] {'z'}, dimensions={0} | all-to-all | bytes 851968 | tf_op jit(solution)/shard_map/all_to_all | solution.py:386
  91.5 3.1 %collective-permute-start.19 = (bf16[28,16,128]{2,1,0:T(8,128)(2,1)S(1)}, bf16[28,16,128]{2,1,0:T(8,128)(2,1)S(1)}, u32[]{:S(2)}, u32[]{:S(2)}) collective-permute-start(bf16[28,16,128]{2,1,0:T(8,128)(2,1)S(1)} %pad_maximum_fusion.4), channel_id=1, source_target_pairs={{0,128},{64,192},{128,0},{192,64},{1,129},{65,193},{129,1},{193,65... | collective-permute-start | bytes 344072 | tf_op jit(solution)/shard_map/ppermute | solution.py:31
  97.2 2.7 %collective-permute-done.16 = bf16[27,16,128]{2,1,0:T(8,128)(2,1)S(1)} collective-permute-done((bf16[27,16,128]{2,1,0:T(8,128)(2,1)S(1)}, bf16[27,16,128]{2,1,0:T(8,128)(2,1)S(1)}, u32[]{:S(2)}, u32[]{:S(2)}) %collective-permute-start.16) | collective-permute-done | bytes 110624 | tf_op jit(solution)/shard_map/ppermute | solution.py:31
  99.9 1.7 %collective-permute-done.17 = bf16[27,16,128]{2,1,0:T(8,128)(2,1)S(1)} collective-permute-done((bf16[27,16,128]{2,1,0:T(8,128)(2,1)S(1)}, bf16[27,16,128]{2,1,0:T(8,128)(2,1)S(1)}, u32[]{:S(2)}, u32[]{:S(2)}) %collective-permute-start.17) | collective-permute-done | bytes 110624 | tf_op jit(solution)/shard_map/ppermute | solution.py:31
  101.8 1.2 collective-permute-start.24
  103.1 2.3 %collective-permute-start.26 = (bf16[112,16,128]{2,1,0:T(8,128)(2,1)S(1)}, bf16[112,16,128]{2,1,0:T(8,128)(2,1)S(1)}, u32[]{:S(2)}, u32[]{:S(2)}) collective-permute-start(bf16[112,16,128]{2,1,0:T(8,128)(2,1)S(1)} %pad_maximum_fusion), channel_id=1, source_target_pairs={{0,3},{1,0},{2,1},{3,2},{4,7},{5,4},{6,5},{7,6},{8,11},{9,8},{10,9... | collective-permute-start | bytes 1376264 | tf_op jit(solution)/shard_map/ppermute | solution.py:361
  105.8 1.3 collective-permute-start.22
  108.2 5.8 %collective-permute-done.24 = bf16[112,16,128]{2,1,0:T(8,128)(2,1)S(1)} collective-permute-done((bf16[112,16,128]{2,1,0:T(8,128)(2,1)S(1)}, bf16[112,16,128]{2,1,0:T(8,128)(2,1)S(1)}, u32[]{:S(2)}, u32[]{:S(2)}) %collective-permute-start.24) | collective-permute-done | bytes 458784 | tf_op jit(solution)/shard_map/ppermute | solution.py:360
  114.1 2.7 %collective-permute-start.27 = (bf16[56,16,128]{2,1,0:T(8,128)(2,1)S(1)}, bf16[56,16,128]{2,1,0:T(8,128)(2,1)S(1)}, u32[]{:S(2)}, u32[]{:S(2)}) collective-permute-start(bf16[56,16,128]{2,1,0:T(8,128)(2,1)S(1)} %slice.49), channel_id=1, source_target_pairs={{0,3},{1,0},{2,1},{3,2},{4,7},{5,4},{6,5},{7,6},{8,11},{9,8},{10,9... | collective-permute-start | bytes 688136 | tf_op jit(solution)/shard_map/ppermute | solution.py:364
  117.9 5.6 %collective-permute-done.22 = bf16[108,16,128]{2,1,0:T(8,128)(2,1)S(1)} collective-permute-done((bf16[108,16,128]{2,1,0:T(8,128)(2,1)S(1)}, bf16[108,16,128]{2,1,0:T(8,128)(2,1)S(1)}, u32[]{:S(2)}, u32[]{:S(2)}) %collective-permute-start.22) | collective-permute-done | bytes 442400 | tf_op jit(solution)/shard_map/ppermute | solution.py:31
  123.5 4.0 %collective-permute-done.23 = bf16[108,16,128]{2,1,0:T(8,128)(2,1)S(1)} collective-permute-done((bf16[108,16,128]{2,1,0:T(8,128)(2,1)S(1)}, bf16[108,16,128]{2,1,0:T(8,128)(2,1)S(1)}, u32[]{:S(2)}, u32[]{:S(2)}) %collective-permute-start.23) | collective-permute-done | bytes 442400 | tf_op jit(solution)/shard_map/ppermute | solution.py:31
  127.5 7.2 %collide.3 = (f32[96,128]{1,0:T(8,128)S(1)}, f32[224,128]{1,0:T(8,128)S(1)}) custom-call(s32[5]{0:T(128)S(1)} %stack.23.place, bf16[6,4,8,2,96,128]{5,4,3,2,1,0:T(8,128)(2,1)} %bitcast.71, bf16[6,4,8,2,96,128]{5,4,3,2,1,0:T(8,128)(2,1)} %collective-permute-done.other, bf16[4,27,16,128]{3,2,1,0:T(8,128)(2,1)S(1)} %bitcast.42, ...), custom_call_target="tpu_custom_call" | custom-call | tf_op jit(solution)/shard_map/collide/pallas_call | solution.py:245
  135.3 1.7 %collective-permute-start.28 = (f32[224,128]{1,0:T(8,128)S(1)}, f32[224,128]{1,0:T(8,128)S(1)}, u32[]{:S(2)}, u32[]{:S(2)}) collective-permute-start(f32[224,128]{1,0:T(8,128)S(1)} %get-tuple-element.108.kept), channel_id=1, source_target_pairs={{0,4},{4,0},{1,5},{5,1},{2,6},{6,2},{3,7},{7,3},{8,12},{12,8},{9,1... | collective-permute-start | bytes 344072 | tf_op jit(solution)/shard_map/ppermute | solution.py:24
  138.7 2.3 %close.1 = (bf16[96,128]{1,0:T(8,128)(2,1)}, bf16[16,128]{1,0:T(8,128)(2,1)}, bf16[16,128]{1,0:T(8,128)(2,1)}, bf16[16,128]{1,0:T(8,128)(2,1)}) custom-call(f32[96,128]{1,0:T(8,128)} %copy-done.2, f32[224,128]{1,0:T(8,128)} %copy-done, f32[224,128]{1,0:T(8,128)} %copy-done.3, bf16[96,128]{1,0:T(8,128)(2,1)} %get-tuple-element.84.row, ...), custom_call_target="tpu_custom_call" | custom-call | tf_op jit(solution)/shard_map/close/pallas_call | solution.py:334
  (57 shorter events, 13.3 us)
Async XLA Ops:
  0.6 22.1 %collective-permute-start = (bf16[6,4,8,2,96,128]{5,4,3,2,1,0:T(8,128)(2,1)}, bf16[6,4,8,2,96,128]{5,4,3,2,1,0:T(8,128)(2,1)}, u32[]{:S(2)}, u32[]{:S(2)}) collective-permute-start(bf16[6,4,8,2,96,128]{5,4,3,2,1,0:T(8,128)(2,1)} %bitcast.67), channel_id=1, source_target_pairs={{0,4},{4,0},{1,5},{5,1},{2,6},{6,2},{3,7},{7,3},{8,12},{12,8},{9,1... | collective-permute-start | bytes 28311560 | tf_op jit(solution)/shard_map/ppermute | solution.py:24
  22.7 8.7 %collective-permute-start.1 = (bf16[24,16,128]{2,1,0:T(8,128)(2,1)S(1)}, bf16[24,16,128]{2,1,0:T(8,128)(2,1)S(1)}, u32[]{:S(2)}, u32[]{:S(2)}) collective-permute-start(bf16[24,16,128]{2,1,0:T(8,128)(2,1)S(1)} %bitcast.80), channel_id=1, source_target_pairs={{0,1},{1,2},{2,3},{3,0},{4,5},{5,6},{6,7},{7,4},{8,9},{9,10},{10,1... | collective-permute-start | bytes 294920 | tf_op jit(solution)/shard_map/ppermute | solution.py:31
  24.1 8.5 %collective-permute-start.2 = (bf16[24,16,128]{2,1,0:T(8,128)(2,1)S(1)}, bf16[24,16,128]{2,1,0:T(8,128)(2,1)S(1)}, u32[]{:S(2)}, u32[]{:S(2)}) collective-permute-start(bf16[24,16,128]{2,1,0:T(8,128)(2,1)S(1)} %bitcast.81), channel_id=1, source_target_pairs={{0,2},{1,3},{2,0},{3,1},{4,6},{5,7},{6,4},{7,5},{8,10},{9,11},{10,... | collective-permute-start | bytes 294920 | tf_op jit(solution)/shard_map/ppermute | solution.py:31
  26.7 5.9 %collective-permute-start.3 = (bf16[24,16,128]{2,1,0:T(8,128)(2,1)S(1)}, bf16[24,16,128]{2,1,0:T(8,128)(2,1)S(1)}, u32[]{:S(2)}, u32[]{:S(2)}) collective-permute-start(bf16[24,16,128]{2,1,0:T(8,128)(2,1)S(1)} %bitcast.82), channel_id=1, source_target_pairs={{0,3},{1,0},{2,1},{3,2},{4,7},{5,4},{6,5},{7,6},{8,11},{9,8},{10,9... | collective-permute-start | bytes 294920 | tf_op jit(solution)/shard_map/ppermute | solution.py:31
  27.8 4.8 %collective-permute-start.4 = (bf16[24,16,128]{2,1,0:T(8,128)(2,1)S(1)}, bf16[24,16,128]{2,1,0:T(8,128)(2,1)S(1)}, u32[]{:S(2)}, u32[]{:S(2)}) collective-permute-start(bf16[24,16,128]{2,1,0:T(8,128)(2,1)S(1)} %bitcast.76), channel_id=1, source_target_pairs={{0,64},{64,128},{128,192},{192,0},{1,65},{65,129},{129,193},{193,1... | collective-permute-start | bytes 294920 | tf_op jit(solution)/shard_map/ppermute | solution.py:31
  29.0 5.6 %collective-permute-start.5 = (bf16[24,16,128]{2,1,0:T(8,128)(2,1)S(1)}, bf16[24,16,128]{2,1,0:T(8,128)(2,1)S(1)}, u32[]{:S(2)}, u32[]{:S(2)}) collective-permute-start(bf16[24,16,128]{2,1,0:T(8,128)(2,1)S(1)} %bitcast.77), channel_id=1, source_target_pairs={{0,128},{64,192},{128,0},{192,64},{1,129},{65,193},{129,1},{193,65... | collective-permute-start | bytes 294920 | tf_op jit(solution)/shard_map/ppermute | solution.py:31
  31.5 4.6 %collective-permute-start.6 = (bf16[24,16,128]{2,1,0:T(8,128)(2,1)S(1)}, bf16[24,16,128]{2,1,0:T(8,128)(2,1)S(1)}, u32[]{:S(2)}, u32[]{:S(2)}) collective-permute-start(bf16[24,16,128]{2,1,0:T(8,128)(2,1)S(1)} %bitcast.78), channel_id=1, source_target_pairs={{0,192},{64,0},{128,64},{192,128},{1,193},{65,1},{129,65},{193,129... | collective-permute-start | bytes 294920 | tf_op jit(solution)/shard_map/ppermute | solution.py:31
  36.1 9.8 %collective-permute-start.10 = (bf16[96,16,128]{2,1,0:T(8,128)(2,1)S(1)}, bf16[96,16,128]{2,1,0:T(8,128)(2,1)S(1)}, u32[]{:S(2)}, u32[]{:S(2)}) collective-permute-start(bf16[96,16,128]{2,1,0:T(8,128)(2,1)S(1)} %get-tuple-element.72), channel_id=1, source_target_pairs={{0,1},{1,2},{2,3},{3,0},{4,5},{5,6},{6,7},{7,4},{8,9},{9,10},{10,1... | collective-permute-start | bytes 1179656 | tf_op jit(solution)/shard_map/ppermute | solution.py:360
  36.6 9.4 %collective-permute-start.12 = (bf16[96,16,128]{2,1,0:T(8,128)(2,1)S(1)}, bf16[96,16,128]{2,1,0:T(8,128)(2,1)S(1)}, u32[]{:S(2)}, u32[]{:S(2)}) collective-permute-start(bf16[96,16,128]{2,1,0:T(8,128)(2,1)S(1)} %get-tuple-element.72), channel_id=1, source_target_pairs={{0,3},{1,0},{2,1},{3,2},{4,7},{5,4},{6,5},{7,6},{8,11},{9,8},{10,9... | collective-permute-start | bytes 1179656 | tf_op jit(solution)/shard_map/ppermute | solution.py:361
  38.9 10.0 %collective-permute-start.7 = (bf16[96,16,128]{2,1,0:T(8,128)(2,1)S(1)}, bf16[96,16,128]{2,1,0:T(8,128)(2,1)S(1)}, u32[]{:S(2)}, u32[]{:S(2)}) collective-permute-start(bf16[96,16,128]{2,1,0:T(8,128)(2,1)S(1)} %get-tuple-element.71), channel_id=1, source_target_pairs={{0,64},{64,128},{128,192},{192,0},{1,65},{65,129},{129,193},{193,1... | collective-permute-start | bytes 1179656 | tf_op jit(solution)/shard_map/ppermute | solution.py:31
  38.9 18.4 %collective-permute-start.8 = (bf16[96,16,128]{2,1,0:T(8,128)(2,1)S(1)}, bf16[96,16,128]{2,1,0:T(8,128)(2,1)S(1)}, u32[]{:S(2)}, u32[]{:S(2)}) collective-permute-start(bf16[96,16,128]{2,1,0:T(8,128)(2,1)S(1)} %get-tuple-element.71), channel_id=1, source_target_pairs={{0,128},{64,192},{128,0},{192,64},{1,129},{65,193},{129,1},{193,65... | collective-permute-start | bytes 1179656 | tf_op jit(solution)/shard_map/ppermute | solution.py:31
  42.4 16.7 %collective-permute-start.9 = (bf16[96,16,128]{2,1,0:T(8,128)(2,1)S(1)}, bf16[96,16,128]{2,1,0:T(8,128)(2,1)S(1)}, u32[]{:S(2)}, u32[]{:S(2)}) collective-permute-start(bf16[96,16,128]{2,1,0:T(8,128)(2,1)S(1)} %get-tuple-element.71), channel_id=1, source_target_pairs={{0,192},{64,0},{128,64},{192,128},{1,193},{65,1},{129,65},{193,129... | collective-permute-start | bytes 1179656 | tf_op jit(solution)/shard_map/ppermute | solution.py:31
  45.9 13.2 %collective-permute-start.11 = (bf16[48,16,128]{2,1,0:T(8,128)(2,1)S(1)}, bf16[48,16,128]{2,1,0:T(8,128)(2,1)S(1)}, u32[]{:S(2)}, u32[]{:S(2)}) collective-permute-start(bf16[48,16,128]{2,1,0:T(8,128)(2,1)S(1)} %slice.42), channel_id=1, source_target_pairs={{0,1},{1,2},{2,3},{3,0},{4,5},{5,6},{6,7},{7,4},{8,9},{9,10},{10,1... | collective-permute-start | bytes 589832 | tf_op jit(solution)/shard_map/ppermute | solution.py:363
  46.0 13.1 %collective-permute-start.13 = (bf16[48,16,128]{2,1,0:T(8,128)(2,1)S(1)}, bf16[48,16,128]{2,1,0:T(8,128)(2,1)S(1)}, u32[]{:S(2)}, u32[]{:S(2)}) collective-permute-start(bf16[48,16,128]{2,1,0:T(8,128)(2,1)S(1)} %slice.43), channel_id=1, source_target_pairs={{0,3},{1,0},{2,1},{3,2},{4,7},{5,4},{6,5},{7,6},{8,11},{9,8},{10,9... | collective-permute-start | bytes 589832 | tf_op jit(solution)/shard_map/ppermute | solution.py:364
  66.5 2.7 %collective-permute-start.14 = (f32[96,128]{1,0:T(8,128)S(1)}, f32[96,128]{1,0:T(8,128)S(1)}, u32[]{:S(2)}, u32[]{:S(2)}) collective-permute-start(f32[96,128]{1,0:T(8,128)S(1)} %get-tuple-element.83), channel_id=1, source_target_pairs={{0,4},{4,0},{1,5},{5,1},{2,6},{6,2},{3,7},{7,3},{8,12},{12,8},{9,1... | collective-permute-start | bytes 147464 | tf_op jit(solution)/shard_map/ppermute | solution.py:24
  69.1 0.6 copy-start.4
  91.1 5.2 %collective-permute-start.15 = (bf16[27,16,128]{2,1,0:T(8,128)(2,1)S(1)}, bf16[27,16,128]{2,1,0:T(8,128)(2,1)S(1)}, u32[]{:S(2)}, u32[]{:S(2)}) collective-permute-start(bf16[27,16,128]{2,1,0:T(8,128)(2,1)S(1)} %pad_maximum_fusion.5), channel_id=1, source_target_pairs={{0,1},{1,2},{2,3},{3,0},{4,5},{5,6},{6,7},{7,4},{8,9},{9,10},{10,1... | collective-permute-start | bytes 331784 | tf_op jit(solution)/shard_map/ppermute | solution.py:31
  91.2 10.5 %collective-permute-start.18 = (bf16[28,16,128]{2,1,0:T(8,128)(2,1)S(1)}, bf16[28,16,128]{2,1,0:T(8,128)(2,1)S(1)}, u32[]{:S(2)}, u32[]{:S(2)}) collective-permute-start(bf16[28,16,128]{2,1,0:T(8,128)(2,1)S(1)} %pad_maximum_fusion.4), channel_id=1, source_target_pairs={{0,64},{64,128},{128,192},{192,0},{1,65},{65,129},{129,193},{193,1... | collective-permute-start | bytes 344072 | tf_op jit(solution)/shard_map/ppermute | solution.py:31
  91.5 10.2 %collective-permute-start.19 = (bf16[28,16,128]{2,1,0:T(8,128)(2,1)S(1)}, bf16[28,16,128]{2,1,0:T(8,128)(2,1)S(1)}, u32[]{:S(2)}, u32[]{:S(2)}) collective-permute-start(bf16[28,16,128]{2,1,0:T(8,128)(2,1)S(1)} %pad_maximum_fusion.4), channel_id=1, source_target_pairs={{0,128},{64,192},{128,0},{192,64},{1,129},{65,193},{129,1},{193,65... | collective-permute-start | bytes 344072 | tf_op jit(solution)/shard_map/ppermute | solution.py:31
  94.5 7.1 %collective-permute-start.20 = (bf16[28,16,128]{2,1,0:T(8,128)(2,1)S(1)}, bf16[28,16,128]{2,1,0:T(8,128)(2,1)S(1)}, u32[]{:S(2)}, u32[]{:S(2)}) collective-permute-start(bf16[28,16,128]{2,1,0:T(8,128)(2,1)S(1)} %pad_maximum_fusion.4), channel_id=1, source_target_pairs={{0,192},{64,0},{128,64},{192,128},{1,193},{65,1},{129,65},{193,129... | collective-permute-start | bytes 344072 | tf_op jit(solution)/shard_map/ppermute | solution.py:31
  94.5 5.4 %collective-permute-start.16 = (bf16[27,16,128]{2,1,0:T(8,128)(2,1)S(1)}, bf16[27,16,128]{2,1,0:T(8,128)(2,1)S(1)}, u32[]{:S(2)}, u32[]{:S(2)}) collective-permute-start(bf16[27,16,128]{2,1,0:T(8,128)(2,1)S(1)} %pad_maximum_fusion.5), channel_id=1, source_target_pairs={{0,2},{1,3},{2,0},{3,1},{4,6},{5,7},{6,4},{7,5},{8,10},{9,11},{10,... | collective-permute-start | bytes 331784 | tf_op jit(solution)/shard_map/ppermute | solution.py:31
  96.3 5.4 %collective-permute-start.17 = (bf16[27,16,128]{2,1,0:T(8,128)(2,1)S(1)}, bf16[27,16,128]{2,1,0:T(8,128)(2,1)S(1)}, u32[]{:S(2)}, u32[]{:S(2)}) collective-permute-start(bf16[27,16,128]{2,1,0:T(8,128)(2,1)S(1)} %pad_maximum_fusion.5), channel_id=1, source_target_pairs={{0,3},{1,0},{2,1},{3,2},{4,7},{5,4},{6,5},{7,6},{8,11},{9,8},{10,9... | collective-permute-start | bytes 331784 | tf_op jit(solution)/shard_map/ppermute | solution.py:31
  101.8 12.2 %collective-permute-start.24 = (bf16[112,16,128]{2,1,0:T(8,128)(2,1)S(1)}, bf16[112,16,128]{2,1,0:T(8,128)(2,1)S(1)}, u32[]{:S(2)}, u32[]{:S(2)}) collective-permute-start(bf16[112,16,128]{2,1,0:T(8,128)(2,1)S(1)} %pad_maximum_fusion), channel_id=1, source_target_pairs={{0,1},{1,2},{2,3},{3,0},{4,5},{5,6},{6,7},{7,4},{8,9},{9,10},{10,1... | collective-permute-start | bytes 1376264 | tf_op jit(solution)/shard_map/ppermute | solution.py:360
  103.1 11.0 %collective-permute-start.26 = (bf16[112,16,128]{2,1,0:T(8,128)(2,1)S(1)}, bf16[112,16,128]{2,1,0:T(8,128)(2,1)S(1)}, u32[]{:S(2)}, u32[]{:S(2)}) collective-permute-start(bf16[112,16,128]{2,1,0:T(8,128)(2,1)S(1)} %pad_maximum_fusion), channel_id=1, source_target_pairs={{0,3},{1,0},{2,1},{3,2},{4,7},{5,4},{6,5},{7,6},{8,11},{9,8},{10,9... | collective-permute-start | bytes 1376264 | tf_op jit(solution)/shard_map/ppermute | solution.py:361
  105.3 12.6 %collective-permute-start.21 = (bf16[108,16,128]{2,1,0:T(8,128)(2,1)S(1)}, bf16[108,16,128]{2,1,0:T(8,128)(2,1)S(1)}, u32[]{:S(2)}, u32[]{:S(2)}) collective-permute-start(bf16[108,16,128]{2,1,0:T(8,128)(2,1)S(1)} %pad_maximum_fusion.1), channel_id=1, source_target_pairs={{0,64},{64,128},{128,192},{192,0},{1,65},{65,129},{129,193},{193,1... | collective-permute-start | bytes 1327112 | tf_op jit(solution)/shard_map/ppermute | solution.py:31
  105.8 17.6 %collective-permute-start.22 = (bf16[108,16,128]{2,1,0:T(8,128)(2,1)S(1)}, bf16[108,16,128]{2,1,0:T(8,128)(2,1)S(1)}, u32[]{:S(2)}, u32[]{:S(2)}) collective-permute-start(bf16[108,16,128]{2,1,0:T(8,128)(2,1)S(1)} %pad_maximum_fusion.1), channel_id=1, source_target_pairs={{0,128},{64,192},{128,0},{192,64},{1,129},{65,193},{129,1},{193,65... | collective-permute-start | bytes 1327112 | tf_op jit(solution)/shard_map/ppermute | solution.py:31
  107.1 20.4 %collective-permute-start.23 = (bf16[108,16,128]{2,1,0:T(8,128)(2,1)S(1)}, bf16[108,16,128]{2,1,0:T(8,128)(2,1)S(1)}, u32[]{:S(2)}, u32[]{:S(2)}) collective-permute-start(bf16[108,16,128]{2,1,0:T(8,128)(2,1)S(1)} %pad_maximum_fusion.1), channel_id=1, source_target_pairs={{0,192},{64,0},{128,64},{192,128},{1,193},{65,1},{129,65},{193,129... | collective-permute-start | bytes 1327112 | tf_op jit(solution)/shard_map/ppermute | solution.py:31
  114.0 13.5 %collective-permute-start.25 = (bf16[56,16,128]{2,1,0:T(8,128)(2,1)S(1)}, bf16[56,16,128]{2,1,0:T(8,128)(2,1)S(1)}, u32[]{:S(2)}, u32[]{:S(2)}) collective-permute-start(bf16[56,16,128]{2,1,0:T(8,128)(2,1)S(1)} %slice.48), channel_id=1, source_target_pairs={{0,1},{1,2},{2,3},{3,0},{4,5},{5,6},{6,7},{7,4},{8,9},{9,10},{10,1... | collective-permute-start | bytes 688136 | tf_op jit(solution)/shard_map/ppermute | solution.py:363
  114.1 13.4 %collective-permute-start.27 = (bf16[56,16,128]{2,1,0:T(8,128)(2,1)S(1)}, bf16[56,16,128]{2,1,0:T(8,128)(2,1)S(1)}, u32[]{:S(2)}, u32[]{:S(2)}) collective-permute-start(bf16[56,16,128]{2,1,0:T(8,128)(2,1)S(1)} %slice.49), channel_id=1, source_target_pairs={{0,3},{1,0},{2,1},{3,2},{4,7},{5,4},{6,5},{7,6},{8,11},{9,8},{10,9... | collective-permute-start | bytes 688136 | tf_op jit(solution)/shard_map/ppermute | solution.py:364
  135.3 2.7 %copy-start = (f32[224,128]{1,0:T(8,128)}, f32[224,128]{1,0:T(8,128)S(1)}, u32[]{:S(2)}) copy-start(f32[224,128]{1,0:T(8,128)S(1)} %get-tuple-element.108.kept) | copy-start | bytes 344068
  135.3 2.7 %collective-permute-start.28 = (f32[224,128]{1,0:T(8,128)S(1)}, f32[224,128]{1,0:T(8,128)S(1)}, u32[]{:S(2)}, u32[]{:S(2)}) collective-permute-start(f32[224,128]{1,0:T(8,128)S(1)} %get-tuple-element.108.kept), channel_id=1, source_target_pairs={{0,4},{4,0},{1,5},{5,1},{2,6},{6,2},{3,7},{7,3},{8,12},{12,8},{9,1... | collective-permute-start | bytes 344072 | tf_op jit(solution)/shard_map/ppermute | solution.py:24
  138.0 0.6 copy-start.3
  (2 other events, 1.2 us)

commit v4 on v3

v4 whole, which is shorter than its diff:
```python
import jax
import jax.numpy as jnp
from jax import lax
from jax.experimental import pallas as pl
from jax.experimental.pallas import tpu as pltpu
from jax.sharding import Mesh, PartitionSpec as P

STEP = 0.08
XS, ZS, CORES, YS = 4, 8, 2, 4
ROUNDS = 6
ORB = 64
ROWS = ORB // YS
WIDE = 2 * ORB
COLS = ROUNDS * ROWS
TIMES = ROUNDS * XS * ZS * CORES
EXTRA = 3
HALF = ROUNDS // 2
GROUP = ZS * HALF
SMALL = pltpu.CompilerParams(vmem_limit_bytes=8 * 1024 * 1024)


def swap_cores(array):
    return lax.ppermute(array, "core", [(0, 1), (1, 0)])


def around(array, axis):
    pieces = {0: array}
    for distance in (1, 3, 2):
        pairs = [(i, (i + distance) % 4) for i in range(4)]
        pieces[distance] = lax.ppermute(array, axis, pairs)
    return [pieces[d] for d in range(4)]


def halves_swapped(value):
    return jnp.concatenate([value[:, ORB:], value[:, :ORB]], axis=-1)


def times_i(value):
    return jnp.concatenate([-value[:, ORB:], value[:, :ORB]], axis=-1)


def matrix_of(value):
    return jnp.concatenate([value, times_i(value)], axis=0)


def stepped(older, change):
    return older.astype(jnp.float32) - STEP * times_i(change)


def self_energy(blocks, gain):
    parts = blocks.astype(jnp.float32)
    square = parts * parts
    return (gain * (square + halves_swapped(square)) * parts).astype(jnp.bfloat16)


def hermitian(whole):
    real_part = whole[:, :ORB]
    imag_part = whole[:, ORB:]
    return jnp.concatenate([real_part + real_part.T, imag_part - imag_part.T], axis=-1)


def gain_of(row, first, count):
    lane = lax.broadcasted_iota(jnp.int32, (count, ORB), 1)
    line = lax.broadcasted_iota(jnp.int32, (count, ORB), 0)
    mine = jnp.where(lane == line + first, jnp.broadcast_to(row, (count, ORB)), 0.0)
    column = jnp.sum(mine, axis=1, keepdims=True)
    return -(column * jnp.concatenate([row, row], axis=1))


def hopped(blocks, hopping):
    empty = jnp.zeros_like(hopping)
    both = jnp.concatenate(
        [
            jnp.concatenate([hopping, empty], axis=1),
            jnp.concatenate([empty, hopping], axis=1),
        ],
        axis=0,
    )
    return lax.dot_general(
        blocks, both, (((1,), (1,)), ((), ())), preferred_element_type=jnp.float32
    )


def own_gain(coupling):
    gain = gain_of(coupling, lax.axis_index("orb") * ROWS, ROWS)
    return jnp.concatenate([gain] * ROUNDS, axis=0)


LAST = pl.BlockSpec((1, 1, COLS, WIDE), lambda i: (ROUNDS - 1, TIMES // ROUNDS - 1, 0, 0))


def plain(shape):
    return pl.BlockSpec(shape, lambda i: (0,) * len(shape))


def head_kernel(last, coupling, payload, row):
    row[...] = last[0, 0]
    sigma = self_energy(last[0, 0], own_gain(coupling[...]))
    for z in range(ZS):
        payload[z] = sigma


def head(rows_of, coupling):
    shape = (ZS, COLS, WIDE)
    return pl.pallas_call(
        head_kernel,
        grid=(1,),
        in_specs=[LAST, plain((1, ORB))],
        out_specs=[plain(shape), plain((COLS, WIDE))],
        out_shape=[
            jax.ShapeDtypeStruct(shape, jnp.bfloat16),
            jax.ShapeDtypeStruct((COLS, WIDE), jnp.bfloat16),
        ],
        compiler_params=pltpu.CompilerParams(vmem_limit_bytes=56 * 1024 * 1024),
        name="head",
    )(rows_of, coupling)


def ring_sum(pieces):
    a, b, c, d = pieces
    return (a + c) + (b + d)


def collect(place, riders, out):
    x, y = place[3], place[4]
    firsts, (b0, b1, low_two, high_two, b3) = riders[:XS], riders[XS:]
    source = lax.rem(x + 1, XS)

    def rider(index):
        rows = []
        for i in range(YS):
            slab = firsts[0][lax.rem(y - i + YS, YS), GROUP + index]
            for d in range(1, XS):
                other = firsts[d][lax.rem(y - i + YS, YS), GROUP + index]
                slab = jnp.where(source == d, other, slab)
            rows.append(slab)
        return jnp.concatenate(rows, axis=0)

    newest = joined(rider(0), rider(1))
    corner = stepped(rider(2), hermitian(newest)).astype(jnp.bfloat16)
    for i in range(YS):
        rings = []
        for dy in range(YS):
            if dy == 2:
                halves = (low_two, high_two)
                slabs = [halves[dx // 2][dx % 2, GROUP + i] for dx in range(XS)]
            else:
                piece = (b0, b1, None, b3)[dy]
                slabs = [piece[dx, GROUP + i] for dx in range(XS)]
            rings.append(ring_sum([slab.astype(jnp.float32) for slab in slabs]))
        out[2 * COLS + i * ROWS : 2 * COLS + (i + 1) * ROWS] = ring_sum(rings)
    out[2 * COLS + ORB :] = corner.astype(jnp.float32)


def load_kernel(core, own, other, *refs):
    buffers, arrived = refs[:-1], refs[-1]
    copies = []
    for a in range(ROUNDS):
        rows = pl.ds(a * ROWS, COLS - a * ROWS)
        for side, table in enumerate((own, other)):
            i = a * CORES + side
            copies.append(
                pltpu.make_async_copy(
                    table.at[a, :, :, core[0], rows, :], buffers[i], arrived.at[i]
                )
            )
            copies[-1].start()
    for copy in copies:
        copy.wait()


def load(core, own, other):
    far = pl.BlockSpec(memory_space=pl.ANY)
    counts = [COLS - a * ROWS for a in range(ROUNDS) for _ in range(CORES)]
    return pl.pallas_call(
        load_kernel,
        in_specs=[pl.BlockSpec(memory_space=pltpu.SMEM), far, far],
        out_specs=[pl.BlockSpec(memory_space=pltpu.VMEM)] * len(counts),
        out_shape=[
            jax.ShapeDtypeStruct((XS, ZS, count, WIDE), jnp.bfloat16) for count in counts
        ],
        scratch_shapes=[pltpu.SemaphoreType.DMA((len(counts),))],
        compiler_params=pltpu.CompilerParams(vmem_limit_bytes=16 * 1024 * 1024),
        cost_estimate=pl.CostEstimate(
            flops=0, bytes_accessed=12000000, transcendentals=0
        ),
        name="load",
    )(core, own, other)


PARTS = 1


def collide_kernel(place, *refs):
    buffers, refs = refs[: ROUNDS * CORES], refs[ROUNDS * CORES :]
    pieces, out, total, factor = refs[:9], refs[9], refs[10], refs[11]
    a0, a1, a2, a3, b0, b1, low_two, high_two, b3 = pieces
    core, x, y = place[0], place[3], place[4]
    firsts = (a0, a1, a2, a3)
    sources = [lax.rem(x - dx + XS, XS) for dx in range(XS)]
    empty = jnp.zeros((ORB, WIDE), jnp.bfloat16)
    for dy in range(YS):
        row = pl.multiple_of(lax.rem(y - dy + YS, YS) * ROWS, ROWS)
        for dx in range(XS):
            if dy == 2:
                piece = (low_two, high_two)[dx // 2].at[dx % 2]
            else:
                piece = (b0, b1, None, b3)[dy].at[dx]
            for z in range(ZS):
                for r in range(HALF):
                    factor[r, dx * ZS + z, pl.ds(row, ROWS), :] = piece[z * HALF + r]

    for a in range(ROUNDS):
        low, count = a * ROWS, COLS - a * ROWS
        for part in range(PARTS):
            groups = [
                (dx, z)
                for dx in range(part * XS // PARTS, (part + 1) * XS // PARTS)
                for z in range(ZS)
            ]
            sides = []
            for side, target in enumerate((place[1], place[2])):
                table = buffers[a * CORES + side]
                blocks = []
                for dx, z in groups:
                    block = table[sources[dx], z]
                    time = (sources[dx] * ZS + z) * CORES + core
                    diagonal = jnp.where(
                        time <= target, block[:ROWS], jnp.zeros_like(block[:ROWS])
                    )
                    if count > ROWS:
                        diagonal = jnp.concatenate([diagonal, block[ROWS:]], axis=0)
                    blocks.append(diagonal)
                sides.append(jnp.concatenate(blocks, axis=1))
            blocks = []
            for dx, z in groups:
                if a < HALF:
                    block = jnp.concatenate(
                        [
                            firsts[dx][lax.rem(y - i + YS, YS), z * HALF + a]
                            for i in range(YS)
                        ],
                        axis=0,
                    )
                else:
                    block = factor[a - HALF, dx * ZS + z]
                blocks.append(jnp.concatenate([block, empty], axis=1))
                blocks.append(jnp.concatenate([empty, block], axis=1))
            product = jnp.dot(
                jnp.concatenate(sides, axis=0),
                jnp.concatenate(blocks, axis=0),
                preferred_element_type=jnp.float32,
            )
            if a == 0 and part == 0:
                total[0], total[1] = product[:count], product[count:]
            else:
                total[0, low:, :] += product[:count]
                total[1, low:, :] += product[count:]

    for side in range(2):
        rows = pl.ds(side * COLS, COLS)
        out[rows, :] = total[side, :, :WIDE] + times_i(total[side, :, WIDE:])
    if pieces[0].shape[1] > GROUP:
        collect(place, pieces, out)


def collide(place, history, first, second):
    pieces = first + second
    riding = first[0].shape[1] > GROUP
    shape = (2 * COLS + (2 * ORB if riding else 0), WIDE)
    whole = pl.BlockSpec(memory_space=pltpu.VMEM)
    return pl.pallas_call(
        collide_kernel,
        in_specs=[pl.BlockSpec(memory_space=pltpu.SMEM)]
        + [whole] * (len(history) + len(pieces)),
        out_specs=whole,
        scratch_shapes=[
            pltpu.VMEM((2, COLS, 2 * WIDE), jnp.float32),
            pltpu.VMEM((HALF, XS * ZS, ORB, WIDE), jnp.bfloat16),
        ],
        out_shape=jax.ShapeDtypeStruct(shape, jnp.float32),
        compiler_params=pltpu.CompilerParams(vmem_limit_bytes=24 * 1024 * 1024),
        name="collide",
    )(place, *history, *pieces)


def pair(value):
    high = value.astype(jnp.bfloat16)
    return high, (value - high.astype(jnp.float32)).astype(jnp.bfloat16)


def joined(high, low):
    return high.astype(jnp.float32) + low.astype(jnp.float32)


def update_kernel(sums, theirs, last, hopping, coupling, row_out, payload):
    older = last[...]
    change = hopped(older, hopping[...]) + STEP * (sums[:COLS] + theirs[...])
    row = stepped(older, change).astype(jnp.bfloat16)
    sigma = self_energy(row, own_gain(coupling[...]))
    row_out[...] = row
    overlap = lax.dot_general(
        row, sigma, (((0,), (0,)), ((), ())), preferred_element_type=jnp.float32
    )
    column = (times_i(overlap[ORB:]) - overlap[:ORB]).astype(jnp.bfloat16)
    riders = pair(change[COLS - ROWS :]) + (older[COLS - ROWS :], column)
    whole = jnp.concatenate((sigma,) + riders, axis=0)
    for z in range(ZS):
        payload[z] = whole


def update(sums, theirs, last, hopping, coupling):
    shapes = [(COLS, WIDE), (ZS, COLS + EXTRA * ROWS + ORB, WIDE)]
    return pl.pallas_call(
        update_kernel,
        out_shape=[jax.ShapeDtypeStruct(shape, jnp.bfloat16) for shape in shapes],
        compiler_params=SMALL,
        name="update",
    )(sums, theirs, last, hopping, coupling)


def close_kernel(sums, theirs, row, hopping, coupling, *refs):
    row_two, corner_one, edge_two, corner_two, lines = refs
    hop = hopping[...]
    on_last = lax.axis_index("core") == 1
    corner = jnp.where(on_last, sums[2 * COLS + ORB :], theirs[COLS + ORB :]).astype(jnp.bfloat16)
    column = sums[2 * COLS : 2 * COLS + ORB] + theirs[COLS : COLS + ORB]
    corner_factor = matrix_of(self_energy(corner, gain_of(coupling[...], 0, ORB)))
    older = row[...]
    change = (
        hopped(older, hop)
        + jnp.dot(older, corner_factor, preferred_element_type=jnp.float32)
        + STEP * (sums[:COLS] + theirs[:COLS])
    )
    row_two[...] = stepped(older, change).astype(jnp.bfloat16)
    edge_change = hopped(corner, hop) + STEP * (
        column + jnp.dot(corner, corner_factor, preferred_element_type=jnp.float32)
    )
    lines[0] = corner.astype(jnp.float32)
    lines[1] = stepped(corner, edge_change)
    lines[2] = stepped(corner, hermitian(edge_change))
    own = pl.ds(pl.multiple_of(lax.axis_index("orb") * ROWS, ROWS), ROWS)
    for i, out in enumerate((corner_one, edge_two, corner_two)):
        out[...] = lines[i, own, :].astype(jnp.bfloat16)


def close(sums, theirs, row, hopping, coupling):
    shapes = [(COLS, WIDE)] + [(ROWS, WIDE)] * 3
    return pl.pallas_call(
        close_kernel,
        out_shape=[jax.ShapeDtypeStruct(shape, jnp.bfloat16) for shape in shapes],
        scratch_shapes=[pltpu.VMEM((3, ORB, WIDE), jnp.float32)],
        compiler_params=SMALL,
        name="close",
    )(sums, theirs, row, hopping, coupling)


def body(history, hopping, coupling):
    x, z = lax.axis_index("x"), lax.axis_index("z")
    core, y = lax.axis_index("core"), lax.axis_index("orb")
    owner = (x * ZS + z) * CORES + core
    place = jnp.stack([core, owner, owner + 1 - 2 * core, x, y]).astype(jnp.int32)
    table = history.reshape(ROUNDS, XS, ZS, CORES, COLS, WIDE)
    rows_of = history.reshape(ROUNDS, TIMES // ROUNDS, COLS, WIDE)
    coupling = coupling.reshape(1, ORB)

    def along_one(first, second):
        first, second = lax.optimization_barrier((first, second))
        first, second = around(first, "orb"), around(second, "x")
        first, second = lax.optimization_barrier((first, second))
        first, second = jnp.concatenate(first), jnp.concatenate(second)
        return lax.optimization_barrier((first, second))

    def along_again(first, second):
        ahead = lax.ppermute(second, "orb", [(i, (i + 1) % YS) for i in range(YS)])
        behind = lax.ppermute(second, "orb", [(i, (i + 3) % YS) for i in range(YS)])
        middle = second.shape[0] // 2
        low = lax.ppermute(ahead[:middle], "orb", [(i, (i + 1) % YS) for i in range(YS)])
        high = lax.ppermute(behind[middle:], "orb", [(i, (i + 3) % YS) for i in range(YS)])
        first = [piece.reshape(YS, -1, ROWS, WIDE) for piece in around(first, "x")]
        second = [
            piece.reshape(-1, second.shape[0] // XS, ROWS, WIDE)
            for piece in (second, ahead, low, high, behind)
        ]
        return lax.optimization_barrier((first, second))

    def plane_parts(planes):
        parts = planes.reshape(ZS, -1, ROWS, WIDE)
        return (
            parts[:, :HALF].reshape(GROUP, ROWS, WIDE),
            parts[:, HALF:ROUNDS].reshape(GROUP, ROWS, WIDE),
        )

    other = swap_cores(table)
    payload, last_row = head(rows_of, coupling)
    planes = lax.all_to_all(payload, "z", 0, 0)
    planes, other = lax.optimization_barrier((planes, other))
    first, second = along_one(*plane_parts(planes))
    first, second, own, other, place = lax.optimization_barrier(
        (first, second, table, other, place)
    )
    history = load(place[:1], own, other)
    first, second = along_again(first, second)
    sums = collide(place, history, first, second)
    row_one, payload = update(sums, swap_cores(sums[COLS:]), last_row, hopping, coupling)

    planes = lax.all_to_all(payload, "z", 0, 0)
    first, second = plane_parts(planes)
    parts = planes.reshape(ZS, -1, ROWS, WIDE)
    riders = parts[ZS - 1, ROUNDS : ROUNDS + EXTRA]
    column = jnp.sum(parts[:, ROUNDS + EXTRA :].astype(jnp.float32), axis=0)
    first, second = along_again(
        *along_one(
            jnp.concatenate([first, riders]),
            jnp.concatenate([second, column.astype(jnp.bfloat16)]),
        )
    )
    sums = collide(place, history, first, second)
    row_two, corner_one, edge_two, corner_two = close(
        sums, swap_cores(sums[COLS:]), row_one, hopping, coupling
    )
    shape = (ROUNDS, 1, ROWS, WIDE)
    return (row_one.reshape(shape), corner_one, row_two.reshape(shape), edge_two, corner_two)


def solution(mesh):
    fine = Mesh(mesh.devices.reshape(XS, ZS, CORES, YS), ("x", "z", "core", "orb"))
    tm = ("x", "z", "core")
    return jax.shard_map(
        body,
        mesh=fine,
        in_specs=(P(None, None, None, tm, "orb", None), P(), P()),
        out_specs=(
            P(None, tm, "orb", None),
            P("orb", None),
            P(None, tm, "orb", None),
            P("orb", None),
            P("orb", None),
        ),
        check_vma=False,
    )
```

time: 141 us -> 130 us (0.922)
  Pallas kernels: 19.9 us -> 11.2 us
  starting transfers between devices: 40.5 us -> 33.9 us
  waiting for transfers between devices: 40.5 us -> 43.9 us
    all_to_all x1 -> x0, blocking collectives: 17.2 us -> none  [body(): planes = lax.all_to_all(head(rows_of, coupling), 'z', 0, 0)]
    all_to_all x1 -> x2, blocking collectives: 19 us -> 35.6 us  [body(): planes = lax.all_to_all(payload, 'z', 0, 0)]
    ppermute x2, waiting for transfers between devices: 9.29 us -> 0.01 us  [along_again(): ahead = lax.ppermute(second, 'orb', [(i, (i + 1) % YS) for i in range(YS)])]
    ppermute x2, waiting for transfers between devices: 0.01 us -> 8.02 us  [along_again(): behind = lax.ppermute(second, 'orb', [(i, (i + 3) % YS) for i in range(YS)])]
    pallas_call x3 -> x4, Pallas kernels: 16.2 us -> 8.37 us  [the longest x2 5.53 us: collide(): pl.pallas_call(collide_kernel, in_specs=[pl.BlockSpec(memory_space=pltpu....]
    ppermute x18, waiting for transfers between devices: 29.4 us -> 34 us  [around(): pieces[distance] = lax.ppermute(array, axis, pairs)]
    ppermute x18, starting transfers between devices: 21.8 us -> 18.4 us  [around(): pieces[distance] = lax.ppermute(array, axis, pairs)]
    ppermute x3, starting transfers between devices: 6.85 us -> 4.84 us  [swap_cores(): return lax.ppermute(array, 'core', [(0, 1), (1, 0)])]
  transfers between devices with their start and end apart: 29 -> 29, of which waited for: 14 -> 16; matrix products, arithmetic and copies ran while one was open for 0% -> 0% of each run, Pallas kernels for 1% -> 3%
where the time goes in v4:
time: 130 us
  waiting for transfers between devices  43.9 us (34%)
  blocking collectives  35.6 us (27%)
  starting transfers between devices  33.9 us (26%)
  Pallas kernels  11.2 us (9%)
  local copies, waits for them, and re-layouts  3.88 us (3%)
    all_to_all x2, blocking collectives, body(): planes = lax.all_to_all(payload, 'z', 0, 0)  35.6 us
    ppermute x18, waiting for transfers between devices, around(): pieces[distance] = lax.ppermute(array, axis, pairs)  34 us
    ppermute x18, starting transfers between devices, around(): pieces[distance] = lax.ppermute(array, axis, pairs)  18.4 us
    ppermute x2, waiting for transfers between devices, along_again(): behind = lax.ppermute(second, 'orb', [(i, (i + 3) % YS) for i in range(YS)])  8.02 us
    pallas_call x2, Pallas kernels, collide(): pl.pallas_call(collide_kernel, in_specs=[pl.BlockSpec(memory_space=pltpu....  5.53 us
    ppermute x2, starting transfers between devices, along_again(): lax.ppermute(behind[middle:], 'orb', [(i, (i + 3) % YS) for i in range(YS)])  5.32 us
    ppermute x3, starting transfers between devices, swap_cores(): return lax.ppermute(array, 'core', [(0, 1), (1, 0)])  4.84 us
    ppermute x2, starting transfers between devices, along_again(): behind = lax.ppermute(second, 'orb', [(i, (i + 3) % YS) for i in range(YS)])  4.39 us
  transfers between devices with their start and end apart: 29, of which 16 were waited for; matrix products, arithmetic and copies ran while one was open for 0% of the time, Pallas kernels for 3%

profile of v4, /device:TPU:1, one launch (start us, length us, event | category | flops | bytes accessed | tf_op | source)
XLA Modules:
  0.0 129.6 jit_solution(18387513891756083562)
XLA Ops:
  0.6 3.3 %collective-permute-start = (bf16[6,4,8,2,96,128]{5,4,3,2,1,0:T(8,128)(2,1)}, bf16[6,4,8,2,96,128]{5,4,3,2,1,0:T(8,128)(2,1)}, u32[]{:S(2)}, u32[]{:S(2)}) collective-permute-start(bf16[6,4,8,2,96,128]{5,4,3,2,1,0:T(8,128)(2,1)} %bitcast.41), channel_id=1, source_target_pairs={{0,4},{4,0},{1,5},{5,1},{2,6},{6,2},{3,7},{7,3},{8,12},{12,8},{9,1... | collective-permute-start | bytes 28311560 | tf_op jit(solution)/shard_map/ppermute | solution.py:23
  4.0 1.5 %head.1 = (bf16[8,96,128]{2,1,0:T(8,128)(2,1)}, bf16[96,128]{1,0:T(8,128)(2,1)}) custom-call(bf16[6,64,96,128]{3,2,1,0:T(8,128)(2,1)} %bitcast.42, f32[1,64]{1,0:T(1,128)} %bitcast.64), custom_call_target="tpu_custom_call" | custom-call | tf_op jit(solution)/shard_map/head/pallas_call | solution.py:105
  5.5 17.2 %all_to_all.10 = bf16[8,96,128]{2,1,0:T(8,128)(2,1)S(1)} all-to-all(bf16[8,96,128]{2,1,0:T(8,128)(2,1)} %get-tuple-element.74), channel_id=1, replica_groups=mesh['x'=4,'z'=8,'core'=2,'orb'=4] {'z'}, dimensions={0} | all-to-all | bytes 393216 | tf_op jit(solution)/shard_map/all_to_all | solution.py:396
  22.7 2.8 %collective-permute-start.3 = (bf16[24,16,128]{2,1,0:T(8,128)(2,1)S(1)}, bf16[24,16,128]{2,1,0:T(8,128)(2,1)S(1)}, u32[]{:S(2)}, u32[]{:S(2)}) collective-permute-start(bf16[24,16,128]{2,1,0:T(8,128)(2,1)S(1)} %bitcast.75), channel_id=1, source_target_pairs={{0,3},{1,0},{2,1},{3,2},{4,7},{5,4},{6,5},{7,6},{8,11},{9,8},{10,9... | collective-permute-start | bytes 294920 | tf_op jit(solution)/shard_map/ppermute | solution.py:30
  26.6 2.5 %collective-permute-start.6 = (bf16[24,16,128]{2,1,0:T(8,128)(2,1)S(1)}, bf16[24,16,128]{2,1,0:T(8,128)(2,1)S(1)}, u32[]{:S(2)}, u32[]{:S(2)}) collective-permute-start(bf16[24,16,128]{2,1,0:T(8,128)(2,1)S(1)} %bitcast.71), channel_id=1, source_target_pairs={{0,192},{64,0},{128,64},{192,128},{1,193},{65,1},{129,65},{193,129... | collective-permute-start | bytes 294920 | tf_op jit(solution)/shard_map/ppermute | solution.py:30
  30.6 2.8 %collective-permute-done.1 = bf16[24,16,128]{2,1,0:T(8,128)(2,1)S(1)} collective-permute-done((bf16[24,16,128]{2,1,0:T(8,128)(2,1)S(1)}, bf16[24,16,128]{2,1,0:T(8,128)(2,1)S(1)}, u32[]{:S(2)}, u32[]{:S(2)}) %collective-permute-start.1) | collective-permute-done | bytes 98336 | tf_op jit(solution)/shard_map/ppermute | solution.py:30
  34.1 1.0 collective-permute-done.4
  35.2 3.3 %collective-permute-start.12 = (bf16[96,16,128]{2,1,0:T(8,128)(2,1)S(1)}, bf16[96,16,128]{2,1,0:T(8,128)(2,1)S(1)}, u32[]{:S(2)}, u32[]{:S(2)}) collective-permute-start(bf16[96,16,128]{2,1,0:T(8,128)(2,1)S(1)} %get-tuple-element.105), channel_id=1, source_target_pairs={{0,3},{1,0},{2,1},{3,2},{4,7},{5,4},{6,5},{7,6},{8,11},{9,8},{10,9... | collective-permute-start | bytes 1179656 | tf_op jit(solution)/shard_map/ppermute | solution.py:376
  38.5 1.7 %collective-permute-start.9 = (bf16[96,16,128]{2,1,0:T(8,128)(2,1)S(1)}, bf16[96,16,128]{2,1,0:T(8,128)(2,1)S(1)}, u32[]{:S(2)}, u32[]{:S(2)}) collective-permute-start(bf16[96,16,128]{2,1,0:T(8,128)(2,1)S(1)} %get-tuple-element.104), channel_id=1, source_target_pairs={{0,192},{64,0},{128,64},{192,128},{1,193},{65,1},{129,65},{193,129... | collective-permute-start | bytes 1179656 | tf_op jit(solution)/shard_map/ppermute | solution.py:30
  41.3 3.5 %collective-permute-done.12 = bf16[96,16,128]{2,1,0:T(8,128)(2,1)S(1)} collective-permute-done((bf16[96,16,128]{2,1,0:T(8,128)(2,1)S(1)}, bf16[96,16,128]{2,1,0:T(8,128)(2,1)S(1)}, u32[]{:S(2)}, u32[]{:S(2)}) %collective-permute-start.12) | collective-permute-done | bytes 393248 | tf_op jit(solution)/shard_map/ppermute | solution.py:376
  44.8 3.5 %collective-permute-start.13 = (bf16[48,16,128]{2,1,0:T(8,128)(2,1)S(1)}, bf16[48,16,128]{2,1,0:T(8,128)(2,1)S(1)}, u32[]{:S(2)}, u32[]{:S(2)}) collective-permute-start(bf16[48,16,128]{2,1,0:T(8,128)(2,1)S(1)} %slice.55), channel_id=1, source_target_pairs={{0,3},{1,0},{2,1},{3,2},{4,7},{5,4},{6,5},{7,6},{8,11},{9,8},{10,9... | collective-permute-start | bytes 589832 | tf_op jit(solution)/shard_map/ppermute | solution.py:379
  48.6 3.7 %copy-done = bf16[6,64,6,1,16,128]{5,4,3,2,1,0:T(8,128)(2,1)S(1)} copy-done((bf16[6,64,6,1,16,128]{5,4,3,2,1,0:T(8,128)(2,1)S(1)}, bf16[6,64,6,1,16,128]{5,4,3,2,1,0:T(8,128)(2,1)}, u32[]{:S(2)}) %copy-start) | copy-done | bytes 9437208
  52.3 1.9 %load.1 = (bf16[4,8,96,128]{3,2,1,0:T(8,128)(2,1)S(1)}, bf16[4,8,96,128]{3,2,1,0:T(8,128)(2,1)S(1)}, bf16[4,8,80,128]{3,2,1,0:T(8,128)(2,1)S(1)}, bf16[4,8,80,12...) custom-call(s32[1]{0:T(128)S(1)} %bitcast.63, ...), custom_call_target="tpu_custom_call" | custom-call | bytes 12000000 | tf_op jit(solution)/shard_map/load/pallas_call | solution.py:175
  54.2 6.9 %collective-permute-done.7 = bf16[96,16,128]{2,1,0:T(8,128)(2,1)S(1)} collective-permute-done((bf16[96,16,128]{2,1,0:T(8,128)(2,1)S(1)}, bf16[96,16,128]{2,1,0:T(8,128)(2,1)S(1)}, u32[]{:S(2)}, u32[]{:S(2)}) %collective-permute-start.7) | collective-permute-done | bytes 393248 | tf_op jit(solution)/shard_map/ppermute | solution.py:30
  61.1 2.7 %collide.2.sums = f32[192,128]{1,0:T(8,128)S(1)} custom-call(s32[5]{0:T(128)S(1)} %stack.23.place, bf16[4,8,96,128]{3,2,1,0:T(8,128)(2,1)S(1)} %get-tuple-element.92.refs_0_, bf16[4,8,96,128]{3,2,1,0:T(8,128)(2,1)S(1)} %get-tuple-element.93.refs_1_, bf16[4,8,80,128]{3,2,1,0:T(8,128)(2,1)S(1)} %get-tuple-element.94.refs_2_, ...), custom_call_target="tpu_custom_call" | custom-call | tf_op jit(solution)/shard_map/collide/pallas_call | solution.py:272
  64.5 0.9 collective-permute-done.14.theirs
  65.4 0.9 update.1
  66.3 18.4 %all_to_all.11 = bf16[8,208,128]{2,1,0:T(8,128)(2,1)S(1)} all-to-all(bf16[8,208,128]{2,1,0:T(8,128)(2,1)S(1)} %get-tuple-element.117), channel_id=1, replica_groups=mesh['x'=4,'z'=8,'core'=2,'orb'=4] {'z'}, dimensions={0} | all-to-all | bytes 851968 | tf_op jit(solution)/shard_map/all_to_all | solution.py:407
  84.7 2.8 %collective-permute-start.17 = (bf16[27,16,128]{2,1,0:T(8,128)(2,1)S(1)}, bf16[27,16,128]{2,1,0:T(8,128)(2,1)S(1)}, u32[]{:S(2)}, u32[]{:S(2)}) collective-permute-start(bf16[27,16,128]{2,1,0:T(8,128)(2,1)S(1)} %pad_maximum_fusion.5), channel_id=1, source_target_pairs={{0,3},{1,0},{2,1},{3,2},{4,7},{5,4},{6,5},{7,6},{8,11},{9,8},{10,9... | collective-permute-start | bytes 331784 | tf_op jit(solution)/shard_map/ppermute | solution.py:30
  89.6 4.7 %collective-permute-done.16 = bf16[27,16,128]{2,1,0:T(8,128)(2,1)S(1)} collective-permute-done((bf16[27,16,128]{2,1,0:T(8,128)(2,1)S(1)}, bf16[27,16,128]{2,1,0:T(8,128)(2,1)S(1)}, u32[]{:S(2)}, u32[]{:S(2)}) %collective-permute-start.16) | collective-permute-done | bytes 110624 | tf_op jit(solution)/shard_map/ppermute | solution.py:30
  94.4 1.7 %collective-permute-done.15 = bf16[27,16,128]{2,1,0:T(8,128)(2,1)S(1)} collective-permute-done((bf16[27,16,128]{2,1,0:T(8,128)(2,1)S(1)}, bf16[27,16,128]{2,1,0:T(8,128)(2,1)S(1)}, u32[]{:S(2)}, u32[]{:S(2)}) %collective-permute-start.15) | collective-permute-done | bytes 110624 | tf_op jit(solution)/shard_map/ppermute | solution.py:30
  96.6 1.1 collective-permute-start.26
  98.1 3.0 %collective-permute-start.23 = (bf16[108,16,128]{2,1,0:T(8,128)(2,1)S(1)}, bf16[108,16,128]{2,1,0:T(8,128)(2,1)S(1)}, u32[]{:S(2)}, u32[]{:S(2)}) collective-permute-start(bf16[108,16,128]{2,1,0:T(8,128)(2,1)S(1)} %pad_maximum_fusion.1), channel_id=1, source_target_pairs={{0,192},{64,0},{128,64},{192,128},{1,193},{65,1},{129,65},{193,129... | collective-permute-start | bytes 1327112 | tf_op jit(solution)/shard_map/ppermute | solution.py:30
  101.9 4.5 %collective-permute-done.26 = bf16[112,16,128]{2,1,0:T(8,128)(2,1)S(1)} collective-permute-done((bf16[112,16,128]{2,1,0:T(8,128)(2,1)S(1)}, bf16[112,16,128]{2,1,0:T(8,128)(2,1)S(1)}, u32[]{:S(2)}, u32[]{:S(2)}) %collective-permute-start.26) | collective-permute-done | bytes 458784 | tf_op jit(solution)/shard_map/ppermute | solution.py:376
  106.4 1.8 %collective-permute-start.27 = (bf16[56,16,128]{2,1,0:T(8,128)(2,1)S(1)}, bf16[56,16,128]{2,1,0:T(8,128)(2,1)S(1)}, u32[]{:S(2)}, u32[]{:S(2)}) collective-permute-start(bf16[56,16,128]{2,1,0:T(8,128)(2,1)S(1)} %slice.62), channel_id=1, source_target_pairs={{0,3},{1,0},{2,1},{3,2},{4,7},{5,4},{6,5},{7,6},{8,11},{9,8},{10,9... | collective-permute-start | bytes 688136 | tf_op jit(solution)/shard_map/ppermute | solution.py:379
  108.6 3.0 %collective-permute-done.23 = bf16[108,16,128]{2,1,0:T(8,128)(2,1)S(1)} collective-permute-done((bf16[108,16,128]{2,1,0:T(8,128)(2,1)S(1)}, bf16[108,16,128]{2,1,0:T(8,128)(2,1)S(1)}, u32[]{:S(2)}, u32[]{:S(2)}) %collective-permute-start.23) | collective-permute-done | bytes 442400 | tf_op jit(solution)/shard_map/ppermute | solution.py:30
  111.6 0.9 collective-permute-done.22
  112.5 11.1 %collective-permute-done.21 = bf16[108,16,128]{2,1,0:T(8,128)(2,1)S(1)} collective-permute-done((bf16[108,16,128]{2,1,0:T(8,128)(2,1)S(1)}, bf16[108,16,128]{2,1,0:T(8,128)(2,1)S(1)}, u32[]{:S(2)}, u32[]{:S(2)}) %collective-permute-start.21) | collective-permute-done | bytes 442400 | tf_op jit(solution)/shard_map/ppermute | solution.py:30
  123.6 2.8 %collide.3.sums = f32[320,128]{1,0:T(8,128)S(1)} custom-call(s32[5]{0:T(128)S(1)} %stack.23.place, bf16[4,8,96,128]{3,2,1,0:T(8,128)(2,1)S(1)} %get-tuple-element.92.refs_0_, bf16[4,8,96,128]{3,2,1,0:T(8,128)(2,1)S(1)} %get-tuple-element.93.refs_1_, bf16[4,8,80,128]{3,2,1,0:T(8,128)(2,1)S(1)} %get-tuple-element.94.refs_2_, ...), custom_call_target="tpu_custom_call" | custom-call | tf_op jit(solution)/shard_map/collide/pallas_call | solution.py:272
  126.4 0.9 collective-permute-start.28
  127.3 1.0 collective-permute-done.28.theirs
  128.3 1.3 close.1
  (60 shorter events, 9.6 us)
Async XLA Ops:
  0.6 22.1 %collective-permute-start = (bf16[6,4,8,2,96,128]{5,4,3,2,1,0:T(8,128)(2,1)}, bf16[6,4,8,2,96,128]{5,4,3,2,1,0:T(8,128)(2,1)}, u32[]{:S(2)}, u32[]{:S(2)}) collective-permute-start(bf16[6,4,8,2,96,128]{5,4,3,2,1,0:T(8,128)(2,1)} %bitcast.41), channel_id=1, source_target_pairs={{0,4},{4,0},{1,5},{5,1},{2,6},{6,2},{3,7},{7,3},{8,12},{12,8},{9,1... | collective-permute-start | bytes 28311560 | tf_op jit(solution)/shard_map/ppermute | solution.py:23
  22.7 6.9 %collective-permute-start.3 = (bf16[24,16,128]{2,1,0:T(8,128)(2,1)S(1)}, bf16[24,16,128]{2,1,0:T(8,128)(2,1)S(1)}, u32[]{:S(2)}, u32[]{:S(2)}) collective-permute-start(bf16[24,16,128]{2,1,0:T(8,128)(2,1)S(1)} %bitcast.75), channel_id=1, source_target_pairs={{0,3},{1,0},{2,1},{3,2},{4,7},{5,4},{6,5},{7,6},{8,11},{9,8},{10,9... | collective-permute-start | bytes 294920 | tf_op jit(solution)/shard_map/ppermute | solution.py:30
  25.5 5.1 %collective-permute-start.2 = (bf16[24,16,128]{2,1,0:T(8,128)(2,1)S(1)}, bf16[24,16,128]{2,1,0:T(8,128)(2,1)S(1)}, u32[]{:S(2)}, u32[]{:S(2)}) collective-permute-start(bf16[24,16,128]{2,1,0:T(8,128)(2,1)S(1)} %bitcast.76), channel_id=1, source_target_pairs={{0,2},{1,3},{2,0},{3,1},{4,6},{5,7},{6,4},{7,5},{8,10},{9,11},{10,... | collective-permute-start | bytes 294920 | tf_op jit(solution)/shard_map/ppermute | solution.py:30
  25.9 7.5 %collective-permute-start.1 = (bf16[24,16,128]{2,1,0:T(8,128)(2,1)S(1)}, bf16[24,16,128]{2,1,0:T(8,128)(2,1)S(1)}, u32[]{:S(2)}, u32[]{:S(2)}) collective-permute-start(bf16[24,16,128]{2,1,0:T(8,128)(2,1)S(1)} %bitcast.77), channel_id=1, source_target_pairs={{0,1},{1,2},{2,3},{3,0},{4,5},{5,6},{6,7},{7,4},{8,9},{9,10},{10,1... | collective-permute-start | bytes 294920 | tf_op jit(solution)/shard_map/ppermute | solution.py:30
  26.6 6.8 %collective-permute-start.6 = (bf16[24,16,128]{2,1,0:T(8,128)(2,1)S(1)}, bf16[24,16,128]{2,1,0:T(8,128)(2,1)S(1)}, u32[]{:S(2)}, u32[]{:S(2)}) collective-permute-start(bf16[24,16,128]{2,1,0:T(8,128)(2,1)S(1)} %bitcast.71), channel_id=1, source_target_pairs={{0,192},{64,0},{128,64},{192,128},{1,193},{65,1},{129,65},{193,129... | collective-permute-start | bytes 294920 | tf_op jit(solution)/shard_map/ppermute | solution.py:30
  29.1 5.1 %collective-permute-start.5 = (bf16[24,16,128]{2,1,0:T(8,128)(2,1)S(1)}, bf16[24,16,128]{2,1,0:T(8,128)(2,1)S(1)}, u32[]{:S(2)}, u32[]{:S(2)}) collective-permute-start(bf16[24,16,128]{2,1,0:T(8,128)(2,1)S(1)} %bitcast.72), channel_id=1, source_target_pairs={{0,128},{64,192},{128,0},{192,64},{1,129},{65,193},{129,1},{193,65... | collective-permute-start | bytes 294920 | tf_op jit(solution)/shard_map/ppermute | solution.py:30
  29.6 5.5 %collective-permute-start.4 = (bf16[24,16,128]{2,1,0:T(8,128)(2,1)S(1)}, bf16[24,16,128]{2,1,0:T(8,128)(2,1)S(1)}, u32[]{:S(2)}, u32[]{:S(2)}) collective-permute-start(bf16[24,16,128]{2,1,0:T(8,128)(2,1)S(1)} %bitcast.73), channel_id=1, source_target_pairs={{0,64},{64,128},{128,192},{192,0},{1,65},{65,129},{129,193},{193,1... | collective-permute-start | bytes 294920 | tf_op jit(solution)/shard_map/ppermute | solution.py:30
  35.2 9.6 %collective-permute-start.12 = (bf16[96,16,128]{2,1,0:T(8,128)(2,1)S(1)}, bf16[96,16,128]{2,1,0:T(8,128)(2,1)S(1)}, u32[]{:S(2)}, u32[]{:S(2)}) collective-permute-start(bf16[96,16,128]{2,1,0:T(8,128)(2,1)S(1)} %get-tuple-element.105), channel_id=1, source_target_pairs={{0,3},{1,0},{2,1},{3,2},{4,7},{5,4},{6,5},{7,6},{8,11},{9,8},{10,9... | collective-permute-start | bytes 1179656 | tf_op jit(solution)/shard_map/ppermute | solution.py:376
  38.5 9.8 %collective-permute-start.10 = (bf16[96,16,128]{2,1,0:T(8,128)(2,1)S(1)}, bf16[96,16,128]{2,1,0:T(8,128)(2,1)S(1)}, u32[]{:S(2)}, u32[]{:S(2)}) collective-permute-start(bf16[96,16,128]{2,1,0:T(8,128)(2,1)S(1)} %get-tuple-element.105), channel_id=1, source_target_pairs={{0,1},{1,2},{2,3},{3,0},{4,5},{5,6},{6,7},{7,4},{8,9},{9,10},{10,1... | collective-permute-start | bytes 1179656 | tf_op jit(solution)/shard_map/ppermute | solution.py:375
  38.5 15.8 %collective-permute-start.9 = (bf16[96,16,128]{2,1,0:T(8,128)(2,1)S(1)}, bf16[96,16,128]{2,1,0:T(8,128)(2,1)S(1)}, u32[]{:S(2)}, u32[]{:S(2)}) collective-permute-start(bf16[96,16,128]{2,1,0:T(8,128)(2,1)S(1)} %get-tuple-element.104), channel_id=1, source_target_pairs={{0,192},{64,0},{128,64},{192,128},{1,193},{65,1},{129,65},{193,129... | collective-permute-start | bytes 1179656 | tf_op jit(solution)/shard_map/ppermute | solution.py:30
  40.2 14.1 %collective-permute-start.8 = (bf16[96,16,128]{2,1,0:T(8,128)(2,1)S(1)}, bf16[96,16,128]{2,1,0:T(8,128)(2,1)S(1)}, u32[]{:S(2)}, u32[]{:S(2)}) collective-permute-start(bf16[96,16,128]{2,1,0:T(8,128)(2,1)S(1)} %get-tuple-element.104), channel_id=1, source_target_pairs={{0,128},{64,192},{128,0},{192,64},{1,129},{65,193},{129,1},{193,65... | collective-permute-start | bytes 1179656 | tf_op jit(solution)/shard_map/ppermute | solution.py:30
  40.7 20.4 %collective-permute-start.7 = (bf16[96,16,128]{2,1,0:T(8,128)(2,1)S(1)}, bf16[96,16,128]{2,1,0:T(8,128)(2,1)S(1)}, u32[]{:S(2)}, u32[]{:S(2)}) collective-permute-start(bf16[96,16,128]{2,1,0:T(8,128)(2,1)S(1)} %get-tuple-element.104), channel_id=1, source_target_pairs={{0,64},{64,128},{128,192},{192,0},{1,65},{65,129},{129,193},{193,1... | collective-permute-start | bytes 1179656 | tf_op jit(solution)/shard_map/ppermute | solution.py:30
  44.8 16.3 %collective-permute-start.13 = (bf16[48,16,128]{2,1,0:T(8,128)(2,1)S(1)}, bf16[48,16,128]{2,1,0:T(8,128)(2,1)S(1)}, u32[]{:S(2)}, u32[]{:S(2)}) collective-permute-start(bf16[48,16,128]{2,1,0:T(8,128)(2,1)S(1)} %slice.55), channel_id=1, source_target_pairs={{0,3},{1,0},{2,1},{3,2},{4,7},{5,4},{6,5},{7,6},{8,11},{9,8},{10,9... | collective-permute-start | bytes 589832 | tf_op jit(solution)/shard_map/ppermute | solution.py:379
  48.3 12.8 %collective-permute-start.11 = (bf16[48,16,128]{2,1,0:T(8,128)(2,1)S(1)}, bf16[48,16,128]{2,1,0:T(8,128)(2,1)S(1)}, u32[]{:S(2)}, u32[]{:S(2)}) collective-permute-start(bf16[48,16,128]{2,1,0:T(8,128)(2,1)S(1)} %slice.54), channel_id=1, source_target_pairs={{0,1},{1,2},{2,3},{3,0},{4,5},{5,6},{6,7},{7,4},{8,9},{9,10},{10,1... | collective-permute-start | bytes 589832 | tf_op jit(solution)/shard_map/ppermute | solution.py:378
  52.3 13.1 %copy-start.3 = (bf16[96,128]{1,0:T(8,128)(2,1)S(1)}, bf16[96,128]{1,0:T(8,128)(2,1)}, u32[]{:S(2)}) copy-start(bf16[96,128]{1,0:T(8,128)(2,1)} %get-tuple-element.115.last) | copy-start | bytes 73732
  52.3 13.1 %copy-start.4 = (f32[64]{0:T(128)S(1)}, f32[64]{0:T(128)}, u32[]{:S(2)}) copy-start(f32[64]{0:T(128)} %param.5) | copy-start | bytes 772
  63.9 1.5 %collective-permute-start.14 = (f32[96,128]{1,0:T(8,128)S(1)}, f32[96,128]{1,0:T(8,128)S(1)}, u32[]{:S(2)}, u32[]{:S(2)}) collective-permute-start(f32[96,128]{1,0:T(8,128)S(1)} %slice.56), channel_id=1, source_target_pairs={{0,4},{4,0},{1,5},{5,1},{2,6},{6,2},{3,7},{7,3},{8,12},{12,8},{9,1... | collective-permute-start | bytes 147464 | tf_op jit(solution)/shard_map/ppermute | solution.py:23
  66.3 62.0 %copy-start.2 = (bf16[96,128]{1,0:T(8,128)(2,1)S(1)}, bf16[96,128]{1,0:T(8,128)(2,1)}, u32[]{:S(2)}) copy-start(bf16[96,128]{1,0:T(8,128)(2,1)} %get-tuple-element.116.row) | copy-start | bytes 73732
  84.7 4.7 %collective-permute-start.17 = (bf16[27,16,128]{2,1,0:T(8,128)(2,1)S(1)}, bf16[27,16,128]{2,1,0:T(8,128)(2,1)S(1)}, u32[]{:S(2)}, u32[]{:S(2)}) collective-permute-start(bf16[27,16,128]{2,1,0:T(8,128)(2,1)S(1)} %pad_maximum_fusion.5), channel_id=1, source_target_pairs={{0,3},{1,0},{2,1},{3,2},{4,7},{5,4},{6,5},{7,6},{8,11},{9,8},{10,9... | collective-permute-start | bytes 331784 | tf_op jit(solution)/shard_map/ppermute | solution.py:30
  87.5 8.6 %collective-permute-start.20 = (bf16[28,16,128]{2,1,0:T(8,128)(2,1)S(1)}, bf16[28,16,128]{2,1,0:T(8,128)(2,1)S(1)}, u32[]{:S(2)}, u32[]{:S(2)}) collective-permute-start(bf16[28,16,128]{2,1,0:T(8,128)(2,1)S(1)} %pad_maximum_fusion.4), channel_id=1, source_target_pairs={{0,192},{64,0},{128,64},{192,128},{1,193},{65,1},{129,65},{193,129... | collective-permute-start | bytes 344072 | tf_op jit(solution)/shard_map/ppermute | solution.py:30
  87.8 8.3 %collective-permute-start.19 = (bf16[28,16,128]{2,1,0:T(8,128)(2,1)S(1)}, bf16[28,16,128]{2,1,0:T(8,128)(2,1)S(1)}, u32[]{:S(2)}, u32[]{:S(2)}) collective-permute-start(bf16[28,16,128]{2,1,0:T(8,128)(2,1)S(1)} %pad_maximum_fusion.4), channel_id=1, source_target_pairs={{0,128},{64,192},{128,0},{192,64},{1,129},{65,193},{129,1},{193,65... | collective-permute-start | bytes 344072 | tf_op jit(solution)/shard_map/ppermute | solution.py:30
  88.3 8.1 %collective-permute-start.18 = (bf16[28,16,128]{2,1,0:T(8,128)(2,1)S(1)}, bf16[28,16,128]{2,1,0:T(8,128)(2,1)S(1)}, u32[]{:S(2)}, u32[]{:S(2)}) collective-permute-start(bf16[28,16,128]{2,1,0:T(8,128)(2,1)S(1)} %pad_maximum_fusion.4), channel_id=1, source_target_pairs={{0,64},{64,128},{128,192},{192,0},{1,65},{65,129},{129,193},{193,1... | collective-permute-start | bytes 344072 | tf_op jit(solution)/shard_map/ppermute | solution.py:30
  89.0 5.4 %collective-permute-start.16 = (bf16[27,16,128]{2,1,0:T(8,128)(2,1)S(1)}, bf16[27,16,128]{2,1,0:T(8,128)(2,1)S(1)}, u32[]{:S(2)}, u32[]{:S(2)}) collective-permute-start(bf16[27,16,128]{2,1,0:T(8,128)(2,1)S(1)} %pad_maximum_fusion.5), channel_id=1, source_target_pairs={{0,2},{1,3},{2,0},{3,1},{4,6},{5,7},{6,4},{7,5},{8,10},{9,11},{10,... | collective-permute-start | bytes 331784 | tf_op jit(solution)/shard_map/ppermute | solution.py:30
  89.5 6.7 %collective-permute-start.15 = (bf16[27,16,128]{2,1,0:T(8,128)(2,1)S(1)}, bf16[27,16,128]{2,1,0:T(8,128)(2,1)S(1)}, u32[]{:S(2)}, u32[]{:S(2)}) collective-permute-start(bf16[27,16,128]{2,1,0:T(8,128)(2,1)S(1)} %pad_maximum_fusion.5), channel_id=1, source_target_pairs={{0,1},{1,2},{2,3},{3,0},{4,5},{5,6},{6,7},{7,4},{8,9},{9,10},{10,1... | collective-permute-start | bytes 331784 | tf_op jit(solution)/shard_map/ppermute | solution.py:30
  96.6 9.8 %collective-permute-start.26 = (bf16[112,16,128]{2,1,0:T(8,128)(2,1)S(1)}, bf16[112,16,128]{2,1,0:T(8,128)(2,1)S(1)}, u32[]{:S(2)}, u32[]{:S(2)}) collective-permute-start(bf16[112,16,128]{2,1,0:T(8,128)(2,1)S(1)} %pad_maximum_fusion), channel_id=1, source_target_pairs={{0,3},{1,0},{2,1},{3,2},{4,7},{5,4},{6,5},{7,6},{8,11},{9,8},{10,9... | collective-permute-start | bytes 1376264 | tf_op jit(solution)/shard_map/ppermute | solution.py:376
  97.7 10.5 %collective-permute-start.24 = (bf16[112,16,128]{2,1,0:T(8,128)(2,1)S(1)}, bf16[112,16,128]{2,1,0:T(8,128)(2,1)S(1)}, u32[]{:S(2)}, u32[]{:S(2)}) collective-permute-start(bf16[112,16,128]{2,1,0:T(8,128)(2,1)S(1)} %pad_maximum_fusion), channel_id=1, source_target_pairs={{0,1},{1,2},{2,3},{3,0},{4,5},{5,6},{6,7},{7,4},{8,9},{9,10},{10,1... | collective-permute-start | bytes 1376264 | tf_op jit(solution)/shard_map/ppermute | solution.py:375
  98.1 13.5 %collective-permute-start.23 = (bf16[108,16,128]{2,1,0:T(8,128)(2,1)S(1)}, bf16[108,16,128]{2,1,0:T(8,128)(2,1)S(1)}, u32[]{:S(2)}, u32[]{:S(2)}) collective-permute-start(bf16[108,16,128]{2,1,0:T(8,128)(2,1)S(1)} %pad_maximum_fusion.1), channel_id=1, source_target_pairs={{0,192},{64,0},{128,64},{192,128},{1,193},{65,1},{129,65},{193,129... | collective-permute-start | bytes 1327112 | tf_op jit(solution)/shard_map/ppermute | solution.py:30
  101.1 11.4 %collective-permute-start.22 = (bf16[108,16,128]{2,1,0:T(8,128)(2,1)S(1)}, bf16[108,16,128]{2,1,0:T(8,128)(2,1)S(1)}, u32[]{:S(2)}, u32[]{:S(2)}) collective-permute-start(bf16[108,16,128]{2,1,0:T(8,128)(2,1)S(1)} %pad_maximum_fusion.1), channel_id=1, source_target_pairs={{0,128},{64,192},{128,0},{192,64},{1,129},{65,193},{129,1},{193,65... | collective-permute-start | bytes 1327112 | tf_op jit(solution)/shard_map/ppermute | solution.py:30
  101.2 22.4 %collective-permute-start.21 = (bf16[108,16,128]{2,1,0:T(8,128)(2,1)S(1)}, bf16[108,16,128]{2,1,0:T(8,128)(2,1)S(1)}, u32[]{:S(2)}, u32[]{:S(2)}) collective-permute-start(bf16[108,16,128]{2,1,0:T(8,128)(2,1)S(1)} %pad_maximum_fusion.1), channel_id=1, source_target_pairs={{0,64},{64,128},{128,192},{192,0},{1,65},{65,129},{129,193},{193,1... | collective-permute-start | bytes 1327112 | tf_op jit(solution)/shard_map/ppermute | solution.py:30
  106.4 17.2 %collective-permute-start.27 = (bf16[56,16,128]{2,1,0:T(8,128)(2,1)S(1)}, bf16[56,16,128]{2,1,0:T(8,128)(2,1)S(1)}, u32[]{:S(2)}, u32[]{:S(2)}) collective-permute-start(bf16[56,16,128]{2,1,0:T(8,128)(2,1)S(1)} %slice.62), channel_id=1, source_target_pairs={{0,3},{1,0},{2,1},{3,2},{4,7},{5,4},{6,5},{7,6},{8,11},{9,8},{10,9... | collective-permute-start | bytes 688136 | tf_op jit(solution)/shard_map/ppermute | solution.py:379
  108.2 15.3 %collective-permute-start.25 = (bf16[56,16,128]{2,1,0:T(8,128)(2,1)S(1)}, bf16[56,16,128]{2,1,0:T(8,128)(2,1)S(1)}, u32[]{:S(2)}, u32[]{:S(2)}) collective-permute-start(bf16[56,16,128]{2,1,0:T(8,128)(2,1)S(1)} %slice.61), channel_id=1, source_target_pairs={{0,1},{1,2},{2,3},{3,0},{4,5},{5,6},{6,7},{7,4},{8,9},{9,10},{10,1... | collective-permute-start | bytes 688136 | tf_op jit(solution)/shard_map/ppermute | solution.py:378
  126.4 1.9 %collective-permute-start.28 = (f32[224,128]{1,0:T(8,128)S(1)}, f32[224,128]{1,0:T(8,128)S(1)}, u32[]{:S(2)}, u32[]{:S(2)}) collective-permute-start(f32[224,128]{1,0:T(8,128)S(1)} %slice.63), channel_id=1, source_target_pairs={{0,4},{4,0},{1,5},{5,1},{2,6},{6,2},{3,7},{7,3},{8,12},{12,8},{9,1... | collective-permute-start | bytes 344072 | tf_op jit(solution)/shard_map/ppermute | solution.py:23
  (2 other events, 16.8 us)

commit v5 on v4

--- a/solution.py
+++ b/solution.py
@@ -121,17 +121,25 @@
     return (a + c) + (b + d)
 
 
+def piece_at(pieces, distance, index, slot):
+    if distance != 2:
+        return pieces[(0, 1, None, 4)[distance]][index, slot]
+    near = lax.rem(index, 2)
+    return jnp.where(index < 2, pieces[2][near, slot], pieces[3][near, slot])
+
+
 def collect(place, riders, out):
     x, y = place[3], place[4]
-    firsts, (b0, b1, low_two, high_two, b3) = riders[:XS], riders[XS:]
+    firsts, (b0, b1, low_two, high_two, b3) = riders[:5], riders[5:]
     source = lax.rem(x + 1, XS)
 
     def rider(index):
         rows = []
         for i in range(YS):
-            slab = firsts[0][lax.rem(y - i + YS, YS), GROUP + index]
+            at = lax.rem(y - i + YS, YS)
+            slab = piece_at(firsts, 0, at, GROUP + index)
             for d in range(1, XS):
-                other = firsts[d][lax.rem(y - i + YS, YS), GROUP + index]
+                other = piece_at(firsts, d, at, GROUP + index)
                 slab = jnp.where(source == d, other, slab)
             rows.append(slab)
         return jnp.concatenate(rows, axis=0)
@@ -180,7 +188,7 @@
             jax.ShapeDtypeStruct((XS, ZS, count, WIDE), jnp.bfloat16) for count in counts
         ],
         scratch_shapes=[pltpu.SemaphoreType.DMA((len(counts),))],
-        compiler_params=pltpu.CompilerParams(vmem_limit_bytes=16 * 1024 * 1024),
+        compiler_params=pltpu.CompilerParams(vmem_limit_bytes=47 * 1024 * 1024),
         cost_estimate=pl.CostEstimate(
             flops=0, bytes_accessed=12000000, transcendentals=0
         ),
@@ -193,10 +201,9 @@
 
 def collide_kernel(place, *refs):
     buffers, refs = refs[: ROUNDS * CORES], refs[ROUNDS * CORES :]
-    pieces, out, total, factor = refs[:9], refs[9], refs[10], refs[11]
-    a0, a1, a2, a3, b0, b1, low_two, high_two, b3 = pieces
+    pieces, (out, total, factor) = refs[:10], refs[10:]
+    firsts, (b0, b1, low_two, high_two, b3) = pieces[:5], pieces[5:]
     core, x, y = place[0], place[3], place[4]
-    firsts = (a0, a1, a2, a3)
     sources = [lax.rem(x - dx + XS, XS) for dx in range(XS)]
     empty = jnp.zeros((ORB, WIDE), jnp.bfloat16)
     for dy in range(YS):
@@ -237,7 +244,7 @@
                 if a < HALF:
                     block = jnp.concatenate(
                         [
-                            firsts[dx][lax.rem(y - i + YS, YS), z * HALF + a]
+                            piece_at(firsts, dx, lax.rem(y - i + YS, YS), z * HALF + a)
                             for i in range(YS)
                         ],
                         axis=0,
@@ -371,18 +378,21 @@
         first, second = jnp.concatenate(first), jnp.concatenate(second)
         return lax.optimization_barrier((first, second))
 
+    def ring(array, axis):
+        forward = [(i, (i + 1) % 4) for i in range(4)]
+        backward = [(i, (i + 3) % 4) for i in range(4)]
+        ahead = lax.ppermute(array, axis, forward)
+        behind = lax.ppermute(array, axis, backward)
+        middle = array.shape[0] // 2
+        low = lax.ppermute(ahead[:middle], axis, forward)
+        high = lax.ppermute(behind[middle:], axis, backward)
+        return [
+            piece.reshape(-1, array.shape[0] // 4, ROWS, WIDE)
+            for piece in (array, ahead, low, high, behind)
+        ]
+
     def along_again(first, second):
-        ahead = lax.ppermute(second, "orb", [(i, (i + 1) % YS) for i in range(YS)])
-        behind = lax.ppermute(second, "orb", [(i, (i + 3) % YS) for i in range(YS)])
-        middle = second.shape[0] // 2
-        low = lax.ppermute(ahead[:middle], "orb", [(i, (i + 1) % YS) for i in range(YS)])
-        high = lax.ppermute(behind[middle:], "orb", [(i, (i + 3) % YS) for i in range(YS)])
-        first = [piece.reshape(YS, -1, ROWS, WIDE) for piece in around(first, "x")]
-        second = [
-            piece.reshape(-1, second.shape[0] // XS, ROWS, WIDE)
-            for piece in (second, ahead, low, high, behind)
-        ]
-        return lax.optimization_barrier((first, second))
+        return lax.optimization_barrier((ring(first, "x"), ring(second, "orb")))
 
     def plane_parts(planes):
         parts = planes.reshape(ZS, -1, ROWS, WIDE)

time: 130 us -> 127 us (0.977)
  waiting for transfers between devices: 43.9 us -> 33.9 us
  starting transfers between devices: 33.9 us -> 43.7 us
  local copies, waits for them, and re-layouts: 3.88 us -> 0.27 us
    ppermute x18 -> x12, waiting for transfers between devices: 34 us -> 11.9 us  [around(): pieces[distance] = lax.ppermute(array, axis, pairs)]
    ppermute x8 -> x16, waiting for transfers between devices: 8.04 us -> 20.1 us  [the longest x4 10.8 us: ring(): behind = lax.ppermute(array, axis, backward)]
    ppermute x8 -> x16, starting transfers between devices: 10.7 us -> 19.9 us  [the longest x4 10.1 us: ring(): high = lax.ppermute(behind[middle:], axis, backward)]
    ppermute x3, starting transfers between devices: 4.84 us -> 11.3 us  [swap_cores(): return lax.ppermute(array, 'core', [(0, 1), (1, 0)])]
    ppermute x18 -> x12, starting transfers between devices: 18.4 us -> 12.4 us  [around(): pieces[distance] = lax.ppermute(array, axis, pairs)]
    unnamed x10 -> x8, local copies, waits for them, and re-layouts: 3.69 us -> 0.02 us
  transfers between devices with their start and end apart: 29 -> 31, of which waited for: 16 -> 15; matrix products, arithmetic and copies ran while one was open for 0% -> 0% of each run, Pallas kernels for 3% -> 3%
where the time goes in v5:
time: 127 us; the launch traced here: 126 us
  starting transfers between devices  43.7 us (34%)
  blocking collectives  35.5 us (28%)
  waiting for transfers between devices  33.9 us (27%)
  Pallas kernels  11.9 us (9%)
    all_to_all x2, blocking collectives, body(): planes = lax.all_to_all(payload, 'z', 0, 0)  35.5 us
    ppermute x12, starting transfers between devices, around(): pieces[distance] = lax.ppermute(array, axis, pairs)  12.4 us
    ppermute x12, waiting for transfers between devices, around(): pieces[distance] = lax.ppermute(array, axis, pairs)  11.9 us
    ppermute x3, starting transfers between devices, swap_cores(): return lax.ppermute(array, 'core', [(0, 1), (1, 0)])  11.3 us
    ppermute x4, waiting for transfers between devices, ring(): behind = lax.ppermute(array, axis, backward)  10.8 us
    ppermute x4, starting transfers between devices, ring(): high = lax.ppermute(behind[middle:], axis, backward)  10.1 us
    ppermute x4, starting transfers between devices, ring(): behind = lax.ppermute(array, axis, backward)  6.23 us
    ppermute x4, waiting for transfers between devices, ring(): low = lax.ppermute(ahead[:middle], axis, forward)  6.11 us
  transfers between devices with their start and end apart: 31, of which 15 were waited for; matrix products, arithmetic and copies ran while one was open for 0% of the time, Pallas kernels for 3%

profile of v5, /device:TPU:1, one launch (start us, length us, event | category | flops | bytes accessed | tf_op | source)
XLA Modules:
  0.0 126.4 jit_solution(8707266999888216796)
XLA Ops:
  0.6 3.3 %collective-permute-start = (bf16[6,4,8,2,96,128]{5,4,3,2,1,0:T(8,128)(2,1)}, bf16[6,4,8,2,96,128]{5,4,3,2,1,0:T(8,128)(2,1)}, u32[]{:S(2)}, u32[]{:S(2)}) collective-permute-start(bf16[6,4,8,2,96,128]{5,4,3,2,1,0:T(8,128)(2,1)} %bitcast.68), channel_id=1, source_target_pairs={{0,4},{4,0},{1,5},{5,1},{2,6},{6,2},{3,7},{7,3},{8,12},{12,8},{9,1... | collective-permute-start | bytes 28311560 | tf_op jit(solution)/shard_map/ppermute | solution.py:23
  4.0 1.5 %head.1 = (bf16[8,96,128]{2,1,0:T(8,128)(2,1)}, bf16[96,128]{1,0:T(8,128)(2,1)}) custom-call(bf16[6,64,96,128]{3,2,1,0:T(8,128)(2,1)} %bitcast.69, f32[1,64]{1,0:T(1,128)} %bitcast.65), custom_call_target="tpu_custom_call" | custom-call | tf_op jit(solution)/shard_map/head/pallas_call | solution.py:105
  5.5 17.2 %all_to_all.10 = bf16[8,96,128]{2,1,0:T(8,128)(2,1)S(1)} all-to-all(bf16[8,96,128]{2,1,0:T(8,128)(2,1)} %get-tuple-element.76), channel_id=1, replica_groups=mesh['x'=4,'z'=8,'core'=2,'orb'=4] {'z'}, dimensions={0} | all-to-all | bytes 393216 | tf_op jit(solution)/shard_map/all_to_all | solution.py:406
  22.7 2.8 %collective-permute-start.3 = (bf16[24,16,128]{2,1,0:T(8,128)(2,1)S(1)}, bf16[24,16,128]{2,1,0:T(8,128)(2,1)S(1)}, u32[]{:S(2)}, u32[]{:S(2)}) collective-permute-start(bf16[24,16,128]{2,1,0:T(8,128)(2,1)S(1)} %bitcast.79), channel_id=1, source_target_pairs={{0,3},{1,0},{2,1},{3,2},{4,7},{5,4},{6,5},{7,6},{8,11},{9,8},{10,9... | collective-permute-start | bytes 294920 | tf_op jit(solution)/shard_map/ppermute | solution.py:30
  26.6 2.5 %collective-permute-start.6 = (bf16[24,16,128]{2,1,0:T(8,128)(2,1)S(1)}, bf16[24,16,128]{2,1,0:T(8,128)(2,1)S(1)}, u32[]{:S(2)}, u32[]{:S(2)}) collective-permute-start(bf16[24,16,128]{2,1,0:T(8,128)(2,1)S(1)} %bitcast.75), channel_id=1, source_target_pairs={{0,192},{64,0},{128,64},{192,128},{1,193},{65,1},{129,65},{193,129... | collective-permute-start | bytes 294920 | tf_op jit(solution)/shard_map/ppermute | solution.py:30
  30.6 2.8 %collective-permute-done.1 = bf16[24,16,128]{2,1,0:T(8,128)(2,1)S(1)} collective-permute-done((bf16[24,16,128]{2,1,0:T(8,128)(2,1)S(1)}, bf16[24,16,128]{2,1,0:T(8,128)(2,1)S(1)}, u32[]{:S(2)}, u32[]{:S(2)}) %collective-permute-start.1) | collective-permute-done | bytes 98336 | tf_op jit(solution)/shard_map/ppermute | solution.py:30
  34.1 1.0 collective-permute-done.4
  36.7 3.4 %collective-permute-start.13 = (bf16[96,16,128]{2,1,0:T(8,128)(2,1)S(1)}, bf16[96,16,128]{2,1,0:T(8,128)(2,1)S(1)}, u32[]{:S(2)}, u32[]{:S(2)}) collective-permute-start(bf16[96,16,128]{2,1,0:T(8,128)(2,1)S(1)} %get-tuple-element.107), channel_id=1, source_target_pairs={{0,3},{1,0},{2,1},{3,2},{4,7},{5,4},{6,5},{7,6},{8,11},{9,8},{10,9... | collective-permute-start | bytes 1179656 | tf_op jit(solution)/shard_map/ppermute | solution.py:385
  40.2 2.8 %collective-permute-done.9 = bf16[96,16,128]{2,1,0:T(8,128)(2,1)S(1)} collective-permute-done((bf16[96,16,128]{2,1,0:T(8,128)(2,1)S(1)}, bf16[96,16,128]{2,1,0:T(8,128)(2,1)S(1)}, u32[]{:S(2)}, u32[]{:S(2)}) %collective-permute-start.9) | collective-permute-done | bytes 393248 | tf_op jit(solution)/shard_map/ppermute | solution.py:385
  43.0 2.6 %collective-permute-start.10 = (bf16[48,16,128]{2,1,0:T(8,128)(2,1)S(1)}, bf16[48,16,128]{2,1,0:T(8,128)(2,1)S(1)}, u32[]{:S(2)}, u32[]{:S(2)}) collective-permute-start(bf16[48,16,128]{2,1,0:T(8,128)(2,1)S(1)} %slice.71), channel_id=1, source_target_pairs={{0,192},{64,0},{128,64},{192,128},{1,193},{65,1},{129,65},{193,129... | collective-permute-start | bytes 589832 | tf_op jit(solution)/shard_map/ppermute | solution.py:388
  46.2 4.8 %collective-permute-start.14 = (bf16[48,16,128]{2,1,0:T(8,128)(2,1)S(1)}, bf16[48,16,128]{2,1,0:T(8,128)(2,1)S(1)}, u32[]{:S(2)}, u32[]{:S(2)}) collective-permute-start(bf16[48,16,128]{2,1,0:T(8,128)(2,1)S(1)} %slice.73), channel_id=1, source_target_pairs={{0,3},{1,0},{2,1},{3,2},{4,7},{5,4},{6,5},{7,6},{8,11},{9,8},{10,9... | collective-permute-start | bytes 589832 | tf_op jit(solution)/shard_map/ppermute | solution.py:388
  51.3 2.7 %load.1 = (bf16[4,8,96,128]{3,2,1,0:T(8,128)(2,1)S(1)}, bf16[4,8,96,128]{3,2,1,0:T(8,128)(2,1)S(1)}, bf16[4,8,80,128]{3,2,1,0:T(8,128)(2,1)S(1)}, bf16[4,8,80,12...) custom-call(s32[1]{0:T(128)S(1)} %bitcast.64, ...), custom_call_target="tpu_custom_call" | custom-call | bytes 12000000 | tf_op jit(solution)/shard_map/load/pallas_call | solution.py:183
  54.0 3.0 %collective-permute-done.12 = bf16[48,16,128]{2,1,0:T(8,128)(2,1)S(1)} collective-permute-done((bf16[48,16,128]{2,1,0:T(8,128)(2,1)S(1)}, bf16[48,16,128]{2,1,0:T(8,128)(2,1)S(1)}, u32[]{:S(2)}, u32[]{:S(2)}) %collective-permute-start.12) | collective-permute-done | bytes 196640 | tf_op jit(solution)/shard_map/ppermute | solution.py:387
  56.9 2.7 %collide.2.sums = f32[192,128]{1,0:T(8,128)S(1)} custom-call(s32[5]{0:T(128)S(1)} %stack.23.place, bf16[4,8,96,128]{3,2,1,0:T(8,128)(2,1)S(1)} %get-tuple-element.94.refs_0_, bf16[4,8,96,128]{3,2,1,0:T(8,128)(2,1)S(1)} %get-tuple-element.95.refs_1_, bf16[4,8,80,128]{3,2,1,0:T(8,128)(2,1)S(1)} %get-tuple-element.96.refs_2_, ...), custom_call_target="tpu_custom_call" | custom-call | tf_op jit(solution)/shard_map/collide/pallas_call | solution.py:279
  59.7 4.1 %collective-permute-start.15 = (f32[96,128]{1,0:T(8,128)S(1)}, f32[96,128]{1,0:T(8,128)S(1)}, u32[]{:S(2)}, u32[]{:S(2)}) collective-permute-start(f32[96,128]{1,0:T(8,128)S(1)} %slice.74), channel_id=1, source_target_pairs={{0,4},{4,0},{1,5},{5,1},{2,6},{6,2},{3,7},{7,3},{8,12},{12,8},{9,1... | collective-permute-start | bytes 147464 | tf_op jit(solution)/shard_map/ppermute | solution.py:23
  64.7 0.9 update.1
  65.6 18.3 %all_to_all.11 = bf16[8,208,128]{2,1,0:T(8,128)(2,1)S(1)} all-to-all(bf16[8,208,128]{2,1,0:T(8,128)(2,1)S(1)} %get-tuple-element.120), channel_id=1, replica_groups=mesh['x'=4,'z'=8,'core'=2,'orb'=4] {'z'}, dimensions={0} | all-to-all | bytes 851968 | tf_op jit(solution)/shard_map/all_to_all | solution.py:417
  84.0 3.1 %collective-permute-start.21 = (bf16[28,16,128]{2,1,0:T(8,128)(2,1)S(1)}, bf16[28,16,128]{2,1,0:T(8,128)(2,1)S(1)}, u32[]{:S(2)}, u32[]{:S(2)}) collective-permute-start(bf16[28,16,128]{2,1,0:T(8,128)(2,1)S(1)} %pad_maximum_fusion.4), channel_id=1, source_target_pairs={{0,192},{64,0},{128,64},{192,128},{1,193},{65,1},{129,65},{193,129... | collective-permute-start | bytes 344072 | tf_op jit(solution)/shard_map/ppermute | solution.py:30
  88.1 1.0 collective-permute-start.16
  89.1 4.1 %collective-permute-done.17 = bf16[27,16,128]{2,1,0:T(8,128)(2,1)S(1)} collective-permute-done((bf16[27,16,128]{2,1,0:T(8,128)(2,1)S(1)}, bf16[27,16,128]{2,1,0:T(8,128)(2,1)S(1)}, u32[]{:S(2)}, u32[]{:S(2)}) %collective-permute-start.17) | collective-permute-done | bytes 110624 | tf_op jit(solution)/shard_map/ppermute | solution.py:30
  93.2 2.8 %collective-permute-done.16 = bf16[27,16,128]{2,1,0:T(8,128)(2,1)S(1)} collective-permute-done((bf16[27,16,128]{2,1,0:T(8,128)(2,1)S(1)}, bf16[27,16,128]{2,1,0:T(8,128)(2,1)S(1)}, u32[]{:S(2)}, u32[]{:S(2)}) %collective-permute-start.16) | collective-permute-done | bytes 110624 | tf_op jit(solution)/shard_map/ppermute | solution.py:30
  96.3 1.5 %collective-permute-start.26 = (bf16[112,16,128]{2,1,0:T(8,128)(2,1)S(1)}, bf16[112,16,128]{2,1,0:T(8,128)(2,1)S(1)}, u32[]{:S(2)}, u32[]{:S(2)}) collective-permute-start(bf16[112,16,128]{2,1,0:T(8,128)(2,1)S(1)} %pad_maximum_fusion), channel_id=1, source_target_pairs={{0,1},{1,2},{2,3},{3,0},{4,5},{5,6},{6,7},{7,4},{8,9},{9,10},{10,1... | collective-permute-start | bytes 1376264 | tf_op jit(solution)/shard_map/ppermute | solution.py:384
  97.8 1.9 %collective-permute-start.24 = (bf16[108,16,128]{2,1,0:T(8,128)(2,1)S(1)}, bf16[108,16,128]{2,1,0:T(8,128)(2,1)S(1)}, u32[]{:S(2)}, u32[]{:S(2)}) collective-permute-start(bf16[108,16,128]{2,1,0:T(8,128)(2,1)S(1)} %pad_maximum_fusion.1), channel_id=1, source_target_pairs={{0,192},{64,0},{128,64},{192,128},{1,193},{65,1},{129,65},{193,129... | collective-permute-start | bytes 1327112 | tf_op jit(solution)/shard_map/ppermute | solution.py:385
  99.6 7.6 %collective-permute-done.28 = bf16[112,16,128]{2,1,0:T(8,128)(2,1)S(1)} collective-permute-done((bf16[112,16,128]{2,1,0:T(8,128)(2,1)S(1)}, bf16[112,16,128]{2,1,0:T(8,128)(2,1)S(1)}, u32[]{:S(2)}, u32[]{:S(2)}) %collective-permute-start.28) | collective-permute-done | bytes 458784 | tf_op jit(solution)/shard_map/ppermute | solution.py:385
  107.9 1.0 collective-permute-start.27
  108.9 2.1 %collective-permute-start.25 = (bf16[54,16,128]{2,1,0:T(8,128)(2,1)S(1)}, bf16[54,16,128]{2,1,0:T(8,128)(2,1)S(1)}, u32[]{:S(2)}, u32[]{:S(2)}) collective-permute-start(bf16[54,16,128]{2,1,0:T(8,128)(2,1)S(1)} %slice.80), channel_id=1, source_target_pairs={{0,192},{64,0},{128,64},{192,128},{1,193},{65,1},{129,65},{193,129... | collective-permute-start | bytes 663560 | tf_op jit(solution)/shard_map/ppermute | solution.py:388
  111.1 3.1 %collective-permute-done.25 = bf16[54,16,128]{2,1,0:T(8,128)(2,1)S(1)} collective-permute-done((bf16[54,16,128]{2,1,0:T(8,128)(2,1)S(1)}, bf16[54,16,128]{2,1,0:T(8,128)(2,1)S(1)}, u32[]{:S(2)}, u32[]{:S(2)}) %collective-permute-start.25) | collective-permute-done | bytes 221216 | tf_op jit(solution)/shard_map/ppermute | solution.py:388
  114.3 3.1 %collective-permute-done.23 = bf16[54,16,128]{2,1,0:T(8,128)(2,1)S(1)} collective-permute-done((bf16[54,16,128]{2,1,0:T(8,128)(2,1)S(1)}, bf16[54,16,128]{2,1,0:T(8,128)(2,1)S(1)}, u32[]{:S(2)}, u32[]{:S(2)}) %collective-permute-start.23) | collective-permute-done | bytes 221216 | tf_op jit(solution)/shard_map/ppermute | solution.py:387
  117.4 2.8 %collide.3.sums = f32[320,128]{1,0:T(8,128)S(1)} custom-call(s32[5]{0:T(128)S(1)} %stack.23.place, bf16[4,8,96,128]{3,2,1,0:T(8,128)(2,1)S(1)} %get-tuple-element.94.refs_0_, bf16[4,8,96,128]{3,2,1,0:T(8,128)(2,1)S(1)} %get-tuple-element.95.refs_1_, bf16[4,8,80,128]{3,2,1,0:T(8,128)(2,1)S(1)} %get-tuple-element.96.refs_2_, ...), custom_call_target="tpu_custom_call" | custom-call | tf_op jit(solution)/shard_map/collide/pallas_call | solution.py:279
  120.2 4.0 %collective-permute-start.30 = (f32[224,128]{1,0:T(8,128)S(1)}, f32[224,128]{1,0:T(8,128)S(1)}, u32[]{:S(2)}, u32[]{:S(2)}) collective-permute-start(f32[224,128]{1,0:T(8,128)S(1)} %slice.83), channel_id=1, source_target_pairs={{0,4},{4,0},{1,5},{5,1},{2,6},{6,2},{3,7},{7,3},{8,12},{12,8},{9,1... | collective-permute-start | bytes 344072 | tf_op jit(solution)/shard_map/ppermute | solution.py:23
  124.2 1.0 collective-permute-done.30.theirs
  125.1 1.3 %close.1 = (bf16[96,128]{1,0:T(8,128)(2,1)}, bf16[16,128]{1,0:T(8,128)(2,1)}, bf16[16,128]{1,0:T(8,128)(2,1)}, bf16[16,128]{1,0:T(8,128)(2,1)}) custom-call(f32[320,128]{1,0:T(8,128)S(1)} %collide.3.sums, f32[224,128]{1,0:T(8,128)S(1)} %collective-permute-done.30.theirs, bf16[96,128]{1,0:T(8,128)(2,1)S(1)} %copy-done.1, bf16[64,64]{1,0:T(8,128)(2,1)S(1)} %copy-done, ...), custom_call_target="tpu_custom_call" | custom-call | tf_op jit(solution)/shard_map/close/pallas_call | solution.py:356
  (66 shorter events, 8.9 us)
Async XLA Ops:
  0.6 22.1 %collective-permute-start = (bf16[6,4,8,2,96,128]{5,4,3,2,1,0:T(8,128)(2,1)}, bf16[6,4,8,2,96,128]{5,4,3,2,1,0:T(8,128)(2,1)}, u32[]{:S(2)}, u32[]{:S(2)}) collective-permute-start(bf16[6,4,8,2,96,128]{5,4,3,2,1,0:T(8,128)(2,1)} %bitcast.68), channel_id=1, source_target_pairs={{0,4},{4,0},{1,5},{5,1},{2,6},{6,2},{3,7},{7,3},{8,12},{12,8},{9,1... | collective-permute-start | bytes 28311560 | tf_op jit(solution)/shard_map/ppermute | solution.py:23
  22.7 6.9 %collective-permute-start.3 = (bf16[24,16,128]{2,1,0:T(8,128)(2,1)S(1)}, bf16[24,16,128]{2,1,0:T(8,128)(2,1)S(1)}, u32[]{:S(2)}, u32[]{:S(2)}) collective-permute-start(bf16[24,16,128]{2,1,0:T(8,128)(2,1)S(1)} %bitcast.79), channel_id=1, source_target_pairs={{0,3},{1,0},{2,1},{3,2},{4,7},{5,4},{6,5},{7,6},{8,11},{9,8},{10,9... | collective-permute-start | bytes 294920 | tf_op jit(solution)/shard_map/ppermute | solution.py:30
  25.5 5.1 %collective-permute-start.2 = (bf16[24,16,128]{2,1,0:T(8,128)(2,1)S(1)}, bf16[24,16,128]{2,1,0:T(8,128)(2,1)S(1)}, u32[]{:S(2)}, u32[]{:S(2)}) collective-permute-start(bf16[24,16,128]{2,1,0:T(8,128)(2,1)S(1)} %bitcast.80), channel_id=1, source_target_pairs={{0,2},{1,3},{2,0},{3,1},{4,6},{5,7},{6,4},{7,5},{8,10},{9,11},{10,... | collective-permute-start | bytes 294920 | tf_op jit(solution)/shard_map/ppermute | solution.py:30
  25.9 7.5 %collective-permute-start.1 = (bf16[24,16,128]{2,1,0:T(8,128)(2,1)S(1)}, bf16[24,16,128]{2,1,0:T(8,128)(2,1)S(1)}, u32[]{:S(2)}, u32[]{:S(2)}) collective-permute-start(bf16[24,16,128]{2,1,0:T(8,128)(2,1)S(1)} %bitcast.81), channel_id=1, source_target_pairs={{0,1},{1,2},{2,3},{3,0},{4,5},{5,6},{6,7},{7,4},{8,9},{9,10},{10,1... | collective-permute-start | bytes 294920 | tf_op jit(solution)/shard_map/ppermute | solution.py:30
  26.6 6.8 %collective-permute-start.6 = (bf16[24,16,128]{2,1,0:T(8,128)(2,1)S(1)}, bf16[24,16,128]{2,1,0:T(8,128)(2,1)S(1)}, u32[]{:S(2)}, u32[]{:S(2)}) collective-permute-start(bf16[24,16,128]{2,1,0:T(8,128)(2,1)S(1)} %bitcast.75), channel_id=1, source_target_pairs={{0,192},{64,0},{128,64},{192,128},{1,193},{65,1},{129,65},{193,129... | collective-permute-start | bytes 294920 | tf_op jit(solution)/shard_map/ppermute | solution.py:30
  29.1 5.1 %collective-permute-start.5 = (bf16[24,16,128]{2,1,0:T(8,128)(2,1)S(1)}, bf16[24,16,128]{2,1,0:T(8,128)(2,1)S(1)}, u32[]{:S(2)}, u32[]{:S(2)}) collective-permute-start(bf16[24,16,128]{2,1,0:T(8,128)(2,1)S(1)} %bitcast.76), channel_id=1, source_target_pairs={{0,128},{64,192},{128,0},{192,64},{1,129},{65,193},{129,1},{193,65... | collective-permute-start | bytes 294920 | tf_op jit(solution)/shard_map/ppermute | solution.py:30
  29.6 5.5 %collective-permute-start.4 = (bf16[24,16,128]{2,1,0:T(8,128)(2,1)S(1)}, bf16[24,16,128]{2,1,0:T(8,128)(2,1)S(1)}, u32[]{:S(2)}, u32[]{:S(2)}) collective-permute-start(bf16[24,16,128]{2,1,0:T(8,128)(2,1)S(1)} %bitcast.77), channel_id=1, source_target_pairs={{0,64},{64,128},{128,192},{192,0},{1,65},{65,129},{129,193},{193,1... | collective-permute-start | bytes 294920 | tf_op jit(solution)/shard_map/ppermute | solution.py:30
  35.2 7.8 %collective-permute-start.9 = (bf16[96,16,128]{2,1,0:T(8,128)(2,1)S(1)}, bf16[96,16,128]{2,1,0:T(8,128)(2,1)S(1)}, u32[]{:S(2)}, u32[]{:S(2)}) collective-permute-start(bf16[96,16,128]{2,1,0:T(8,128)(2,1)S(1)} %get-tuple-element.106), channel_id=1, source_target_pairs={{0,192},{64,0},{128,64},{192,128},{1,193},{65,1},{129,65},{193,129... | collective-permute-start | bytes 1179656 | tf_op jit(solution)/shard_map/ppermute | solution.py:385
  36.0 9.5 %collective-permute-start.7 = (bf16[96,16,128]{2,1,0:T(8,128)(2,1)S(1)}, bf16[96,16,128]{2,1,0:T(8,128)(2,1)S(1)}, u32[]{:S(2)}, u32[]{:S(2)}) collective-permute-start(bf16[96,16,128]{2,1,0:T(8,128)(2,1)S(1)} %get-tuple-element.106), channel_id=1, source_target_pairs={{0,64},{64,128},{128,192},{192,0},{1,65},{65,129},{129,193},{193,1... | collective-permute-start | bytes 1179656 | tf_op jit(solution)/shard_map/ppermute | solution.py:384
  36.7 9.4 %collective-permute-start.13 = (bf16[96,16,128]{2,1,0:T(8,128)(2,1)S(1)}, bf16[96,16,128]{2,1,0:T(8,128)(2,1)S(1)}, u32[]{:S(2)}, u32[]{:S(2)}) collective-permute-start(bf16[96,16,128]{2,1,0:T(8,128)(2,1)S(1)} %get-tuple-element.107), channel_id=1, source_target_pairs={{0,3},{1,0},{2,1},{3,2},{4,7},{5,4},{6,5},{7,6},{8,11},{9,8},{10,9... | collective-permute-start | bytes 1179656 | tf_op jit(solution)/shard_map/ppermute | solution.py:385
  40.2 10.8 %collective-permute-start.11 = (bf16[96,16,128]{2,1,0:T(8,128)(2,1)S(1)}, bf16[96,16,128]{2,1,0:T(8,128)(2,1)S(1)}, u32[]{:S(2)}, u32[]{:S(2)}) collective-permute-start(bf16[96,16,128]{2,1,0:T(8,128)(2,1)S(1)} %get-tuple-element.107), channel_id=1, source_target_pairs={{0,1},{1,2},{2,3},{3,0},{4,5},{5,6},{6,7},{7,4},{8,9},{9,10},{10,1... | collective-permute-start | bytes 1179656 | tf_op jit(solution)/shard_map/ppermute | solution.py:384
  43.0 11.0 %collective-permute-start.10 = (bf16[48,16,128]{2,1,0:T(8,128)(2,1)S(1)}, bf16[48,16,128]{2,1,0:T(8,128)(2,1)S(1)}, u32[]{:S(2)}, u32[]{:S(2)}) collective-permute-start(bf16[48,16,128]{2,1,0:T(8,128)(2,1)S(1)} %slice.71), channel_id=1, source_target_pairs={{0,192},{64,0},{128,64},{192,128},{1,193},{65,1},{129,65},{193,129... | collective-permute-start | bytes 589832 | tf_op jit(solution)/shard_map/ppermute | solution.py:388
  45.6 8.4 %collective-permute-start.8 = (bf16[48,16,128]{2,1,0:T(8,128)(2,1)S(1)}, bf16[48,16,128]{2,1,0:T(8,128)(2,1)S(1)}, u32[]{:S(2)}, u32[]{:S(2)}) collective-permute-start(bf16[48,16,128]{2,1,0:T(8,128)(2,1)S(1)} %slice.70), channel_id=1, source_target_pairs={{0,64},{64,128},{128,192},{192,0},{1,65},{65,129},{129,193},{193,1... | collective-permute-start | bytes 589832 | tf_op jit(solution)/shard_map/ppermute | solution.py:387
  46.2 7.8 %collective-permute-start.14 = (bf16[48,16,128]{2,1,0:T(8,128)(2,1)S(1)}, bf16[48,16,128]{2,1,0:T(8,128)(2,1)S(1)}, u32[]{:S(2)}, u32[]{:S(2)}) collective-permute-start(bf16[48,16,128]{2,1,0:T(8,128)(2,1)S(1)} %slice.73), channel_id=1, source_target_pairs={{0,3},{1,0},{2,1},{3,2},{4,7},{5,4},{6,5},{7,6},{8,11},{9,8},{10,9... | collective-permute-start | bytes 589832 | tf_op jit(solution)/shard_map/ppermute | solution.py:388
  51.0 6.0 %collective-permute-start.12 = (bf16[48,16,128]{2,1,0:T(8,128)(2,1)S(1)}, bf16[48,16,128]{2,1,0:T(8,128)(2,1)S(1)}, u32[]{:S(2)}, u32[]{:S(2)}) collective-permute-start(bf16[48,16,128]{2,1,0:T(8,128)(2,1)S(1)} %slice.72), channel_id=1, source_target_pairs={{0,1},{1,2},{2,3},{3,0},{4,5},{5,6},{6,7},{7,4},{8,9},{9,10},{10,1... | collective-permute-start | bytes 589832 | tf_op jit(solution)/shard_map/ppermute | solution.py:387
  59.7 4.9 %collective-permute-start.15 = (f32[96,128]{1,0:T(8,128)S(1)}, f32[96,128]{1,0:T(8,128)S(1)}, u32[]{:S(2)}, u32[]{:S(2)}) collective-permute-start(f32[96,128]{1,0:T(8,128)S(1)} %slice.74), channel_id=1, source_target_pairs={{0,4},{4,0},{1,5},{5,1},{2,6},{6,2},{3,7},{7,3},{8,12},{12,8},{9,1... | collective-permute-start | bytes 147464 | tf_op jit(solution)/shard_map/ppermute | solution.py:23
  65.6 59.6 %copy-start.1 = (bf16[96,128]{1,0:T(8,128)(2,1)S(1)}, bf16[96,128]{1,0:T(8,128)(2,1)}, u32[]{:S(2)}) copy-start(bf16[96,128]{1,0:T(8,128)(2,1)} %get-tuple-element.119.row) | copy-start | bytes 73732
  84.0 4.1 %collective-permute-start.18 = (bf16[27,16,128]{2,1,0:T(8,128)(2,1)S(1)}, bf16[27,16,128]{2,1,0:T(8,128)(2,1)S(1)}, u32[]{:S(2)}, u32[]{:S(2)}) collective-permute-start(bf16[27,16,128]{2,1,0:T(8,128)(2,1)S(1)} %pad_maximum_fusion.5), channel_id=1, source_target_pairs={{0,3},{1,0},{2,1},{3,2},{4,7},{5,4},{6,5},{7,6},{8,11},{9,8},{10,9... | collective-permute-start | bytes 331784 | tf_op jit(solution)/shard_map/ppermute | solution.py:30
  84.0 12.0 %collective-permute-start.21 = (bf16[28,16,128]{2,1,0:T(8,128)(2,1)S(1)}, bf16[28,16,128]{2,1,0:T(8,128)(2,1)S(1)}, u32[]{:S(2)}, u32[]{:S(2)}) collective-permute-start(bf16[28,16,128]{2,1,0:T(8,128)(2,1)S(1)} %pad_maximum_fusion.4), channel_id=1, source_target_pairs={{0,192},{64,0},{128,64},{192,128},{1,193},{65,1},{129,65},{193,129... | collective-permute-start | bytes 344072 | tf_op jit(solution)/shard_map/ppermute | solution.py:30
  87.1 8.9 %collective-permute-start.20 = (bf16[28,16,128]{2,1,0:T(8,128)(2,1)S(1)}, bf16[28,16,128]{2,1,0:T(8,128)(2,1)S(1)}, u32[]{:S(2)}, u32[]{:S(2)}) collective-permute-start(bf16[28,16,128]{2,1,0:T(8,128)(2,1)S(1)} %pad_maximum_fusion.4), channel_id=1, source_target_pairs={{0,128},{64,192},{128,0},{192,64},{1,129},{65,193},{129,1},{193,65... | collective-permute-start | bytes 344072 | tf_op jit(solution)/shard_map/ppermute | solution.py:30
  87.1 8.9 %collective-permute-start.19 = (bf16[28,16,128]{2,1,0:T(8,128)(2,1)S(1)}, bf16[28,16,128]{2,1,0:T(8,128)(2,1)S(1)}, u32[]{:S(2)}, u32[]{:S(2)}) collective-permute-start(bf16[28,16,128]{2,1,0:T(8,128)(2,1)S(1)} %pad_maximum_fusion.4), channel_id=1, source_target_pairs={{0,64},{64,128},{128,192},{192,0},{1,65},{65,129},{129,193},{193,1... | collective-permute-start | bytes 344072 | tf_op jit(solution)/shard_map/ppermute | solution.py:30
  87.8 5.4 %collective-permute-start.17 = (bf16[27,16,128]{2,1,0:T(8,128)(2,1)S(1)}, bf16[27,16,128]{2,1,0:T(8,128)(2,1)S(1)}, u32[]{:S(2)}, u32[]{:S(2)}) collective-permute-start(bf16[27,16,128]{2,1,0:T(8,128)(2,1)S(1)} %pad_maximum_fusion.5), channel_id=1, source_target_pairs={{0,2},{1,3},{2,0},{3,1},{4,6},{5,7},{6,4},{7,5},{8,10},{9,11},{10,... | collective-permute-start | bytes 331784 | tf_op jit(solution)/shard_map/ppermute | solution.py:30
  88.1 8.0 %collective-permute-start.16 = (bf16[27,16,128]{2,1,0:T(8,128)(2,1)S(1)}, bf16[27,16,128]{2,1,0:T(8,128)(2,1)S(1)}, u32[]{:S(2)}, u32[]{:S(2)}) collective-permute-start(bf16[27,16,128]{2,1,0:T(8,128)(2,1)S(1)} %pad_maximum_fusion.5), channel_id=1, source_target_pairs={{0,1},{1,2},{2,3},{3,0},{4,5},{5,6},{6,7},{7,4},{8,9},{9,10},{10,1... | collective-permute-start | bytes 331784 | tf_op jit(solution)/shard_map/ppermute | solution.py:30
  96.2 11.0 %collective-permute-start.28 = (bf16[112,16,128]{2,1,0:T(8,128)(2,1)S(1)}, bf16[112,16,128]{2,1,0:T(8,128)(2,1)S(1)}, u32[]{:S(2)}, u32[]{:S(2)}) collective-permute-start(bf16[112,16,128]{2,1,0:T(8,128)(2,1)S(1)} %pad_maximum_fusion), channel_id=1, source_target_pairs={{0,3},{1,0},{2,1},{3,2},{4,7},{5,4},{6,5},{7,6},{8,11},{9,8},{10,9... | collective-permute-start | bytes 1376264 | tf_op jit(solution)/shard_map/ppermute | solution.py:385
  96.3 11.5 %collective-permute-start.26 = (bf16[112,16,128]{2,1,0:T(8,128)(2,1)S(1)}, bf16[112,16,128]{2,1,0:T(8,128)(2,1)S(1)}, u32[]{:S(2)}, u32[]{:S(2)}) collective-permute-start(bf16[112,16,128]{2,1,0:T(8,128)(2,1)S(1)} %pad_maximum_fusion), channel_id=1, source_target_pairs={{0,1},{1,2},{2,3},{3,0},{4,5},{5,6},{6,7},{7,4},{8,9},{9,10},{10,1... | collective-permute-start | bytes 1376264 | tf_op jit(solution)/shard_map/ppermute | solution.py:384
  97.8 11.1 %collective-permute-start.24 = (bf16[108,16,128]{2,1,0:T(8,128)(2,1)S(1)}, bf16[108,16,128]{2,1,0:T(8,128)(2,1)S(1)}, u32[]{:S(2)}, u32[]{:S(2)}) collective-permute-start(bf16[108,16,128]{2,1,0:T(8,128)(2,1)S(1)} %pad_maximum_fusion.1), channel_id=1, source_target_pairs={{0,192},{64,0},{128,64},{192,128},{1,193},{65,1},{129,65},{193,129... | collective-permute-start | bytes 1327112 | tf_op jit(solution)/shard_map/ppermute | solution.py:385
  99.6 11.4 %collective-permute-start.22 = (bf16[108,16,128]{2,1,0:T(8,128)(2,1)S(1)}, bf16[108,16,128]{2,1,0:T(8,128)(2,1)S(1)}, u32[]{:S(2)}, u32[]{:S(2)}) collective-permute-start(bf16[108,16,128]{2,1,0:T(8,128)(2,1)S(1)} %pad_maximum_fusion.1), channel_id=1, source_target_pairs={{0,64},{64,128},{128,192},{192,0},{1,65},{65,129},{129,193},{193,1... | collective-permute-start | bytes 1327112 | tf_op jit(solution)/shard_map/ppermute | solution.py:384
  107.2 10.2 %collective-permute-start.29 = (bf16[56,16,128]{2,1,0:T(8,128)(2,1)S(1)}, bf16[56,16,128]{2,1,0:T(8,128)(2,1)S(1)}, u32[]{:S(2)}, u32[]{:S(2)}) collective-permute-start(bf16[56,16,128]{2,1,0:T(8,128)(2,1)S(1)} %slice.82), channel_id=1, source_target_pairs={{0,3},{1,0},{2,1},{3,2},{4,7},{5,4},{6,5},{7,6},{8,11},{9,8},{10,9... | collective-permute-start | bytes 688136 | tf_op jit(solution)/shard_map/ppermute | solution.py:388
  107.9 9.5 %collective-permute-start.27 = (bf16[56,16,128]{2,1,0:T(8,128)(2,1)S(1)}, bf16[56,16,128]{2,1,0:T(8,128)(2,1)S(1)}, u32[]{:S(2)}, u32[]{:S(2)}) collective-permute-start(bf16[56,16,128]{2,1,0:T(8,128)(2,1)S(1)} %slice.81), channel_id=1, source_target_pairs={{0,1},{1,2},{2,3},{3,0},{4,5},{5,6},{6,7},{7,4},{8,9},{9,10},{10,1... | collective-permute-start | bytes 688136 | tf_op jit(solution)/shard_map/ppermute | solution.py:387
  108.9 5.4 %collective-permute-start.25 = (bf16[54,16,128]{2,1,0:T(8,128)(2,1)S(1)}, bf16[54,16,128]{2,1,0:T(8,128)(2,1)S(1)}, u32[]{:S(2)}, u32[]{:S(2)}) collective-permute-start(bf16[54,16,128]{2,1,0:T(8,128)(2,1)S(1)} %slice.80), channel_id=1, source_target_pairs={{0,192},{64,0},{128,64},{192,128},{1,193},{65,1},{129,65},{193,129... | collective-permute-start | bytes 663560 | tf_op jit(solution)/shard_map/ppermute | solution.py:388
  111.0 6.4 %collective-permute-start.23 = (bf16[54,16,128]{2,1,0:T(8,128)(2,1)S(1)}, bf16[54,16,128]{2,1,0:T(8,128)(2,1)S(1)}, u32[]{:S(2)}, u32[]{:S(2)}) collective-permute-start(bf16[54,16,128]{2,1,0:T(8,128)(2,1)S(1)} %slice.79), channel_id=1, source_target_pairs={{0,64},{64,128},{128,192},{192,0},{1,65},{65,129},{129,193},{193,1... | collective-permute-start | bytes 663560 | tf_op jit(solution)/shard_map/ppermute | solution.py:387
  120.2 4.9 %collective-permute-start.30 = (f32[224,128]{1,0:T(8,128)S(1)}, f32[224,128]{1,0:T(8,128)S(1)}, u32[]{:S(2)}, u32[]{:S(2)}) collective-permute-start(f32[224,128]{1,0:T(8,128)S(1)} %slice.83), channel_id=1, source_target_pairs={{0,4},{4,0},{1,5},{5,1},{2,6},{6,2},{3,7},{7,3},{8,12},{12,8},{9,1... | collective-permute-start | bytes 344072 | tf_op jit(solution)/shard_map/ppermute | solution.py:23
  (3 other events, 40.3 us)

commit v6 on v5

--- a/solution.py
+++ b/solution.py
@@ -374,9 +374,9 @@
     def along_one(first, second):
         first, second = lax.optimization_barrier((first, second))
         first, second = around(first, "orb"), around(second, "x")
-        first, second = lax.optimization_barrier((first, second))
+        first, second = lax.optimization_barrier(first), lax.optimization_barrier(second)
         first, second = jnp.concatenate(first), jnp.concatenate(second)
-        return lax.optimization_barrier((first, second))
+        return lax.optimization_barrier(first), lax.optimization_barrier(second)
 
     def ring(array, axis):
         forward = [(i, (i + 1) % 4) for i in range(4)]
@@ -406,9 +406,7 @@
     planes = lax.all_to_all(payload, "z", 0, 0)
     planes, other = lax.optimization_barrier((planes, other))
     first, second = along_one(*plane_parts(planes))
-    first, second, own, other, place = lax.optimization_barrier(
-        (first, second, table, other, place)
-    )
+    first, own, other, place = lax.optimization_barrier((first, table, other, place))
     history = load(place[:1], own, other)
     first, second = along_again(first, second)
     sums = collide(place, history, first, second)

time: 127 us -> 123 us (0.969)
  waiting for transfers between devices: 33.9 us -> 29.3 us
    ppermute x3, starting transfers between devices: 11.3 us -> 15.3 us  [swap_cores(): return lax.ppermute(array, 'core', [(0, 1), (1, 0)])]
    ppermute x12, waiting for transfers between devices: 11.9 us -> 8.6 us  [around(): pieces[distance] = lax.ppermute(array, axis, pairs)]
    ppermute x4, starting transfers between devices: 10.1 us -> 6.87 us  [ring(): high = lax.ppermute(behind[middle:], axis, backward)]
    ppermute x4, waiting for transfers between devices: 6.11 us -> 4.07 us  [ring(): low = lax.ppermute(ahead[:middle], axis, forward)]
    ppermute x4, starting transfers between devices: 1.42 us -> 2.84 us  [ring(): low = lax.ppermute(ahead[:middle], axis, forward)]
  transfers between devices with their start and end apart: 31 -> 31, of which waited for: 15 -> 12; matrix products, arithmetic and copies ran while one was open for 0% -> 0% of each run, Pallas kernels for 3% -> 3%
where the time goes in v6:
time: 123 us; the launch traced here: 122 us
  starting transfers between devices  44.8 us (36%)
  blocking collectives  34.9 us (28%)
  waiting for transfers between devices  29.3 us (24%)
  Pallas kernels  11.9 us (10%)
    all_to_all x2, blocking collectives, body(): planes = lax.all_to_all(payload, 'z', 0, 0)  34.9 us
    ppermute x3, starting transfers between devices, swap_cores(): return lax.ppermute(array, 'core', [(0, 1), (1, 0)])  15.3 us
    ppermute x12, starting transfers between devices, around(): pieces[distance] = lax.ppermute(array, axis, pairs)  11.8 us
    ppermute x4, waiting for transfers between devices, ring(): behind = lax.ppermute(array, axis, backward)  10.4 us
    ppermute x12, waiting for transfers between devices, around(): pieces[distance] = lax.ppermute(array, axis, pairs)  8.6 us
    ppermute x4, starting transfers between devices, ring(): behind = lax.ppermute(array, axis, backward)  7.01 us
    ppermute x4, starting transfers between devices, ring(): high = lax.ppermute(behind[middle:], axis, backward)  6.87 us
    pallas_call x2, Pallas kernels, collide(): pl.pallas_call(collide_kernel, in_specs=[pl.BlockSpec(memory_space=pltpu....  5.52 us
  transfers between devices with their start and end apart: 31, of which 12 were waited for; matrix products, arithmetic and copies ran while one was open for 0% of the time, Pallas kernels for 3%

profile of v6, /device:TPU:1, one launch (start us, length us, event | category | flops | bytes accessed | tf_op | source)
XLA Modules:
  0.0 122.3 jit_solution(5174987027012445056)
XLA Ops:
  0.6 3.3 %collective-permute-start = (bf16[6,4,8,2,96,128]{5,4,3,2,1,0:T(8,128)(2,1)}, bf16[6,4,8,2,96,128]{5,4,3,2,1,0:T(8,128)(2,1)}, u32[]{:S(2)}, u32[]{:S(2)}) collective-permute-start(bf16[6,4,8,2,96,128]{5,4,3,2,1,0:T(8,128)(2,1)} %bitcast.68), channel_id=1, source_target_pairs={{0,4},{4,0},{1,5},{5,1},{2,6},{6,2},{3,7},{7,3},{8,12},{12,8},{9,1... | collective-permute-start | bytes 28311560 | tf_op jit(solution)/shard_map/ppermute | solution.py:23
  4.0 1.5 %head.1 = (bf16[8,96,128]{2,1,0:T(8,128)(2,1)}, bf16[96,128]{1,0:T(8,128)(2,1)}) custom-call(bf16[6,64,96,128]{3,2,1,0:T(8,128)(2,1)} %bitcast.69, f32[1,64]{1,0:T(1,128)} %bitcast.65), custom_call_target="tpu_custom_call" | custom-call | tf_op jit(solution)/shard_map/head/pallas_call | solution.py:105
  5.5 17.2 %all_to_all.10 = bf16[8,96,128]{2,1,0:T(8,128)(2,1)S(1)} all-to-all(bf16[8,96,128]{2,1,0:T(8,128)(2,1)} %get-tuple-element.71), channel_id=1, replica_groups=mesh['x'=4,'z'=8,'core'=2,'orb'=4] {'z'}, dimensions={0} | all-to-all | bytes 393216 | tf_op jit(solution)/shard_map/all_to_all | solution.py:406
  22.7 2.6 %collective-permute-start.10 = (bf16[24,16,128]{2,1,0:T(8,128)(2,1)S(1)}, bf16[24,16,128]{2,1,0:T(8,128)(2,1)S(1)}, u32[]{:S(2)}, u32[]{:S(2)}) collective-permute-start(bf16[24,16,128]{2,1,0:T(8,128)(2,1)S(1)} %bitcast.79), channel_id=1, source_target_pairs={{0,192},{64,0},{128,64},{192,128},{1,193},{65,1},{129,65},{193,129... | collective-permute-start | bytes 294920 | tf_op jit(solution)/shard_map/ppermute | solution.py:30
  26.5 2.7 %collective-permute-start.3 = (bf16[24,16,128]{2,1,0:T(8,128)(2,1)S(1)}, bf16[24,16,128]{2,1,0:T(8,128)(2,1)S(1)}, u32[]{:S(2)}, u32[]{:S(2)}) collective-permute-start(bf16[24,16,128]{2,1,0:T(8,128)(2,1)S(1)} %bitcast.75), channel_id=1, source_target_pairs={{0,3},{1,0},{2,1},{3,2},{4,7},{5,4},{6,5},{7,6},{8,11},{9,8},{10,9... | collective-permute-start | bytes 294920 | tf_op jit(solution)/shard_map/ppermute | solution.py:30
  30.3 2.7 %collective-permute-done.8 = bf16[24,16,128]{2,1,0:T(8,128)(2,1)S(1)} collective-permute-done((bf16[24,16,128]{2,1,0:T(8,128)(2,1)S(1)}, bf16[24,16,128]{2,1,0:T(8,128)(2,1)S(1)}, u32[]{:S(2)}, u32[]{:S(2)}) %collective-permute-start.8) | collective-permute-done | bytes 98336 | tf_op jit(solution)/shard_map/ppermute | solution.py:30
  33.1 2.8 %collective-permute-start.13 = (bf16[96,16,128]{2,1,0:T(8,128)(2,1)S(1)}, bf16[96,16,128]{2,1,0:T(8,128)(2,1)S(1)}, u32[]{:S(2)}, u32[]{:S(2)}) collective-permute-start(bf16[96,16,128]{2,1,0:T(8,128)(2,1)S(1)} %pad_maximum_fusion.3), channel_id=1, source_target_pairs={{0,3},{1,0},{2,1},{3,2},{4,7},{5,4},{6,5},{7,6},{8,11},{9,8},{10,9... | collective-permute-start | bytes 1179656 | tf_op jit(solution)/shard_map/ppermute | solution.py:385
  36.0 1.5 %collective-permute-start.6 = (bf16[96,16,128]{2,1,0:T(8,128)(2,1)S(1)}, bf16[96,16,128]{2,1,0:T(8,128)(2,1)S(1)}, u32[]{:S(2)}, u32[]{:S(2)}) collective-permute-start(bf16[96,16,128]{2,1,0:T(8,128)(2,1)S(1)} %pad_maximum_fusion.2), channel_id=1, source_target_pairs={{0,192},{64,0},{128,64},{192,128},{1,193},{65,1},{129,65},{193,129... | collective-permute-start | bytes 1179656 | tf_op jit(solution)/shard_map/ppermute | solution.py:385
  37.5 5.7 %collective-permute-done.13 = bf16[96,16,128]{2,1,0:T(8,128)(2,1)S(1)} collective-permute-done((bf16[96,16,128]{2,1,0:T(8,128)(2,1)S(1)}, bf16[96,16,128]{2,1,0:T(8,128)(2,1)S(1)}, u32[]{:S(2)}, u32[]{:S(2)}) %collective-permute-start.13) | collective-permute-done | bytes 393248 | tf_op jit(solution)/shard_map/ppermute | solution.py:385
  43.2 3.5 %collective-permute-start.14 = (bf16[48,16,128]{2,1,0:T(8,128)(2,1)S(1)}, bf16[48,16,128]{2,1,0:T(8,128)(2,1)S(1)}, u32[]{:S(2)}, u32[]{:S(2)}) collective-permute-start(bf16[48,16,128]{2,1,0:T(8,128)(2,1)S(1)} %slice.73), channel_id=1, source_target_pairs={{0,3},{1,0},{2,1},{3,2},{4,7},{5,4},{6,5},{7,6},{8,11},{9,8},{10,9... | collective-permute-start | bytes 589832 | tf_op jit(solution)/shard_map/ppermute | solution.py:388
  47.0 1.7 %collective-permute-start.5 = (bf16[48,16,128]{2,1,0:T(8,128)(2,1)S(1)}, bf16[48,16,128]{2,1,0:T(8,128)(2,1)S(1)}, u32[]{:S(2)}, u32[]{:S(2)}) collective-permute-start(bf16[48,16,128]{2,1,0:T(8,128)(2,1)S(1)} %slice.70), channel_id=1, source_target_pairs={{0,64},{64,128},{128,192},{192,0},{1,65},{65,129},{129,193},{193,1... | collective-permute-start | bytes 589832 | tf_op jit(solution)/shard_map/ppermute | solution.py:387
  48.7 2.7 %load.1 = (bf16[4,8,96,128]{3,2,1,0:T(8,128)(2,1)S(1)}, bf16[4,8,96,128]{3,2,1,0:T(8,128)(2,1)S(1)}, bf16[4,8,80,128]{3,2,1,0:T(8,128)(2,1)S(1)}, bf16[4,8,80,12...) custom-call(s32[1]{0:T(128)S(1)} %bitcast.64, ...), custom_call_target="tpu_custom_call" | custom-call | bytes 12000000 | tf_op jit(solution)/shard_map/load/pallas_call | solution.py:183
  51.4 1.1 collective-permute-done.12
  53.0 2.7 %collide.2.sums = f32[192,128]{1,0:T(8,128)S(1)} custom-call(s32[5]{0:T(128)S(1)} %stack.23.place, bf16[4,8,96,128]{3,2,1,0:T(8,128)(2,1)S(1)} %get-tuple-element.82.refs_0_, bf16[4,8,96,128]{3,2,1,0:T(8,128)(2,1)S(1)} %get-tuple-element.83.refs_1_, bf16[4,8,80,128]{3,2,1,0:T(8,128)(2,1)S(1)} %get-tuple-element.84.refs_2_, ...), custom_call_target="tpu_custom_call" | custom-call | tf_op jit(solution)/shard_map/collide/pallas_call | solution.py:279
  55.8 4.8 %collective-permute-start.15 = (f32[96,128]{1,0:T(8,128)S(1)}, f32[96,128]{1,0:T(8,128)S(1)}, u32[]{:S(2)}, u32[]{:S(2)}) collective-permute-start(f32[96,128]{1,0:T(8,128)S(1)} %slice.74), channel_id=1, source_target_pairs={{0,4},{4,0},{1,5},{5,1},{2,6},{6,2},{3,7},{7,3},{8,12},{12,8},{9,1... | collective-permute-start | bytes 147464 | tf_op jit(solution)/shard_map/ppermute | solution.py:23
  61.5 0.9 update.1
  62.4 17.7 %all_to_all.11 = bf16[8,208,128]{2,1,0:T(8,128)(2,1)S(1)} all-to-all(bf16[8,208,128]{2,1,0:T(8,128)(2,1)S(1)} %get-tuple-element.112), channel_id=1, replica_groups=mesh['x'=4,'z'=8,'core'=2,'orb'=4] {'z'}, dimensions={0} | all-to-all | bytes 851968 | tf_op jit(solution)/shard_map/all_to_all | solution.py:415
  80.1 1.9 %collective-permute-start.18 = (bf16[27,16,128]{2,1,0:T(8,128)(2,1)S(1)}, bf16[27,16,128]{2,1,0:T(8,128)(2,1)S(1)}, u32[]{:S(2)}, u32[]{:S(2)}) collective-permute-start(bf16[27,16,128]{2,1,0:T(8,128)(2,1)S(1)} %pad_maximum_fusion.5), channel_id=1, source_target_pairs={{0,3},{1,0},{2,1},{3,2},{4,7},{5,4},{6,5},{7,6},{8,11},{9,8},{10,9... | collective-permute-start | bytes 331784 | tf_op jit(solution)/shard_map/ppermute | solution.py:30
  82.1 1.6 %collective-permute-start.24 = (bf16[28,16,128]{2,1,0:T(8,128)(2,1)S(1)}, bf16[28,16,128]{2,1,0:T(8,128)(2,1)S(1)}, u32[]{:S(2)}, u32[]{:S(2)}) collective-permute-start(bf16[28,16,128]{2,1,0:T(8,128)(2,1)S(1)} %pad_maximum_fusion.4), channel_id=1, source_target_pairs={{0,128},{64,192},{128,0},{192,64},{1,129},{65,193},{129,1},{193,65... | collective-permute-start | bytes 344072 | tf_op jit(solution)/shard_map/ppermute | solution.py:30
  84.5 4.6 %collective-permute-done.17 = bf16[27,16,128]{2,1,0:T(8,128)(2,1)S(1)} collective-permute-done((bf16[27,16,128]{2,1,0:T(8,128)(2,1)S(1)}, bf16[27,16,128]{2,1,0:T(8,128)(2,1)S(1)}, u32[]{:S(2)}, u32[]{:S(2)}) %collective-permute-start.17) | collective-permute-done | bytes 110624 | tf_op jit(solution)/shard_map/ppermute | solution.py:30
  89.1 1.2 collective-permute-done.16
  90.9 1.0 collective-permute-start.26
  92.0 2.2 %collective-permute-start.21 = (bf16[108,16,128]{2,1,0:T(8,128)(2,1)S(1)}, bf16[108,16,128]{2,1,0:T(8,128)(2,1)S(1)}, u32[]{:S(2)}, u32[]{:S(2)}) collective-permute-start(bf16[108,16,128]{2,1,0:T(8,128)(2,1)S(1)} %pad_maximum_fusion.1), channel_id=1, source_target_pairs={{0,192},{64,0},{128,64},{192,128},{1,193},{65,1},{129,65},{193,129... | collective-permute-start | bytes 1327112 | tf_op jit(solution)/shard_map/ppermute | solution.py:385
  94.1 4.7 %collective-permute-done.28 = bf16[112,16,128]{2,1,0:T(8,128)(2,1)S(1)} collective-permute-done((bf16[112,16,128]{2,1,0:T(8,128)(2,1)S(1)}, bf16[112,16,128]{2,1,0:T(8,128)(2,1)S(1)}, u32[]{:S(2)}, u32[]{:S(2)}) %collective-permute-start.28) | collective-permute-done | bytes 458784 | tf_op jit(solution)/shard_map/ppermute | solution.py:385
  99.6 1.0 collective-permute-start.27
  100.6 2.6 %collective-permute-start.22 = (bf16[54,16,128]{2,1,0:T(8,128)(2,1)S(1)}, bf16[54,16,128]{2,1,0:T(8,128)(2,1)S(1)}, u32[]{:S(2)}, u32[]{:S(2)}) collective-permute-start(bf16[54,16,128]{2,1,0:T(8,128)(2,1)S(1)} %slice.80), channel_id=1, source_target_pairs={{0,192},{64,0},{128,64},{192,128},{1,193},{65,1},{129,65},{193,129... | collective-permute-start | bytes 663560 | tf_op jit(solution)/shard_map/ppermute | solution.py:388
  103.3 4.3 %collective-permute-done.22 = bf16[54,16,128]{2,1,0:T(8,128)(2,1)S(1)} collective-permute-done((bf16[54,16,128]{2,1,0:T(8,128)(2,1)S(1)}, bf16[54,16,128]{2,1,0:T(8,128)(2,1)S(1)}, u32[]{:S(2)}, u32[]{:S(2)}) %collective-permute-start.22) | collective-permute-done | bytes 221216 | tf_op jit(solution)/shard_map/ppermute | solution.py:388
  107.6 2.5 %collective-permute-done.20 = bf16[54,16,128]{2,1,0:T(8,128)(2,1)S(1)} collective-permute-done((bf16[54,16,128]{2,1,0:T(8,128)(2,1)S(1)}, bf16[54,16,128]{2,1,0:T(8,128)(2,1)S(1)}, u32[]{:S(2)}, u32[]{:S(2)}) %collective-permute-start.20) | collective-permute-done | bytes 221216 | tf_op jit(solution)/shard_map/ppermute | solution.py:387
  110.2 2.8 %collide.3.sums = f32[320,128]{1,0:T(8,128)S(1)} custom-call(s32[5]{0:T(128)S(1)} %stack.23.place, bf16[4,8,96,128]{3,2,1,0:T(8,128)(2,1)S(1)} %get-tuple-element.82.refs_0_, bf16[4,8,96,128]{3,2,1,0:T(8,128)(2,1)S(1)} %get-tuple-element.83.refs_1_, bf16[4,8,80,128]{3,2,1,0:T(8,128)(2,1)S(1)} %get-tuple-element.84.refs_2_, ...), custom_call_target="tpu_custom_call" | custom-call | tf_op jit(solution)/shard_map/collide/pallas_call | solution.py:279
  113.0 7.1 %collective-permute-start.30 = (f32[224,128]{1,0:T(8,128)S(1)}, f32[224,128]{1,0:T(8,128)S(1)}, u32[]{:S(2)}, u32[]{:S(2)}) collective-permute-start(f32[224,128]{1,0:T(8,128)S(1)} %slice.83), channel_id=1, source_target_pairs={{0,4},{4,0},{1,5},{5,1},{2,6},{6,2},{3,7},{7,3},{8,12},{12,8},{9,1... | collective-permute-start | bytes 344072 | tf_op jit(solution)/shard_map/ppermute | solution.py:23
  120.1 1.0 collective-permute-done.30.theirs
  121.1 1.3 %close.1 = (bf16[96,128]{1,0:T(8,128)(2,1)}, bf16[16,128]{1,0:T(8,128)(2,1)}, bf16[16,128]{1,0:T(8,128)(2,1)}, bf16[16,128]{1,0:T(8,128)(2,1)}) custom-call(f32[320,128]{1,0:T(8,128)S(1)} %collide.3.sums, f32[224,128]{1,0:T(8,128)S(1)} %collective-permute-done.30.theirs, bf16[96,128]{1,0:T(8,128)(2,1)S(1)} %copy-done.1, bf16[64,64]{1,0:T(8,128)(2,1)S(1)} %copy-done, ...), custom_call_target="tpu_custom_call" | custom-call | tf_op jit(solution)/shard_map/close/pallas_call | solution.py:356
  (67 shorter events, 6.4 us)
Async XLA Ops:
  0.6 22.1 %collective-permute-start = (bf16[6,4,8,2,96,128]{5,4,3,2,1,0:T(8,128)(2,1)}, bf16[6,4,8,2,96,128]{5,4,3,2,1,0:T(8,128)(2,1)}, u32[]{:S(2)}, u32[]{:S(2)}) collective-permute-start(bf16[6,4,8,2,96,128]{5,4,3,2,1,0:T(8,128)(2,1)} %bitcast.68), channel_id=1, source_target_pairs={{0,4},{4,0},{1,5},{5,1},{2,6},{6,2},{3,7},{7,3},{8,12},{12,8},{9,1... | collective-permute-start | bytes 28311560 | tf_op jit(solution)/shard_map/ppermute | solution.py:23
  22.7 6.9 %collective-permute-start.10 = (bf16[24,16,128]{2,1,0:T(8,128)(2,1)S(1)}, bf16[24,16,128]{2,1,0:T(8,128)(2,1)S(1)}, u32[]{:S(2)}, u32[]{:S(2)}) collective-permute-start(bf16[24,16,128]{2,1,0:T(8,128)(2,1)S(1)} %bitcast.79), channel_id=1, source_target_pairs={{0,192},{64,0},{128,64},{192,128},{1,193},{65,1},{129,65},{193,129... | collective-permute-start | bytes 294920 | tf_op jit(solution)/shard_map/ppermute | solution.py:30
  25.3 5.1 %collective-permute-start.9 = (bf16[24,16,128]{2,1,0:T(8,128)(2,1)S(1)}, bf16[24,16,128]{2,1,0:T(8,128)(2,1)S(1)}, u32[]{:S(2)}, u32[]{:S(2)}) collective-permute-start(bf16[24,16,128]{2,1,0:T(8,128)(2,1)S(1)} %bitcast.80), channel_id=1, source_target_pairs={{0,128},{64,192},{128,0},{192,64},{1,129},{65,193},{129,1},{193,65... | collective-permute-start | bytes 294920 | tf_op jit(solution)/shard_map/ppermute | solution.py:30
  25.8 7.2 %collective-permute-start.8 = (bf16[24,16,128]{2,1,0:T(8,128)(2,1)S(1)}, bf16[24,16,128]{2,1,0:T(8,128)(2,1)S(1)}, u32[]{:S(2)}, u32[]{:S(2)}) collective-permute-start(bf16[24,16,128]{2,1,0:T(8,128)(2,1)S(1)} %bitcast.81), channel_id=1, source_target_pairs={{0,64},{64,128},{128,192},{192,0},{1,65},{65,129},{129,193},{193,1... | collective-permute-start | bytes 294920 | tf_op jit(solution)/shard_map/ppermute | solution.py:30
  26.5 9.4 %collective-permute-start.3 = (bf16[24,16,128]{2,1,0:T(8,128)(2,1)S(1)}, bf16[24,16,128]{2,1,0:T(8,128)(2,1)S(1)}, u32[]{:S(2)}, u32[]{:S(2)}) collective-permute-start(bf16[24,16,128]{2,1,0:T(8,128)(2,1)S(1)} %bitcast.75), channel_id=1, source_target_pairs={{0,3},{1,0},{2,1},{3,2},{4,7},{5,4},{6,5},{7,6},{8,11},{9,8},{10,9... | collective-permute-start | bytes 294920 | tf_op jit(solution)/shard_map/ppermute | solution.py:30
  29.2 6.7 %collective-permute-start.2 = (bf16[24,16,128]{2,1,0:T(8,128)(2,1)S(1)}, bf16[24,16,128]{2,1,0:T(8,128)(2,1)S(1)}, u32[]{:S(2)}, u32[]{:S(2)}) collective-permute-start(bf16[24,16,128]{2,1,0:T(8,128)(2,1)S(1)} %bitcast.76), channel_id=1, source_target_pairs={{0,2},{1,3},{2,0},{3,1},{4,6},{5,7},{6,4},{7,5},{8,10},{9,11},{10,... | collective-permute-start | bytes 294920 | tf_op jit(solution)/shard_map/ppermute | solution.py:30
  29.6 6.3 %collective-permute-start.1 = (bf16[24,16,128]{2,1,0:T(8,128)(2,1)S(1)}, bf16[24,16,128]{2,1,0:T(8,128)(2,1)S(1)}, u32[]{:S(2)}, u32[]{:S(2)}) collective-permute-start(bf16[24,16,128]{2,1,0:T(8,128)(2,1)S(1)} %bitcast.77), channel_id=1, source_target_pairs={{0,1},{1,2},{2,3},{3,0},{4,5},{5,6},{6,7},{7,4},{8,9},{9,10},{10,1... | collective-permute-start | bytes 294920 | tf_op jit(solution)/shard_map/ppermute | solution.py:30
  33.1 10.1 %collective-permute-start.13 = (bf16[96,16,128]{2,1,0:T(8,128)(2,1)S(1)}, bf16[96,16,128]{2,1,0:T(8,128)(2,1)S(1)}, u32[]{:S(2)}, u32[]{:S(2)}) collective-permute-start(bf16[96,16,128]{2,1,0:T(8,128)(2,1)S(1)} %pad_maximum_fusion.3), channel_id=1, source_target_pairs={{0,3},{1,0},{2,1},{3,2},{4,7},{5,4},{6,5},{7,6},{8,11},{9,8},{10,9... | collective-permute-start | bytes 1179656 | tf_op jit(solution)/shard_map/ppermute | solution.py:385
  35.9 10.8 %collective-permute-start.11 = (bf16[96,16,128]{2,1,0:T(8,128)(2,1)S(1)}, bf16[96,16,128]{2,1,0:T(8,128)(2,1)S(1)}, u32[]{:S(2)}, u32[]{:S(2)}) collective-permute-start(bf16[96,16,128]{2,1,0:T(8,128)(2,1)S(1)} %pad_maximum_fusion.3), channel_id=1, source_target_pairs={{0,1},{1,2},{2,3},{3,0},{4,5},{5,6},{6,7},{7,4},{8,9},{9,10},{10,1... | collective-permute-start | bytes 1179656 | tf_op jit(solution)/shard_map/ppermute | solution.py:384
  36.0 10.9 %collective-permute-start.6 = (bf16[96,16,128]{2,1,0:T(8,128)(2,1)S(1)}, bf16[96,16,128]{2,1,0:T(8,128)(2,1)S(1)}, u32[]{:S(2)}, u32[]{:S(2)}) collective-permute-start(bf16[96,16,128]{2,1,0:T(8,128)(2,1)S(1)} %pad_maximum_fusion.2), channel_id=1, source_target_pairs={{0,192},{64,0},{128,64},{192,128},{1,193},{65,1},{129,65},{193,129... | collective-permute-start | bytes 1179656 | tf_op jit(solution)/shard_map/ppermute | solution.py:385
  37.5 9.5 %collective-permute-start.4 = (bf16[96,16,128]{2,1,0:T(8,128)(2,1)S(1)}, bf16[96,16,128]{2,1,0:T(8,128)(2,1)S(1)}, u32[]{:S(2)}, u32[]{:S(2)}) collective-permute-start(bf16[96,16,128]{2,1,0:T(8,128)(2,1)S(1)} %pad_maximum_fusion.2), channel_id=1, source_target_pairs={{0,64},{64,128},{128,192},{192,0},{1,65},{65,129},{129,193},{193,1... | collective-permute-start | bytes 1179656 | tf_op jit(solution)/shard_map/ppermute | solution.py:384
  43.2 8.2 %collective-permute-start.14 = (bf16[48,16,128]{2,1,0:T(8,128)(2,1)S(1)}, bf16[48,16,128]{2,1,0:T(8,128)(2,1)S(1)}, u32[]{:S(2)}, u32[]{:S(2)}) collective-permute-start(bf16[48,16,128]{2,1,0:T(8,128)(2,1)S(1)} %slice.73), channel_id=1, source_target_pairs={{0,3},{1,0},{2,1},{3,2},{4,7},{5,4},{6,5},{7,6},{8,11},{9,8},{10,9... | collective-permute-start | bytes 589832 | tf_op jit(solution)/shard_map/ppermute | solution.py:388
  46.8 5.8 %collective-permute-start.12 = (bf16[48,16,128]{2,1,0:T(8,128)(2,1)S(1)}, bf16[48,16,128]{2,1,0:T(8,128)(2,1)S(1)}, u32[]{:S(2)}, u32[]{:S(2)}) collective-permute-start(bf16[48,16,128]{2,1,0:T(8,128)(2,1)S(1)} %slice.72), channel_id=1, source_target_pairs={{0,1},{1,2},{2,3},{3,0},{4,5},{5,6},{6,7},{7,4},{8,9},{9,10},{10,1... | collective-permute-start | bytes 589832 | tf_op jit(solution)/shard_map/ppermute | solution.py:387
  46.9 5.7 %collective-permute-start.7 = (bf16[48,16,128]{2,1,0:T(8,128)(2,1)S(1)}, bf16[48,16,128]{2,1,0:T(8,128)(2,1)S(1)}, u32[]{:S(2)}, u32[]{:S(2)}) collective-permute-start(bf16[48,16,128]{2,1,0:T(8,128)(2,1)S(1)} %slice.71), channel_id=1, source_target_pairs={{0,192},{64,0},{128,64},{192,128},{1,193},{65,1},{129,65},{193,129... | collective-permute-start | bytes 589832 | tf_op jit(solution)/shard_map/ppermute | solution.py:388
  47.0 6.0 %collective-permute-start.5 = (bf16[48,16,128]{2,1,0:T(8,128)(2,1)S(1)}, bf16[48,16,128]{2,1,0:T(8,128)(2,1)S(1)}, u32[]{:S(2)}, u32[]{:S(2)}) collective-permute-start(bf16[48,16,128]{2,1,0:T(8,128)(2,1)S(1)} %slice.70), channel_id=1, source_target_pairs={{0,64},{64,128},{128,192},{192,0},{1,65},{65,129},{129,193},{193,1... | collective-permute-start | bytes 589832 | tf_op jit(solution)/shard_map/ppermute | solution.py:387
  55.8 5.7 %collective-permute-start.15 = (f32[96,128]{1,0:T(8,128)S(1)}, f32[96,128]{1,0:T(8,128)S(1)}, u32[]{:S(2)}, u32[]{:S(2)}) collective-permute-start(f32[96,128]{1,0:T(8,128)S(1)} %slice.74), channel_id=1, source_target_pairs={{0,4},{4,0},{1,5},{5,1},{2,6},{6,2},{3,7},{7,3},{8,12},{12,8},{9,1... | collective-permute-start | bytes 147464 | tf_op jit(solution)/shard_map/ppermute | solution.py:23
  62.4 58.7 %copy-start.1 = (bf16[96,128]{1,0:T(8,128)(2,1)S(1)}, bf16[96,128]{1,0:T(8,128)(2,1)}, u32[]{:S(2)}) copy-start(bf16[96,128]{1,0:T(8,128)(2,1)} %get-tuple-element.111.row) | copy-start | bytes 73732
  80.1 3.7 %collective-permute-start.18 = (bf16[27,16,128]{2,1,0:T(8,128)(2,1)S(1)}, bf16[27,16,128]{2,1,0:T(8,128)(2,1)S(1)}, u32[]{:S(2)}, u32[]{:S(2)}) collective-permute-start(bf16[27,16,128]{2,1,0:T(8,128)(2,1)S(1)} %pad_maximum_fusion.5), channel_id=1, source_target_pairs={{0,3},{1,0},{2,1},{3,2},{4,7},{5,4},{6,5},{7,6},{8,11},{9,8},{10,9... | collective-permute-start | bytes 331784 | tf_op jit(solution)/shard_map/ppermute | solution.py:30
  82.1 8.2 %collective-permute-start.25 = (bf16[28,16,128]{2,1,0:T(8,128)(2,1)S(1)}, bf16[28,16,128]{2,1,0:T(8,128)(2,1)S(1)}, u32[]{:S(2)}, u32[]{:S(2)}) collective-permute-start(bf16[28,16,128]{2,1,0:T(8,128)(2,1)S(1)} %pad_maximum_fusion.4), channel_id=1, source_target_pairs={{0,192},{64,0},{128,64},{192,128},{1,193},{65,1},{129,65},{193,129... | collective-permute-start | bytes 344072 | tf_op jit(solution)/shard_map/ppermute | solution.py:30
  82.1 8.2 %collective-permute-start.24 = (bf16[28,16,128]{2,1,0:T(8,128)(2,1)S(1)}, bf16[28,16,128]{2,1,0:T(8,128)(2,1)S(1)}, u32[]{:S(2)}, u32[]{:S(2)}) collective-permute-start(bf16[28,16,128]{2,1,0:T(8,128)(2,1)S(1)} %pad_maximum_fusion.4), channel_id=1, source_target_pairs={{0,128},{64,192},{128,0},{192,64},{1,129},{65,193},{129,1},{193,65... | collective-permute-start | bytes 344072 | tf_op jit(solution)/shard_map/ppermute | solution.py:30
  83.7 6.6 %collective-permute-start.23 = (bf16[28,16,128]{2,1,0:T(8,128)(2,1)S(1)}, bf16[28,16,128]{2,1,0:T(8,128)(2,1)S(1)}, u32[]{:S(2)}, u32[]{:S(2)}) collective-permute-start(bf16[28,16,128]{2,1,0:T(8,128)(2,1)S(1)} %pad_maximum_fusion.4), channel_id=1, source_target_pairs={{0,64},{64,128},{128,192},{192,0},{1,65},{65,129},{129,193},{193,1... | collective-permute-start | bytes 344072 | tf_op jit(solution)/shard_map/ppermute | solution.py:30
  83.7 5.4 %collective-permute-start.17 = (bf16[27,16,128]{2,1,0:T(8,128)(2,1)S(1)}, bf16[27,16,128]{2,1,0:T(8,128)(2,1)S(1)}, u32[]{:S(2)}, u32[]{:S(2)}) collective-permute-start(bf16[27,16,128]{2,1,0:T(8,128)(2,1)S(1)} %pad_maximum_fusion.5), channel_id=1, source_target_pairs={{0,2},{1,3},{2,0},{3,1},{4,6},{5,7},{6,4},{7,5},{8,10},{9,11},{10,... | collective-permute-start | bytes 331784 | tf_op jit(solution)/shard_map/ppermute | solution.py:30
  83.9 6.4 %collective-permute-start.16 = (bf16[27,16,128]{2,1,0:T(8,128)(2,1)S(1)}, bf16[27,16,128]{2,1,0:T(8,128)(2,1)S(1)}, u32[]{:S(2)}, u32[]{:S(2)}) collective-permute-start(bf16[27,16,128]{2,1,0:T(8,128)(2,1)S(1)} %pad_maximum_fusion.5), channel_id=1, source_target_pairs={{0,1},{1,2},{2,3},{3,0},{4,5},{5,6},{6,7},{7,4},{8,9},{9,10},{10,1... | collective-permute-start | bytes 331784 | tf_op jit(solution)/shard_map/ppermute | solution.py:30
  90.4 8.5 %collective-permute-start.28 = (bf16[112,16,128]{2,1,0:T(8,128)(2,1)S(1)}, bf16[112,16,128]{2,1,0:T(8,128)(2,1)S(1)}, u32[]{:S(2)}, u32[]{:S(2)}) collective-permute-start(bf16[112,16,128]{2,1,0:T(8,128)(2,1)S(1)} %pad_maximum_fusion), channel_id=1, source_target_pairs={{0,3},{1,0},{2,1},{3,2},{4,7},{5,4},{6,5},{7,6},{8,11},{9,8},{10,9... | collective-permute-start | bytes 1376264 | tf_op jit(solution)/shard_map/ppermute | solution.py:385
  90.9 8.6 %collective-permute-start.26 = (bf16[112,16,128]{2,1,0:T(8,128)(2,1)S(1)}, bf16[112,16,128]{2,1,0:T(8,128)(2,1)S(1)}, u32[]{:S(2)}, u32[]{:S(2)}) collective-permute-start(bf16[112,16,128]{2,1,0:T(8,128)(2,1)S(1)} %pad_maximum_fusion), channel_id=1, source_target_pairs={{0,1},{1,2},{2,3},{3,0},{4,5},{5,6},{6,7},{7,4},{8,9},{9,10},{10,1... | collective-permute-start | bytes 1376264 | tf_op jit(solution)/shard_map/ppermute | solution.py:384
  92.0 8.6 %collective-permute-start.21 = (bf16[108,16,128]{2,1,0:T(8,128)(2,1)S(1)}, bf16[108,16,128]{2,1,0:T(8,128)(2,1)S(1)}, u32[]{:S(2)}, u32[]{:S(2)}) collective-permute-start(bf16[108,16,128]{2,1,0:T(8,128)(2,1)S(1)} %pad_maximum_fusion.1), channel_id=1, source_target_pairs={{0,192},{64,0},{128,64},{192,128},{1,193},{65,1},{129,65},{193,129... | collective-permute-start | bytes 1327112 | tf_op jit(solution)/shard_map/ppermute | solution.py:385
  94.1 9.1 %collective-permute-start.19 = (bf16[108,16,128]{2,1,0:T(8,128)(2,1)S(1)}, bf16[108,16,128]{2,1,0:T(8,128)(2,1)S(1)}, u32[]{:S(2)}, u32[]{:S(2)}) collective-permute-start(bf16[108,16,128]{2,1,0:T(8,128)(2,1)S(1)} %pad_maximum_fusion.1), channel_id=1, source_target_pairs={{0,64},{64,128},{128,192},{192,0},{1,65},{65,129},{129,193},{193,1... | collective-permute-start | bytes 1327112 | tf_op jit(solution)/shard_map/ppermute | solution.py:384
  98.9 11.3 %collective-permute-start.29 = (bf16[56,16,128]{2,1,0:T(8,128)(2,1)S(1)}, bf16[56,16,128]{2,1,0:T(8,128)(2,1)S(1)}, u32[]{:S(2)}, u32[]{:S(2)}) collective-permute-start(bf16[56,16,128]{2,1,0:T(8,128)(2,1)S(1)} %slice.82), channel_id=1, source_target_pairs={{0,3},{1,0},{2,1},{3,2},{4,7},{5,4},{6,5},{7,6},{8,11},{9,8},{10,9... | collective-permute-start | bytes 688136 | tf_op jit(solution)/shard_map/ppermute | solution.py:388
  99.6 10.6 %collective-permute-start.27 = (bf16[56,16,128]{2,1,0:T(8,128)(2,1)S(1)}, bf16[56,16,128]{2,1,0:T(8,128)(2,1)S(1)}, u32[]{:S(2)}, u32[]{:S(2)}) collective-permute-start(bf16[56,16,128]{2,1,0:T(8,128)(2,1)S(1)} %slice.81), channel_id=1, source_target_pairs={{0,1},{1,2},{2,3},{3,0},{4,5},{5,6},{6,7},{7,4},{8,9},{9,10},{10,1... | collective-permute-start | bytes 688136 | tf_op jit(solution)/shard_map/ppermute | solution.py:387
  100.6 7.1 %collective-permute-start.22 = (bf16[54,16,128]{2,1,0:T(8,128)(2,1)S(1)}, bf16[54,16,128]{2,1,0:T(8,128)(2,1)S(1)}, u32[]{:S(2)}, u32[]{:S(2)}) collective-permute-start(bf16[54,16,128]{2,1,0:T(8,128)(2,1)S(1)} %slice.80), channel_id=1, source_target_pairs={{0,192},{64,0},{128,64},{192,128},{1,193},{65,1},{129,65},{193,129... | collective-permute-start | bytes 663560 | tf_op jit(solution)/shard_map/ppermute | solution.py:388
  103.2 6.9 %collective-permute-start.20 = (bf16[54,16,128]{2,1,0:T(8,128)(2,1)S(1)}, bf16[54,16,128]{2,1,0:T(8,128)(2,1)S(1)}, u32[]{:S(2)}, u32[]{:S(2)}) collective-permute-start(bf16[54,16,128]{2,1,0:T(8,128)(2,1)S(1)} %slice.79), channel_id=1, source_target_pairs={{0,64},{64,128},{128,192},{192,0},{1,65},{65,129},{129,193},{193,1... | collective-permute-start | bytes 663560 | tf_op jit(solution)/shard_map/ppermute | solution.py:387
  113.0 8.1 %collective-permute-start.30 = (f32[224,128]{1,0:T(8,128)S(1)}, f32[224,128]{1,0:T(8,128)S(1)}, u32[]{:S(2)}, u32[]{:S(2)}) collective-permute-start(f32[224,128]{1,0:T(8,128)S(1)} %slice.83), channel_id=1, source_target_pairs={{0,4},{4,0},{1,5},{5,1},{2,6},{6,2},{3,7},{7,3},{8,12},{12,8},{9,1... | collective-permute-start | bytes 344072 | tf_op jit(solution)/shard_map/ppermute | solution.py:23
  (3 other events, 38.3 us)

commit v7 on v6

--- a/solution.py
+++ b/solution.py
@@ -404,7 +404,6 @@
     other = swap_cores(table)
     payload, last_row = head(rows_of, coupling)
     planes = lax.all_to_all(payload, "z", 0, 0)
-    planes, other = lax.optimization_barrier((planes, other))
     first, second = along_one(*plane_parts(planes))
     first, own, other, place = lax.optimization_barrier((first, table, other, place))
     history = load(place[:1], own, other)

time: 123 us -> 123 us (level)
  waiting for transfers between devices: 29.3 us -> 20.7 us
  starting transfers between devices: 44.8 us -> 53.1 us
    ppermute x4, waiting for transfers between devices: 10.4 us -> 0.12 us  [ring(): behind = lax.ppermute(array, axis, backward)]
    ppermute x4, waiting for transfers between devices: 0.01 us -> 10.1 us  [ring(): ahead = lax.ppermute(array, axis, forward)]
    ppermute x12, starting transfers between devices: 11.8 us -> 18.1 us  [around(): pieces[distance] = lax.ppermute(array, axis, pairs)]
    ppermute x4, waiting for transfers between devices: 4.32 us -> 0.01 us  [ring(): high = lax.ppermute(behind[middle:], axis, backward)]
    ppermute x12, waiting for transfers between devices: 8.6 us -> 4.77 us  [around(): pieces[distance] = lax.ppermute(array, axis, pairs)]
    ppermute x4, starting transfers between devices: 6.87 us -> 9.99 us  [ring(): high = lax.ppermute(behind[middle:], axis, backward)]
    ppermute x3, starting transfers between devices: 15.3 us -> 12.4 us  [swap_cores(): return lax.ppermute(array, 'core', [(0, 1), (1, 0)])]
    ppermute x4, starting transfers between devices: 7.01 us -> 9.16 us  [ring(): behind = lax.ppermute(array, axis, backward)]
  transfers between devices with their start and end apart: 31 -> 31, of which waited for: 12 -> 10; matrix products, arithmetic and copies ran while one was open for 0% -> 0% of each run, Pallas kernels for 3% -> 3%
where the time goes in v7:
time: 123 us
  starting transfers between devices  53.1 us (43%)
  blocking collectives  35.6 us (29%)
  waiting for transfers between devices  20.7 us (17%)
  Pallas kernels  11.9 us (10%)
    all_to_all x2, blocking collectives, body(): planes = lax.all_to_all(payload, 'z', 0, 0)  35.6 us
    ppermute x12, starting transfers between devices, around(): pieces[distance] = lax.ppermute(array, axis, pairs)  18.1 us
    ppermute x3, starting transfers between devices, swap_cores(): return lax.ppermute(array, 'core', [(0, 1), (1, 0)])  12.4 us
    ppermute x4, waiting for transfers between devices, ring(): ahead = lax.ppermute(array, axis, forward)  10.1 us
    ppermute x4, starting transfers between devices, ring(): high = lax.ppermute(behind[middle:], axis, backward)  9.99 us
    ppermute x4, starting transfers between devices, ring(): behind = lax.ppermute(array, axis, backward)  9.16 us
    pallas_call x2, Pallas kernels, collide(): pl.pallas_call(collide_kernel, in_specs=[pl.BlockSpec(memory_space=pltpu....  5.54 us
    ppermute x12, waiting for transfers between devices, around(): pieces[distance] = lax.ppermute(array, axis, pairs)  4.77 us
  transfers between devices with their start and end apart: 31, of which 10 were waited for; matrix products, arithmetic and copies ran while one was open for 0% of the time, Pallas kernels for 3%

profile of v7, /device:TPU:1, one launch (start us, length us, event | category | flops | bytes accessed | tf_op | source)
XLA Modules:
  0.0 122.8 jit_solution(17586315869722635803)
XLA Ops:
  0.6 3.3 %collective-permute-start.3 = (bf16[6,4,8,2,96,128]{5,4,3,2,1,0:T(8,128)(2,1)}, bf16[6,4,8,2,96,128]{5,4,3,2,1,0:T(8,128)(2,1)}, u32[]{:S(2)}, u32[]{:S(2)}) collective-permute-start(bf16[6,4,8,2,96,128]{5,4,3,2,1,0:T(8,128)(2,1)} %bitcast.68), channel_id=1, source_target_pairs={{0,4},{4,0},{1,5},{5,1},{2,6},{6,2},{3,7},{7,3},{8,12},{12,8},{9,1... | collective-permute-start | bytes 28311560 | tf_op jit(solution)/shard_map/ppermute | solution.py:23
  4.0 1.5 %head.1 = (bf16[8,96,128]{2,1,0:T(8,128)(2,1)}, bf16[96,128]{1,0:T(8,128)(2,1)}) custom-call(bf16[6,64,96,128]{3,2,1,0:T(8,128)(2,1)} %bitcast.69, f32[1,64]{1,0:T(1,128)} %bitcast.65), custom_call_target="tpu_custom_call" | custom-call | tf_op jit(solution)/shard_map/head/pallas_call | solution.py:105
  5.5 17.2 %all_to_all.10 = bf16[8,96,128]{2,1,0:T(8,128)(2,1)S(1)} all-to-all(bf16[8,96,128]{2,1,0:T(8,128)(2,1)} %get-tuple-element.69), channel_id=1, replica_groups=mesh['x'=4,'z'=8,'core'=2,'orb'=4] {'z'}, dimensions={0} | all-to-all | bytes 393216 | tf_op jit(solution)/shard_map/all_to_all | solution.py:406
  22.7 1.3 %collective-permute-start.8 = (bf16[24,16,128]{2,1,0:T(8,128)(2,1)S(1)}, bf16[24,16,128]{2,1,0:T(8,128)(2,1)S(1)}, u32[]{:S(2)}, u32[]{:S(2)}) collective-permute-start(bf16[24,16,128]{2,1,0:T(8,128)(2,1)S(1)} %bitcast.79), channel_id=1, source_target_pairs={{0,64},{64,128},{128,192},{192,0},{1,65},{65,129},{129,193},{193,1... | collective-permute-start | bytes 294920 | tf_op jit(solution)/shard_map/ppermute | solution.py:30
  24.0 2.5 %collective-permute-start.9 = (bf16[24,16,128]{2,1,0:T(8,128)(2,1)S(1)}, bf16[24,16,128]{2,1,0:T(8,128)(2,1)S(1)}, u32[]{:S(2)}, u32[]{:S(2)}) collective-permute-start(bf16[24,16,128]{2,1,0:T(8,128)(2,1)S(1)} %bitcast.80), channel_id=1, source_target_pairs={{0,128},{64,192},{128,0},{192,64},{1,129},{65,193},{129,1},{193,65... | collective-permute-start | bytes 294920 | tf_op jit(solution)/shard_map/ppermute | solution.py:30
  27.7 1.3 %collective-permute-start = (bf16[24,16,128]{2,1,0:T(8,128)(2,1)S(1)}, bf16[24,16,128]{2,1,0:T(8,128)(2,1)S(1)}, u32[]{:S(2)}, u32[]{:S(2)}) collective-permute-start(bf16[24,16,128]{2,1,0:T(8,128)(2,1)S(1)} %bitcast.75), channel_id=1, source_target_pairs={{0,1},{1,2},{2,3},{3,0},{4,5},{5,6},{6,7},{7,4},{8,9},{9,10},{10,1... | collective-permute-start | bytes 294920 | tf_op jit(solution)/shard_map/ppermute | solution.py:30
  29.0 2.6 %collective-permute-start.1 = (bf16[24,16,128]{2,1,0:T(8,128)(2,1)S(1)}, bf16[24,16,128]{2,1,0:T(8,128)(2,1)S(1)}, u32[]{:S(2)}, u32[]{:S(2)}) collective-permute-start(bf16[24,16,128]{2,1,0:T(8,128)(2,1)S(1)} %bitcast.76), channel_id=1, source_target_pairs={{0,2},{1,3},{2,0},{3,1},{4,6},{5,7},{6,4},{7,5},{8,10},{9,11},{10,... | collective-permute-start | bytes 294920 | tf_op jit(solution)/shard_map/ppermute | solution.py:30
  31.6 1.6 %collective-permute-start.2 = (bf16[24,16,128]{2,1,0:T(8,128)(2,1)S(1)}, bf16[24,16,128]{2,1,0:T(8,128)(2,1)S(1)}, u32[]{:S(2)}, u32[]{:S(2)}) collective-permute-start(bf16[24,16,128]{2,1,0:T(8,128)(2,1)S(1)} %bitcast.77), channel_id=1, source_target_pairs={{0,3},{1,0},{2,1},{3,2},{4,7},{5,4},{6,5},{7,6},{8,11},{9,8},{10,9... | collective-permute-start | bytes 294920 | tf_op jit(solution)/shard_map/ppermute | solution.py:30
  33.4 2.7 %collective-permute-start.13 = (bf16[96,16,128]{2,1,0:T(8,128)(2,1)S(1)}, bf16[96,16,128]{2,1,0:T(8,128)(2,1)S(1)}, u32[]{:S(2)}, u32[]{:S(2)}) collective-permute-start(bf16[96,16,128]{2,1,0:T(8,128)(2,1)S(1)} %pad_maximum_fusion.3), channel_id=1, source_target_pairs={{0,3},{1,0},{2,1},{3,2},{4,7},{5,4},{6,5},{7,6},{8,11},{9,8},{10,9... | collective-permute-start | bytes 1179656 | tf_op jit(solution)/shard_map/ppermute | solution.py:385
  36.8 2.3 %collective-permute-start.6 = (bf16[96,16,128]{2,1,0:T(8,128)(2,1)S(1)}, bf16[96,16,128]{2,1,0:T(8,128)(2,1)S(1)}, u32[]{:S(2)}, u32[]{:S(2)}) collective-permute-start(bf16[96,16,128]{2,1,0:T(8,128)(2,1)S(1)} %pad_maximum_fusion.2), channel_id=1, source_target_pairs={{0,192},{64,0},{128,64},{192,128},{1,193},{65,1},{129,65},{193,129... | collective-permute-start | bytes 1179656 | tf_op jit(solution)/shard_map/ppermute | solution.py:385
  39.1 4.6 %collective-permute-done.11 = bf16[96,16,128]{2,1,0:T(8,128)(2,1)S(1)} collective-permute-done((bf16[96,16,128]{2,1,0:T(8,128)(2,1)S(1)}, bf16[96,16,128]{2,1,0:T(8,128)(2,1)S(1)}, u32[]{:S(2)}, u32[]{:S(2)}) %collective-permute-start.11) | collective-permute-done | bytes 393248 | tf_op jit(solution)/shard_map/ppermute | solution.py:384
  44.1 2.5 %collective-permute-start.14 = (bf16[48,16,128]{2,1,0:T(8,128)(2,1)S(1)}, bf16[48,16,128]{2,1,0:T(8,128)(2,1)S(1)}, u32[]{:S(2)}, u32[]{:S(2)}) collective-permute-start(bf16[48,16,128]{2,1,0:T(8,128)(2,1)S(1)} %slice.73), channel_id=1, source_target_pairs={{0,3},{1,0},{2,1},{3,2},{4,7},{5,4},{6,5},{7,6},{8,11},{9,8},{10,9... | collective-permute-start | bytes 589832 | tf_op jit(solution)/shard_map/ppermute | solution.py:388
  46.8 2.9 %collective-permute-start.7 = (bf16[48,16,128]{2,1,0:T(8,128)(2,1)S(1)}, bf16[48,16,128]{2,1,0:T(8,128)(2,1)S(1)}, u32[]{:S(2)}, u32[]{:S(2)}) collective-permute-start(bf16[48,16,128]{2,1,0:T(8,128)(2,1)S(1)} %slice.71), channel_id=1, source_target_pairs={{0,192},{64,0},{128,64},{192,128},{1,193},{65,1},{129,65},{193,129... | collective-permute-start | bytes 589832 | tf_op jit(solution)/shard_map/ppermute | solution.py:388
  49.7 2.7 %load.1 = (bf16[4,8,96,128]{3,2,1,0:T(8,128)(2,1)S(1)}, bf16[4,8,96,128]{3,2,1,0:T(8,128)(2,1)S(1)}, bf16[4,8,80,128]{3,2,1,0:T(8,128)(2,1)S(1)}, bf16[4,8,80,12...) custom-call(s32[1]{0:T(128)S(1)} %bitcast.64, ...), custom_call_target="tpu_custom_call" | custom-call | bytes 12000000 | tf_op jit(solution)/shard_map/load/pallas_call | solution.py:183
  52.7 2.8 %collide.2.sums = f32[192,128]{1,0:T(8,128)S(1)} custom-call(s32[5]{0:T(128)S(1)} %stack.23.place, bf16[4,8,96,128]{3,2,1,0:T(8,128)(2,1)S(1)} %get-tuple-element.78.refs_0_, bf16[4,8,96,128]{3,2,1,0:T(8,128)(2,1)S(1)} %get-tuple-element.79.refs_1_, bf16[4,8,80,128]{3,2,1,0:T(8,128)(2,1)S(1)} %get-tuple-element.80.refs_2_, ...), custom_call_target="tpu_custom_call" | custom-call | tf_op jit(solution)/shard_map/collide/pallas_call | solution.py:279
  55.5 4.2 %collective-permute-start.15 = (f32[96,128]{1,0:T(8,128)S(1)}, f32[96,128]{1,0:T(8,128)S(1)}, u32[]{:S(2)}, u32[]{:S(2)}) collective-permute-start(f32[96,128]{1,0:T(8,128)S(1)} %slice.74), channel_id=1, source_target_pairs={{0,4},{4,0},{1,5},{5,1},{2,6},{6,2},{3,7},{7,3},{8,12},{12,8},{9,1... | collective-permute-start | bytes 147464 | tf_op jit(solution)/shard_map/ppermute | solution.py:23
  61.5 18.4 %all_to_all.11 = bf16[8,208,128]{2,1,0:T(8,128)(2,1)S(1)} all-to-all(bf16[8,208,128]{2,1,0:T(8,128)(2,1)S(1)} %get-tuple-element.108), channel_id=1, replica_groups=mesh['x'=4,'z'=8,'core'=2,'orb'=4] {'z'}, dimensions={0} | all-to-all | bytes 851968 | tf_op jit(solution)/shard_map/all_to_all | solution.py:414
  80.2 4.4 %collective-permute-start.24 = (bf16[28,16,128]{2,1,0:T(8,128)(2,1)S(1)}, bf16[28,16,128]{2,1,0:T(8,128)(2,1)S(1)}, u32[]{:S(2)}, u32[]{:S(2)}) collective-permute-start(bf16[28,16,128]{2,1,0:T(8,128)(2,1)S(1)} %pad_maximum_fusion.4), channel_id=1, source_target_pairs={{0,128},{64,192},{128,0},{192,64},{1,129},{65,193},{129,1},{193,65... | collective-permute-start | bytes 344072 | tf_op jit(solution)/shard_map/ppermute | solution.py:30
  84.5 3.1 %collective-permute-start.17 = (bf16[27,16,128]{2,1,0:T(8,128)(2,1)S(1)}, bf16[27,16,128]{2,1,0:T(8,128)(2,1)S(1)}, u32[]{:S(2)}, u32[]{:S(2)}) collective-permute-start(bf16[27,16,128]{2,1,0:T(8,128)(2,1)S(1)} %pad_maximum_fusion.5), channel_id=1, source_target_pairs={{0,2},{1,3},{2,0},{3,1},{4,6},{5,7},{6,4},{7,5},{8,10},{9,11},{10,... | collective-permute-start | bytes 331784 | tf_op jit(solution)/shard_map/ppermute | solution.py:30
  87.6 2.4 %collective-permute-done.17 = bf16[27,16,128]{2,1,0:T(8,128)(2,1)S(1)} collective-permute-done((bf16[27,16,128]{2,1,0:T(8,128)(2,1)S(1)}, bf16[27,16,128]{2,1,0:T(8,128)(2,1)S(1)}, u32[]{:S(2)}, u32[]{:S(2)}) %collective-permute-start.17) | collective-permute-done | bytes 110624 | tf_op jit(solution)/shard_map/ppermute | solution.py:30
  90.1 2.1 %collective-permute-done.18 = bf16[27,16,128]{2,1,0:T(8,128)(2,1)S(1)} collective-permute-done((bf16[27,16,128]{2,1,0:T(8,128)(2,1)S(1)}, bf16[27,16,128]{2,1,0:T(8,128)(2,1)S(1)}, u32[]{:S(2)}, u32[]{:S(2)}) %collective-permute-start.18) | collective-permute-done | bytes 110624 | tf_op jit(solution)/shard_map/ppermute | solution.py:30
  92.3 2.7 %collective-permute-start.28 = (bf16[112,16,128]{2,1,0:T(8,128)(2,1)S(1)}, bf16[112,16,128]{2,1,0:T(8,128)(2,1)S(1)}, u32[]{:S(2)}, u32[]{:S(2)}) collective-permute-start(bf16[112,16,128]{2,1,0:T(8,128)(2,1)S(1)} %pad_maximum_fusion), channel_id=1, source_target_pairs={{0,3},{1,0},{2,1},{3,2},{4,7},{5,4},{6,5},{7,6},{8,11},{9,8},{10,9... | collective-permute-start | bytes 1376264 | tf_op jit(solution)/shard_map/ppermute | solution.py:385
  95.0 1.2 %collective-permute-start.19 = (bf16[108,16,128]{2,1,0:T(8,128)(2,1)S(1)}, bf16[108,16,128]{2,1,0:T(8,128)(2,1)S(1)}, u32[]{:S(2)}, u32[]{:S(2)}) collective-permute-start(bf16[108,16,128]{2,1,0:T(8,128)(2,1)S(1)} %pad_maximum_fusion.1), channel_id=1, source_target_pairs={{0,64},{64,128},{128,192},{192,0},{1,65},{65,129},{129,193},{193,1... | collective-permute-start | bytes 1327112 | tf_op jit(solution)/shard_map/ppermute | solution.py:384
  96.3 1.5 %collective-permute-start.21 = (bf16[108,16,128]{2,1,0:T(8,128)(2,1)S(1)}, bf16[108,16,128]{2,1,0:T(8,128)(2,1)S(1)}, u32[]{:S(2)}, u32[]{:S(2)}) collective-permute-start(bf16[108,16,128]{2,1,0:T(8,128)(2,1)S(1)} %pad_maximum_fusion.1), channel_id=1, source_target_pairs={{0,192},{64,0},{128,64},{192,128},{1,193},{65,1},{129,65},{193,129... | collective-permute-start | bytes 1327112 | tf_op jit(solution)/shard_map/ppermute | solution.py:385
  97.8 5.6 %collective-permute-done.26 = bf16[112,16,128]{2,1,0:T(8,128)(2,1)S(1)} collective-permute-done((bf16[112,16,128]{2,1,0:T(8,128)(2,1)S(1)}, bf16[112,16,128]{2,1,0:T(8,128)(2,1)S(1)}, u32[]{:S(2)}, u32[]{:S(2)}) %collective-permute-start.26) | collective-permute-done | bytes 458784 | tf_op jit(solution)/shard_map/ppermute | solution.py:384
  103.5 2.7 %collective-permute-start.29 = (bf16[56,16,128]{2,1,0:T(8,128)(2,1)S(1)}, bf16[56,16,128]{2,1,0:T(8,128)(2,1)S(1)}, u32[]{:S(2)}, u32[]{:S(2)}) collective-permute-start(bf16[56,16,128]{2,1,0:T(8,128)(2,1)S(1)} %slice.82), channel_id=1, source_target_pairs={{0,3},{1,0},{2,1},{3,2},{4,7},{5,4},{6,5},{7,6},{8,11},{9,8},{10,9... | collective-permute-start | bytes 688136 | tf_op jit(solution)/shard_map/ppermute | solution.py:388
  106.2 1.2 collective-permute-start.20
  107.4 1.9 %collective-permute-start.22 = (bf16[54,16,128]{2,1,0:T(8,128)(2,1)S(1)}, bf16[54,16,128]{2,1,0:T(8,128)(2,1)S(1)}, u32[]{:S(2)}, u32[]{:S(2)}) collective-permute-start(bf16[54,16,128]{2,1,0:T(8,128)(2,1)S(1)} %slice.80), channel_id=1, source_target_pairs={{0,192},{64,0},{128,64},{192,128},{1,193},{65,1},{129,65},{193,129... | collective-permute-start | bytes 663560 | tf_op jit(solution)/shard_map/ppermute | solution.py:388
  109.3 3.5 %collective-permute-done.20 = bf16[54,16,128]{2,1,0:T(8,128)(2,1)S(1)} collective-permute-done((bf16[54,16,128]{2,1,0:T(8,128)(2,1)S(1)}, bf16[54,16,128]{2,1,0:T(8,128)(2,1)S(1)}, u32[]{:S(2)}, u32[]{:S(2)}) %collective-permute-start.20) | collective-permute-done | bytes 221216 | tf_op jit(solution)/shard_map/ppermute | solution.py:387
  112.8 2.8 %collide.3.sums = f32[320,128]{1,0:T(8,128)S(1)} custom-call(s32[5]{0:T(128)S(1)} %stack.23.place, bf16[4,8,96,128]{3,2,1,0:T(8,128)(2,1)S(1)} %get-tuple-element.78.refs_0_, bf16[4,8,96,128]{3,2,1,0:T(8,128)(2,1)S(1)} %get-tuple-element.79.refs_1_, bf16[4,8,80,128]{3,2,1,0:T(8,128)(2,1)S(1)} %get-tuple-element.80.refs_2_, ...), custom_call_target="tpu_custom_call" | custom-call | tf_op jit(solution)/shard_map/collide/pallas_call | solution.py:279
  115.6 4.9 %collective-permute-start.30 = (f32[224,128]{1,0:T(8,128)S(1)}, f32[224,128]{1,0:T(8,128)S(1)}, u32[]{:S(2)}, u32[]{:S(2)}) collective-permute-start(f32[224,128]{1,0:T(8,128)S(1)} %slice.83), channel_id=1, source_target_pairs={{0,4},{4,0},{1,5},{5,1},{2,6},{6,2},{3,7},{7,3},{8,12},{12,8},{9,1... | collective-permute-start | bytes 344072 | tf_op jit(solution)/shard_map/ppermute | solution.py:23
  121.5 1.3 %close.1 = (bf16[96,128]{1,0:T(8,128)(2,1)}, bf16[16,128]{1,0:T(8,128)(2,1)}, bf16[16,128]{1,0:T(8,128)(2,1)}, bf16[16,128]{1,0:T(8,128)(2,1)}) custom-call(f32[320,128]{1,0:T(8,128)S(1)} %collide.3.sums, f32[224,128]{1,0:T(8,128)S(1)} %collective-permute-done.30.theirs, bf16[96,128]{1,0:T(8,128)(2,1)S(1)} %copy-done.1, bf16[64,64]{1,0:T(8,128)(2,1)S(1)} %copy-done, ...), custom_call_target="tpu_custom_call" | custom-call | tf_op jit(solution)/shard_map/close/pallas_call | solution.py:356
  (67 shorter events, 6.4 us)
Async XLA Ops:
  0.6 35.7 %collective-permute-start.3 = (bf16[6,4,8,2,96,128]{5,4,3,2,1,0:T(8,128)(2,1)}, bf16[6,4,8,2,96,128]{5,4,3,2,1,0:T(8,128)(2,1)}, u32[]{:S(2)}, u32[]{:S(2)}) collective-permute-start(bf16[6,4,8,2,96,128]{5,4,3,2,1,0:T(8,128)(2,1)} %bitcast.68), channel_id=1, source_target_pairs={{0,4},{4,0},{1,5},{5,1},{2,6},{6,2},{3,7},{7,3},{8,12},{12,8},{9,1... | collective-permute-start | bytes 28311560 | tf_op jit(solution)/shard_map/ppermute | solution.py:23
  22.7 6.3 %collective-permute-start.8 = (bf16[24,16,128]{2,1,0:T(8,128)(2,1)S(1)}, bf16[24,16,128]{2,1,0:T(8,128)(2,1)S(1)}, u32[]{:S(2)}, u32[]{:S(2)}) collective-permute-start(bf16[24,16,128]{2,1,0:T(8,128)(2,1)S(1)} %bitcast.79), channel_id=1, source_target_pairs={{0,64},{64,128},{128,192},{192,0},{1,65},{65,129},{129,193},{193,1... | collective-permute-start | bytes 294920 | tf_op jit(solution)/shard_map/ppermute | solution.py:30
  24.0 7.6 %collective-permute-start.9 = (bf16[24,16,128]{2,1,0:T(8,128)(2,1)S(1)}, bf16[24,16,128]{2,1,0:T(8,128)(2,1)S(1)}, u32[]{:S(2)}, u32[]{:S(2)}) collective-permute-start(bf16[24,16,128]{2,1,0:T(8,128)(2,1)S(1)} %bitcast.80), channel_id=1, source_target_pairs={{0,128},{64,192},{128,0},{192,64},{1,129},{65,193},{129,1},{193,65... | collective-permute-start | bytes 294920 | tf_op jit(solution)/shard_map/ppermute | solution.py:30
  26.5 6.8 %collective-permute-start.10 = (bf16[24,16,128]{2,1,0:T(8,128)(2,1)S(1)}, bf16[24,16,128]{2,1,0:T(8,128)(2,1)S(1)}, u32[]{:S(2)}, u32[]{:S(2)}) collective-permute-start(bf16[24,16,128]{2,1,0:T(8,128)(2,1)S(1)} %bitcast.81), channel_id=1, source_target_pairs={{0,192},{64,0},{128,64},{192,128},{1,193},{65,1},{129,65},{193,129... | collective-permute-start | bytes 294920 | tf_op jit(solution)/shard_map/ppermute | solution.py:30
  27.7 5.7 %collective-permute-start = (bf16[24,16,128]{2,1,0:T(8,128)(2,1)S(1)}, bf16[24,16,128]{2,1,0:T(8,128)(2,1)S(1)}, u32[]{:S(2)}, u32[]{:S(2)}) collective-permute-start(bf16[24,16,128]{2,1,0:T(8,128)(2,1)S(1)} %bitcast.75), channel_id=1, source_target_pairs={{0,1},{1,2},{2,3},{3,0},{4,5},{5,6},{6,7},{7,4},{8,9},{9,10},{10,1... | collective-permute-start | bytes 294920 | tf_op jit(solution)/shard_map/ppermute | solution.py:30
  29.0 7.1 %collective-permute-start.1 = (bf16[24,16,128]{2,1,0:T(8,128)(2,1)S(1)}, bf16[24,16,128]{2,1,0:T(8,128)(2,1)S(1)}, u32[]{:S(2)}, u32[]{:S(2)}) collective-permute-start(bf16[24,16,128]{2,1,0:T(8,128)(2,1)S(1)} %bitcast.76), channel_id=1, source_target_pairs={{0,2},{1,3},{2,0},{3,1},{4,6},{5,7},{6,4},{7,5},{8,10},{9,11},{10,... | collective-permute-start | bytes 294920 | tf_op jit(solution)/shard_map/ppermute | solution.py:30
  31.6 4.7 %collective-permute-start.2 = (bf16[24,16,128]{2,1,0:T(8,128)(2,1)S(1)}, bf16[24,16,128]{2,1,0:T(8,128)(2,1)S(1)}, u32[]{:S(2)}, u32[]{:S(2)}) collective-permute-start(bf16[24,16,128]{2,1,0:T(8,128)(2,1)S(1)} %bitcast.77), channel_id=1, source_target_pairs={{0,3},{1,0},{2,1},{3,2},{4,7},{5,4},{6,5},{7,6},{8,11},{9,8},{10,9... | collective-permute-start | bytes 294920 | tf_op jit(solution)/shard_map/ppermute | solution.py:30
  33.3 10.4 %collective-permute-start.11 = (bf16[96,16,128]{2,1,0:T(8,128)(2,1)S(1)}, bf16[96,16,128]{2,1,0:T(8,128)(2,1)S(1)}, u32[]{:S(2)}, u32[]{:S(2)}) collective-permute-start(bf16[96,16,128]{2,1,0:T(8,128)(2,1)S(1)} %pad_maximum_fusion.3), channel_id=1, source_target_pairs={{0,1},{1,2},{2,3},{3,0},{4,5},{5,6},{6,7},{7,4},{8,9},{9,10},{10,1... | collective-permute-start | bytes 1179656 | tf_op jit(solution)/shard_map/ppermute | solution.py:384
  33.4 10.7 %collective-permute-start.13 = (bf16[96,16,128]{2,1,0:T(8,128)(2,1)S(1)}, bf16[96,16,128]{2,1,0:T(8,128)(2,1)S(1)}, u32[]{:S(2)}, u32[]{:S(2)}) collective-permute-start(bf16[96,16,128]{2,1,0:T(8,128)(2,1)S(1)} %pad_maximum_fusion.3), channel_id=1, source_target_pairs={{0,3},{1,0},{2,1},{3,2},{4,7},{5,4},{6,5},{7,6},{8,11},{9,8},{10,9... | collective-permute-start | bytes 1179656 | tf_op jit(solution)/shard_map/ppermute | solution.py:385
  36.4 10.2 %collective-permute-start.4 = (bf16[96,16,128]{2,1,0:T(8,128)(2,1)S(1)}, bf16[96,16,128]{2,1,0:T(8,128)(2,1)S(1)}, u32[]{:S(2)}, u32[]{:S(2)}) collective-permute-start(bf16[96,16,128]{2,1,0:T(8,128)(2,1)S(1)} %pad_maximum_fusion.2), channel_id=1, source_target_pairs={{0,64},{64,128},{128,192},{192,0},{1,65},{65,129},{129,193},{193,1... | collective-permute-start | bytes 1179656 | tf_op jit(solution)/shard_map/ppermute | solution.py:384
  36.8 9.9 %collective-permute-start.6 = (bf16[96,16,128]{2,1,0:T(8,128)(2,1)S(1)}, bf16[96,16,128]{2,1,0:T(8,128)(2,1)S(1)}, u32[]{:S(2)}, u32[]{:S(2)}) collective-permute-start(bf16[96,16,128]{2,1,0:T(8,128)(2,1)S(1)} %pad_maximum_fusion.2), channel_id=1, source_target_pairs={{0,192},{64,0},{128,64},{192,128},{1,193},{65,1},{129,65},{193,129... | collective-permute-start | bytes 1179656 | tf_op jit(solution)/shard_map/ppermute | solution.py:385
  43.7 8.6 %collective-permute-start.12 = (bf16[48,16,128]{2,1,0:T(8,128)(2,1)S(1)}, bf16[48,16,128]{2,1,0:T(8,128)(2,1)S(1)}, u32[]{:S(2)}, u32[]{:S(2)}) collective-permute-start(bf16[48,16,128]{2,1,0:T(8,128)(2,1)S(1)} %slice.72), channel_id=1, source_target_pairs={{0,1},{1,2},{2,3},{3,0},{4,5},{5,6},{6,7},{7,4},{8,9},{9,10},{10,1... | collective-permute-start | bytes 589832 | tf_op jit(solution)/shard_map/ppermute | solution.py:387
  44.1 8.3 %collective-permute-start.14 = (bf16[48,16,128]{2,1,0:T(8,128)(2,1)S(1)}, bf16[48,16,128]{2,1,0:T(8,128)(2,1)S(1)}, u32[]{:S(2)}, u32[]{:S(2)}) collective-permute-start(bf16[48,16,128]{2,1,0:T(8,128)(2,1)S(1)} %slice.73), channel_id=1, source_target_pairs={{0,3},{1,0},{2,1},{3,2},{4,7},{5,4},{6,5},{7,6},{8,11},{9,8},{10,9... | collective-permute-start | bytes 589832 | tf_op jit(solution)/shard_map/ppermute | solution.py:388
  46.6 6.1 %collective-permute-start.5 = (bf16[48,16,128]{2,1,0:T(8,128)(2,1)S(1)}, bf16[48,16,128]{2,1,0:T(8,128)(2,1)S(1)}, u32[]{:S(2)}, u32[]{:S(2)}) collective-permute-start(bf16[48,16,128]{2,1,0:T(8,128)(2,1)S(1)} %slice.70), channel_id=1, source_target_pairs={{0,64},{64,128},{128,192},{192,0},{1,65},{65,129},{129,193},{193,1... | collective-permute-start | bytes 589832 | tf_op jit(solution)/shard_map/ppermute | solution.py:387
  46.8 6.0 %collective-permute-start.7 = (bf16[48,16,128]{2,1,0:T(8,128)(2,1)S(1)}, bf16[48,16,128]{2,1,0:T(8,128)(2,1)S(1)}, u32[]{:S(2)}, u32[]{:S(2)}) collective-permute-start(bf16[48,16,128]{2,1,0:T(8,128)(2,1)S(1)} %slice.71), channel_id=1, source_target_pairs={{0,192},{64,0},{128,64},{192,128},{1,193},{65,1},{129,65},{193,129... | collective-permute-start | bytes 589832 | tf_op jit(solution)/shard_map/ppermute | solution.py:388
  55.5 5.1 %collective-permute-start.15 = (f32[96,128]{1,0:T(8,128)S(1)}, f32[96,128]{1,0:T(8,128)S(1)}, u32[]{:S(2)}, u32[]{:S(2)}) collective-permute-start(f32[96,128]{1,0:T(8,128)S(1)} %slice.74), channel_id=1, source_target_pairs={{0,4},{4,0},{1,5},{5,1},{2,6},{6,2},{3,7},{7,3},{8,12},{12,8},{9,1... | collective-permute-start | bytes 147464 | tf_op jit(solution)/shard_map/ppermute | solution.py:23
  61.5 60.0 %copy-start.1 = (bf16[96,128]{1,0:T(8,128)(2,1)S(1)}, bf16[96,128]{1,0:T(8,128)(2,1)}, u32[]{:S(2)}) copy-start(bf16[96,128]{1,0:T(8,128)(2,1)} %get-tuple-element.107.row) | copy-start | bytes 73732
  80.0 7.7 %collective-permute-start.16 = (bf16[27,16,128]{2,1,0:T(8,128)(2,1)S(1)}, bf16[27,16,128]{2,1,0:T(8,128)(2,1)S(1)}, u32[]{:S(2)}, u32[]{:S(2)}) collective-permute-start(bf16[27,16,128]{2,1,0:T(8,128)(2,1)S(1)} %pad_maximum_fusion.5), channel_id=1, source_target_pairs={{0,1},{1,2},{2,3},{3,0},{4,5},{5,6},{6,7},{7,4},{8,9},{9,10},{10,1... | collective-permute-start | bytes 331784 | tf_op jit(solution)/shard_map/ppermute | solution.py:30
  80.0 12.1 %collective-permute-start.23 = (bf16[28,16,128]{2,1,0:T(8,128)(2,1)S(1)}, bf16[28,16,128]{2,1,0:T(8,128)(2,1)S(1)}, u32[]{:S(2)}, u32[]{:S(2)}) collective-permute-start(bf16[28,16,128]{2,1,0:T(8,128)(2,1)S(1)} %pad_maximum_fusion.4), channel_id=1, source_target_pairs={{0,64},{64,128},{128,192},{192,0},{1,65},{65,129},{129,193},{193,1... | collective-permute-start | bytes 344072 | tf_op jit(solution)/shard_map/ppermute | solution.py:30
  80.2 12.0 %collective-permute-start.24 = (bf16[28,16,128]{2,1,0:T(8,128)(2,1)S(1)}, bf16[28,16,128]{2,1,0:T(8,128)(2,1)S(1)}, u32[]{:S(2)}, u32[]{:S(2)}) collective-permute-start(bf16[28,16,128]{2,1,0:T(8,128)(2,1)S(1)} %pad_maximum_fusion.4), channel_id=1, source_target_pairs={{0,128},{64,192},{128,0},{192,64},{1,129},{65,193},{129,1},{193,65... | collective-permute-start | bytes 344072 | tf_op jit(solution)/shard_map/ppermute | solution.py:30
  84.5 7.6 %collective-permute-start.25 = (bf16[28,16,128]{2,1,0:T(8,128)(2,1)S(1)}, bf16[28,16,128]{2,1,0:T(8,128)(2,1)S(1)}, u32[]{:S(2)}, u32[]{:S(2)}) collective-permute-start(bf16[28,16,128]{2,1,0:T(8,128)(2,1)S(1)} %pad_maximum_fusion.4), channel_id=1, source_target_pairs={{0,192},{64,0},{128,64},{192,128},{1,193},{65,1},{129,65},{193,129... | collective-permute-start | bytes 344072 | tf_op jit(solution)/shard_map/ppermute | solution.py:30
  84.5 5.5 %collective-permute-start.17 = (bf16[27,16,128]{2,1,0:T(8,128)(2,1)S(1)}, bf16[27,16,128]{2,1,0:T(8,128)(2,1)S(1)}, u32[]{:S(2)}, u32[]{:S(2)}) collective-permute-start(bf16[27,16,128]{2,1,0:T(8,128)(2,1)S(1)} %pad_maximum_fusion.5), channel_id=1, source_target_pairs={{0,2},{1,3},{2,0},{3,1},{4,6},{5,7},{6,4},{7,5},{8,10},{9,11},{10,... | collective-permute-start | bytes 331784 | tf_op jit(solution)/shard_map/ppermute | solution.py:30
  87.6 4.5 %collective-permute-start.18 = (bf16[27,16,128]{2,1,0:T(8,128)(2,1)S(1)}, bf16[27,16,128]{2,1,0:T(8,128)(2,1)S(1)}, u32[]{:S(2)}, u32[]{:S(2)}) collective-permute-start(bf16[27,16,128]{2,1,0:T(8,128)(2,1)S(1)} %pad_maximum_fusion.5), channel_id=1, source_target_pairs={{0,3},{1,0},{2,1},{3,2},{4,7},{5,4},{6,5},{7,6},{8,11},{9,8},{10,9... | collective-permute-start | bytes 331784 | tf_op jit(solution)/shard_map/ppermute | solution.py:30
  92.2 11.1 %collective-permute-start.26 = (bf16[112,16,128]{2,1,0:T(8,128)(2,1)S(1)}, bf16[112,16,128]{2,1,0:T(8,128)(2,1)S(1)}, u32[]{:S(2)}, u32[]{:S(2)}) collective-permute-start(bf16[112,16,128]{2,1,0:T(8,128)(2,1)S(1)} %pad_maximum_fusion), channel_id=1, source_target_pairs={{0,1},{1,2},{2,3},{3,0},{4,5},{5,6},{6,7},{7,4},{8,9},{9,10},{10,1... | collective-permute-start | bytes 1376264 | tf_op jit(solution)/shard_map/ppermute | solution.py:384
  92.3 11.2 %collective-permute-start.28 = (bf16[112,16,128]{2,1,0:T(8,128)(2,1)S(1)}, bf16[112,16,128]{2,1,0:T(8,128)(2,1)S(1)}, u32[]{:S(2)}, u32[]{:S(2)}) collective-permute-start(bf16[112,16,128]{2,1,0:T(8,128)(2,1)S(1)} %pad_maximum_fusion), channel_id=1, source_target_pairs={{0,3},{1,0},{2,1},{3,2},{4,7},{5,4},{6,5},{7,6},{8,11},{9,8},{10,9... | collective-permute-start | bytes 1376264 | tf_op jit(solution)/shard_map/ppermute | solution.py:385
  95.0 11.2 %collective-permute-start.19 = (bf16[108,16,128]{2,1,0:T(8,128)(2,1)S(1)}, bf16[108,16,128]{2,1,0:T(8,128)(2,1)S(1)}, u32[]{:S(2)}, u32[]{:S(2)}) collective-permute-start(bf16[108,16,128]{2,1,0:T(8,128)(2,1)S(1)} %pad_maximum_fusion.1), channel_id=1, source_target_pairs={{0,64},{64,128},{128,192},{192,0},{1,65},{65,129},{129,193},{193,1... | collective-permute-start | bytes 1327112 | tf_op jit(solution)/shard_map/ppermute | solution.py:384
  96.3 11.1 %collective-permute-start.21 = (bf16[108,16,128]{2,1,0:T(8,128)(2,1)S(1)}, bf16[108,16,128]{2,1,0:T(8,128)(2,1)S(1)}, u32[]{:S(2)}, u32[]{:S(2)}) collective-permute-start(bf16[108,16,128]{2,1,0:T(8,128)(2,1)S(1)} %pad_maximum_fusion.1), channel_id=1, source_target_pairs={{0,192},{64,0},{128,64},{192,128},{1,193},{65,1},{129,65},{193,129... | collective-permute-start | bytes 1327112 | tf_op jit(solution)/shard_map/ppermute | solution.py:385
  103.4 9.5 %collective-permute-start.27 = (bf16[56,16,128]{2,1,0:T(8,128)(2,1)S(1)}, bf16[56,16,128]{2,1,0:T(8,128)(2,1)S(1)}, u32[]{:S(2)}, u32[]{:S(2)}) collective-permute-start(bf16[56,16,128]{2,1,0:T(8,128)(2,1)S(1)} %slice.81), channel_id=1, source_target_pairs={{0,1},{1,2},{2,3},{3,0},{4,5},{5,6},{6,7},{7,4},{8,9},{9,10},{10,1... | collective-permute-start | bytes 688136 | tf_op jit(solution)/shard_map/ppermute | solution.py:387
  103.5 9.3 %collective-permute-start.29 = (bf16[56,16,128]{2,1,0:T(8,128)(2,1)S(1)}, bf16[56,16,128]{2,1,0:T(8,128)(2,1)S(1)}, u32[]{:S(2)}, u32[]{:S(2)}) collective-permute-start(bf16[56,16,128]{2,1,0:T(8,128)(2,1)S(1)} %slice.82), channel_id=1, source_target_pairs={{0,3},{1,0},{2,1},{3,2},{4,7},{5,4},{6,5},{7,6},{8,11},{9,8},{10,9... | collective-permute-start | bytes 688136 | tf_op jit(solution)/shard_map/ppermute | solution.py:388
  106.2 6.6 %collective-permute-start.20 = (bf16[54,16,128]{2,1,0:T(8,128)(2,1)S(1)}, bf16[54,16,128]{2,1,0:T(8,128)(2,1)S(1)}, u32[]{:S(2)}, u32[]{:S(2)}) collective-permute-start(bf16[54,16,128]{2,1,0:T(8,128)(2,1)S(1)} %slice.79), channel_id=1, source_target_pairs={{0,64},{64,128},{128,192},{192,0},{1,65},{65,129},{129,193},{193,1... | collective-permute-start | bytes 663560 | tf_op jit(solution)/shard_map/ppermute | solution.py:387
  107.4 5.4 %collective-permute-start.22 = (bf16[54,16,128]{2,1,0:T(8,128)(2,1)S(1)}, bf16[54,16,128]{2,1,0:T(8,128)(2,1)S(1)}, u32[]{:S(2)}, u32[]{:S(2)}) collective-permute-start(bf16[54,16,128]{2,1,0:T(8,128)(2,1)S(1)} %slice.80), channel_id=1, source_target_pairs={{0,192},{64,0},{128,64},{192,128},{1,193},{65,1},{129,65},{193,129... | collective-permute-start | bytes 663560 | tf_op jit(solution)/shard_map/ppermute | solution.py:388
  115.6 5.9 %collective-permute-start.30 = (f32[224,128]{1,0:T(8,128)S(1)}, f32[224,128]{1,0:T(8,128)S(1)}, u32[]{:S(2)}, u32[]{:S(2)}) collective-permute-start(f32[224,128]{1,0:T(8,128)S(1)} %slice.83), channel_id=1, source_target_pairs={{0,4},{4,0},{1,5},{5,1},{2,6},{6,2},{3,7},{7,3},{8,12},{12,8},{9,1... | collective-permute-start | bytes 344072 | tf_op jit(solution)/shard_map/ppermute | solution.py:23
  (3 other events, 32.7 us)
